TPU v7x, 512 devices: a whole 4x8x8 slice. The times are simulated.
512 devices in a mesh: group: 2 (over core), gx: 16 (over z, y_hi), gy: 16 (over y_lo, x).
Axes of the slice: x: 4, y: 8 (y_hi: 2, y_lo: 4; y = y_hi * 4 + y_lo), z: 8, core: 2. Of those that a mesh axis runs over, the one named last changes fastest.
Arguments:
- forcing: float32 [256, 128, 256], P('gx', 'gy', 'group'), may hold values from -6 to 6
- metric: float32 [256, 128, 256], P('gx', 'gy', 'group'), may hold values from 0.5 to 2
- sweeps: int32 [2, 3], replicated, may hold values from 1 to 4, as said below
Outputs:
- solution: float32 [256, 128, 256], P('gx', 'gy', 'group')
- residual: float32 [256, 128, 256], P('gx', 'gy', 'group')
Inputs may be any that keep to these rules, and one draw needn't show every extreme that they name: `sweeps`: at least one entry is 4.
All inputs are finite; a program needn't handle non-finite values.
Results may differ from a plain program's by a relative error of at most 0.0001.
Values sent between devices are 32-bit elements; how exact they have to be, the bound alone decides.
No kernel may reach another device: no remote copies, remote signals or barrier semaphores. Data moves between devices by JAX's collectives and lax.ppermute only.
A program may use at most 64 MiB of HBM per device.

v0:
```python
import jax
import jax.numpy as jnp
from jax import lax
from jax.sharding import PartitionSpec as P

MAXSWEEPS = 4
CYCLES = 2


RELAXATION = 0.8
SIDE_WEIGHT = 0.05 ** (1.0 / 3.0)
MID_WEIGHT = 2.0 * SIDE_WEIGHT
SELF_WEIGHT = 3.4


def padded_2(block, sides, width):
    for axis, dim in sides:
        count = lax.axis_size(axis)
        forward = [(i, i + 1) for i in range(count - 1)]
        backward = [(target, source) for source, target in forward]
        low = lax.ppermute(
            lax.slice_in_dim(block, block.shape[dim] - width, None, axis=dim), axis, forward
        )
        high = lax.ppermute(lax.slice_in_dim(block, 0, width, axis=dim), axis, backward)
        block = jnp.concatenate([low, block, high], axis=dim)
    return block


def stencil_padded(padded):
    summed = MID_WEIGHT * padded[1:-1] + SIDE_WEIGHT * (padded[2:] + padded[:-2])
    summed = MID_WEIGHT * summed[:, 1:-1] + SIDE_WEIGHT * (summed[:, 2:] + summed[:, :-2])
    return MID_WEIGHT * summed[:, :, 1:-1] + SIDE_WEIGHT * (summed[:, :, 2:] + summed[:, :, :-2])


def block_sum(field):
    dims = field.shape
    return field.reshape(dims[0] // 2, 2, dims[1] // 2, 2, dims[2] // 2, 2).sum(axis=(1, 3, 5))


def prolong(coarse):
    dims = coarse.shape
    spread = jnp.broadcast_to(
        coarse[:, None, :, None, :, None], (dims[0], 2, dims[1], 2, dims[2], 2)
    )
    return 0.5 * spread.reshape(2 * dims[0], 2 * dims[1], 2 * dims[2])


def apply_fine(field, metric):
    weighted = metric * field
    padded = padded_2(weighted, (("gx", 0), ("gy", 1), ("group", 2)), 1)
    return metric * (SELF_WEIGHT * weighted - stencil_padded(padded))


def apply_slab(field, weights, factor):
    weighted = weights * field
    padded = padded_2(weighted, ((("group", "gx"), 0), ("gy", 1)), 1)
    padded = jnp.pad(padded, ((0, 0), (0, 0), (1, 1)))
    return factor * weights * (SELF_WEIGHT * weighted - stencil_padded(padded))


def relax(rhs_field, diagonal, count, operator):
    update = jnp.zeros_like(rhs_field)
    for sweep_index in range(MAXSWEEPS):
        active = (sweep_index < count).astype(jnp.float32)
        update = update + active * (RELAXATION * (rhs_field - operator(update)) / diagonal)
    return update


def on_device(forcing, metric, sweeps):
    metric_blocks = jnp.transpose(0.125 * block_sum(metric), (2, 1, 0))
    metric_one = lax.all_to_all(metric_blocks, "gx", split_axis=0, concat_axis=2, tiled=True)
    metric_two = 0.125 * block_sum(metric_one)
    diag_zero = 1.0 * 3.0 * metric * metric
    diag_one = 0.25 * 3.0 * metric_one * metric_one
    diag_two = 0.0625 * 3.0 * metric_two * metric_two
    solution = jnp.zeros_like(forcing)
    for cycle_index in range(CYCLES):
        res_zero = forcing - apply_fine(solution, metric)
        fine_corr = relax(
            res_zero, diag_zero, sweeps[cycle_index, 0], lambda field: apply_fine(field, metric)
        )
        res_blocks = jnp.transpose(0.5 * block_sum(res_zero), (2, 1, 0))
        res_one = lax.all_to_all(res_blocks, "gx", split_axis=0, concat_axis=2, tiled=True)
        mid_corr = relax(
            res_one,
            diag_one,
            sweeps[cycle_index, 1],
            lambda field: apply_slab(field, metric_one, 0.25),
        )
        res_two = 0.5 * block_sum(res_one)
        low_corr = relax(
            res_two,
            diag_two,
            sweeps[cycle_index, 2],
            lambda field: apply_slab(field, metric_two, 0.0625),
        )
        mid_corr = mid_corr + prolong(low_corr)
        returned = lax.all_to_all(mid_corr, "gx", split_axis=2, concat_axis=0, tiled=True)
        solution = solution + fine_corr + prolong(jnp.transpose(returned, (2, 1, 0)))
    residual = forcing - apply_fine(solution, metric)
    return (solution, residual)


def solution(mesh):
    return jax.shard_map(
        on_device,
        mesh=mesh,
        in_specs=(P("gx", "gy", "group"), P("gx", "gy", "group"), P()),
        out_specs=(P("gx", "gy", "group"), P("gx", "gy", "group")),
        check_vma=False,
    )
```

profile of v0, /device:TPU:57, one launch (start us, length us, event | category | flops | bytes accessed | tf_op | source)
XLA Modules:
  0.0 704.9 jit_solution(1834123809397758587)
XLA Ops:
  5.9 5.7 collective-permute-start
  11.6 6.3 reshape.142
  21.4 15.1 %all-to-all-start.1 = ((f32[16,1,128]{2,1,0:T(1,128)}), f32[16,1,128]{2,1,0:T(1,128)S(1)}, u32[]{:S(2)}, u32[]{:S(2)}) async-start(f32[16,1,128]{2,1,0:T(1,128)} %reshape.175), calls=%async_computation.1 | async-start | bytes 16384 | tf_op jit(solution)/shard_map/all_to_all | solution.py:71
  59.7 5.6 reshape.141
  70.7 8.2 %collective-permute-start.6 = (f32[1,8,128]{2,1,0:T(8,128)S(1)}, f32[1,8,128]{2,1,0:T(8,128)S(1)}, u32[]{:S(2)}, u32[]{:S(2)}) collective-permute-start(f32[1,8,128]{2,1,0:T(8,128)S(1)} %get-tuple-element.87), channel_id=1, source_target_pairs={{0,16},{16,32},{32,48},{48,64},{64,80},{80,96},{96,112},{112,128},... | collective-permute-start | bytes 12296 | tf_op jit(solution)/shard_map/ppermute | solution.py:21
  78.9 11.5 %all-to-all-start = ((f32[16,1,128]{2,1,0:T(1,128)}), f32[16,1,128]{2,1,0:T(1,128)S(1)}, u32[]{:S(2)}, u32[]{:S(2)}) async-start(f32[16,1,128]{2,1,0:T(1,128)} %reshape.177), calls=%async_computation | async-start | bytes 16384 | tf_op jit(solution)/shard_map/all_to_all | solution.py:83
  94.1 8.1 %collective-permute-start.40 = (f32[1,2,64]{2,1,0:T(2,128)S(1)}, f32[1,2,64]{2,1,0:T(2,128)S(1)}, u32[]{:S(2)}, u32[]{:S(2)}) collective-permute-start(f32[1,2,64]{2,1,0:T(2,128)S(1)} %get-tuple-element.145), channel_id=1, source_target_pairs={{0,16},{16,32},{32,48},{48,64},{64,80},{80,96},{96,112},{112,128},... | collective-permute-start | bytes 1544 | tf_op jit(solution)/shard_map/ppermute | solution.py:21
  105.6 5.8 collective-permute-start.43
  113.3 10.0 %collective-permute-start.25 = (f32[1,4,128]{2,1,0:T(4,128)S(1)}, f32[1,4,128]{2,1,0:T(4,128)S(1)}, u32[]{:S(2)}, u32[]{:S(2)}) collective-permute-start(f32[1,4,128]{2,1,0:T(4,128)S(1)} %get-tuple-element.118), channel_id=1, source_target_pairs={{16,0},{32,16},{48,32},{64,48},{80,64},{96,80},{112,96},{128,112},... | collective-permute-start | bytes 6152 | tf_op jit(solution)/shard_map/ppermute | solution.py:24
  125.3 6.2 collective-permute-done.24
  131.5 5.5 collective-permute-start.27
  138.9 5.5 collective-permute-start.9
  178.0 10.0 %collective-permute-start.13 = (f32[1,8,128]{2,1,0:T(8,128)S(1)}, f32[1,8,128]{2,1,0:T(8,128)S(1)}, u32[]{:S(2)}, u32[]{:S(2)}) collective-permute-start(f32[1,8,128]{2,1,0:T(8,128)S(1)} %get-tuple-element.86), channel_id=1, source_target_pairs={{16,0},{32,16},{48,32},{64,48},{80,64},{96,80},{112,96},{128,112},... | collective-permute-start | bytes 12296 | tf_op jit(solution)/shard_map/ppermute | solution.py:24
  190.2 7.3 %collective-permute-start.49 = (f32[1,2,64]{2,1,0:T(2,128)S(1)}, f32[1,2,64]{2,1,0:T(2,128)S(1)}, u32[]{:S(2)}, u32[]{:S(2)}) collective-permute-start(f32[1,2,64]{2,1,0:T(2,128)S(1)} %get-tuple-element.142), channel_id=1, source_target_pairs={{16,0},{32,16},{48,32},{64,48},{80,64},{96,80},{112,96},{128,112},... | collective-permute-start | bytes 1544 | tf_op jit(solution)/shard_map/ppermute | solution.py:24
  226.2 5.9 collective-permute-start.52
  232.1 5.5 collective-permute-start.31
  239.6 5.5 collective-permute-start.55
  247.0 5.5 collective-permute-start.15
  254.8 7.4 %collective-permute-start.33 = (f32[1,4,128]{2,1,0:T(4,128)S(1)}, f32[1,4,128]{2,1,0:T(4,128)S(1)}, u32[]{:S(2)}, u32[]{:S(2)}) collective-permute-start(f32[1,4,128]{2,1,0:T(4,128)S(1)} %get-tuple-element.114), channel_id=1, source_target_pairs={{16,0},{32,16},{48,32},{64,48},{80,64},{96,80},{112,96},{128,112},... | collective-permute-start | bytes 6152 | tf_op jit(solution)/shard_map/ppermute | solution.py:24
  265.0 7.8 %collective-permute-done.32 = f32[1,4,128]{2,1,0:T(4,128)S(1)} collective-permute-done((f32[1,4,128]{2,1,0:T(4,128)S(1)}, f32[1,4,128]{2,1,0:T(4,128)S(1)}, u32[]{:S(2)}, u32[]{:S(2)}) %collective-permute-start.32) | collective-permute-done | bytes 2080 | tf_op jit(solution)/shard_map/ppermute | solution.py:21
  272.8 5.8 collective-permute-start.35
  285.3 10.0 %collective-permute-start.37 = (f32[1,4,128]{2,1,0:T(4,128)S(1)}, f32[1,4,128]{2,1,0:T(4,128)S(1)}, u32[]{:S(2)}, u32[]{:S(2)}) collective-permute-start(f32[1,4,128]{2,1,0:T(4,128)S(1)} %get-tuple-element.112), channel_id=1, source_target_pairs={{16,0},{32,16},{48,32},{64,48},{80,64},{96,80},{112,96},{128,112},... | collective-permute-start | bytes 6152 | tf_op jit(solution)/shard_map/ppermute | solution.py:24
  309.3 6.1 collective-permute-start.19
  340.7 11.8 %all-to-all-start.2 = ((f32[16,1,128]{2,1,0:T(1,128)}), f32[16,1,128]{2,1,0:T(1,128)S(1)}, u32[]{:S(2)}, u32[]{:S(2)}) async-start(f32[16,1,128]{2,1,0:T(1,128)} %reshape.179), calls=%async_computation.2 | async-start | bytes 16384 | tf_op jit(solution)/shard_map/all_to_all | solution.py:98
  352.9 5.8 all-to-all-done.2
  366.9 7.0 collective-permute-start.57
  390.7 7.1 %collective-permute-start.61 = (f32[18,10,1]{2,1,0:T(8,128)S(1)}, f32[18,10,1]{2,1,0:T(8,128)S(1)}, u32[]{:S(2)}, u32[]{:S(2)}) collective-permute-start(f32[18,10,1]{2,1,0:T(8,128)S(1)} %get-tuple-element.46), channel_id=1, source_target_pairs={{256,0},{257,1},{258,2},{259,3},{260,4},{261,5},{262,6},{263,7},{2... | collective-permute-start | bytes 2168 | tf_op jit(solution)/shard_map/ppermute | solution.py:24
  403.4 8.2 %collective-permute-start.62 = (f32[1,8,128]{2,1,0:T(8,128)S(1)}, f32[1,8,128]{2,1,0:T(8,128)S(1)}, u32[]{:S(2)}, u32[]{:S(2)}) collective-permute-start(f32[1,8,128]{2,1,0:T(8,128)S(1)} %get-tuple-element.79), channel_id=1, source_target_pairs={{0,16},{16,32},{32,48},{48,64},{64,80},{80,96},{96,112},{112,128},... | collective-permute-start | bytes 12296 | tf_op jit(solution)/shard_map/ppermute | solution.py:21
  424.7 5.6 reshape.145
  439.0 10.8 %all-to-all-start.3 = ((f32[16,1,128]{2,1,0:T(1,128)}), f32[16,1,128]{2,1,0:T(1,128)S(1)}, u32[]{:S(2)}, u32[]{:S(2)}) async-start(f32[16,1,128]{2,1,0:T(1,128)} %reshape.181), calls=%async_computation.3 | async-start | bytes 16384 | tf_op jit(solution)/shard_map/all_to_all | solution.py:83
  450.2 5.8 all-to-all-done.3
  457.2 7.0 collective-permute-start.93
  478.1 7.3 %collective-permute-start.69 = (f32[1,8,128]{2,1,0:T(8,128)S(1)}, f32[1,8,128]{2,1,0:T(8,128)S(1)}, u32[]{:S(2)}, u32[]{:S(2)}) collective-permute-start(f32[1,8,128]{2,1,0:T(8,128)S(1)} %get-tuple-element.78), channel_id=1, source_target_pairs={{16,0},{32,16},{48,32},{64,48},{80,64},{96,80},{112,96},{128,112},... | collective-permute-start | bytes 12296 | tf_op jit(solution)/shard_map/ppermute | solution.py:24
  488.5 6.4 collective-permute-start.97
  503.3 5.7 collective-permute-start.99
  515.3 5.8 collective-permute-start.80
  524.7 6.7 collective-permute-start.100
  531.4 5.5 collective-permute-start.83
  538.8 5.5 collective-permute-start.103
  554.1 6.5 collective-permute-start.85
  564.2 6.9 collective-permute-done.84
  571.2 5.8 collective-permute-start.87
  583.6 10.0 %collective-permute-start.89 = (f32[1,4,128]{2,1,0:T(4,128)S(1)}, f32[1,4,128]{2,1,0:T(4,128)S(1)}, u32[]{:S(2)}, u32[]{:S(2)}) collective-permute-start(f32[1,4,128]{2,1,0:T(4,128)S(1)} %get-tuple-element.106), channel_id=1, source_target_pairs={{16,0},{32,16},{48,32},{64,48},{80,64},{96,80},{112,96},{128,112},... | collective-permute-start | bytes 6152 | tf_op jit(solution)/shard_map/ppermute | solution.py:24
  607.6 7.1 %collective-permute-start.75 = (f32[1,8,128]{2,1,0:T(8,128)S(1)}, f32[1,8,128]{2,1,0:T(8,128)S(1)}, u32[]{:S(2)}, u32[]{:S(2)}) collective-permute-start(f32[1,8,128]{2,1,0:T(8,128)S(1)} %get-tuple-element.76), channel_id=1, source_target_pairs={{16,0},{32,16},{48,32},{64,48},{80,64},{96,80},{112,96},{128,112},... | collective-permute-start | bytes 12296 | tf_op jit(solution)/shard_map/ppermute | solution.py:24
  639.0 15.6 %all-to-all-start.4 = ((f32[16,1,128]{2,1,0:T(1,128)}), f32[16,1,128]{2,1,0:T(1,128)S(1)}, u32[]{:S(2)}, u32[]{:S(2)}) async-start(f32[16,1,128]{2,1,0:T(1,128)} %reshape.183), calls=%async_computation.4 | async-start | bytes 16384 | tf_op jit(solution)/shard_map/all_to_all | solution.py:98
  655.0 5.8 all-to-all-done.4
  669.7 7.0 collective-permute-start.105
  693.5 7.1 %collective-permute-start.109 = (f32[18,10,1]{2,1,0:T(8,128)S(1)}, f32[18,10,1]{2,1,0:T(8,128)S(1)}, u32[]{:S(2)}, u32[]{:S(2)}) collective-permute-start(f32[18,10,1]{2,1,0:T(8,128)S(1)} %get-tuple-element.38), channel_id=1, source_target_pairs={{256,0},{257,1},{258,2},{259,3},{260,4},{261,5},{262,6},{263,7},{2... | collective-permute-start | bytes 2168 | tf_op jit(solution)/shard_map/ppermute | solution.py:24
  (420 shorter events, 332.3 us)
Async XLA Ops:
  1.5 35.1 %collective-permute-start.1 = (f32[1,8,128]{2,1,0:T(8,128)S(1)}, f32[1,8,128]{2,1,0:T(8,128)S(1)}, u32[]{:S(2)}, u32[]{:S(2)}) collective-permute-start(f32[1,8,128]{2,1,0:T(8,128)S(1)} %get-tuple-element.90), channel_id=1, source_target_pairs={{16,0},{32,16},{48,32},{64,48},{80,64},{96,80},{112,96},{128,112},... | collective-permute-start | bytes 12296 | tf_op jit(solution)/shard_map/ppermute | solution.py:24
  5.9 30.6 %collective-permute-start = (f32[1,8,128]{2,1,0:T(8,128)S(1)}, f32[1,8,128]{2,1,0:T(8,128)S(1)}, u32[]{:S(2)}, u32[]{:S(2)}) collective-permute-start(f32[1,8,128]{2,1,0:T(8,128)S(1)} %get-tuple-element.89), channel_id=1, source_target_pairs={{0,16},{16,32},{32,48},{48,64},{64,80},{80,96},{96,112},{112,128},... | collective-permute-start | bytes 12296 | tf_op jit(solution)/shard_map/ppermute | solution.py:21
  21.4 57.5 %all-to-all-start.1 = ((f32[16,1,128]{2,1,0:T(1,128)}), f32[16,1,128]{2,1,0:T(1,128)S(1)}, u32[]{:S(2)}, u32[]{:S(2)}) async-start(f32[16,1,128]{2,1,0:T(1,128)} %reshape.175), calls=%async_computation.1 | async-start | bytes 16384 | tf_op jit(solution)/shard_map/all_to_all | solution.py:71
  36.6 15.2 %collective-permute-start.3 = (f32[18,1,128]{2,1,0:T(1,128)S(1)}, f32[18,1,128]{2,1,0:T(1,128)S(1)}, u32[]{:S(2)}, u32[]{:S(2)}) collective-permute-start(f32[18,1,128]{2,1,0:T(1,128)S(1)} %get-tuple-element.72), channel_id=1, source_target_pairs={{1,0},{2,1},{3,2},{4,3},{5,4},{6,5},{7,6},{8,7},{9,8},{10,9},{11,1... | collective-permute-start | bytes 27656 | tf_op jit(solution)/shard_map/ppermute | solution.py:24
  68.8 70.1 %collective-permute-start.7 = (f32[1,8,128]{2,1,0:T(8,128)S(1)}, f32[1,8,128]{2,1,0:T(8,128)S(1)}, u32[]{:S(2)}, u32[]{:S(2)}) collective-permute-start(f32[1,8,128]{2,1,0:T(8,128)S(1)} %get-tuple-element.88), channel_id=1, source_target_pairs={{16,0},{32,16},{48,32},{64,48},{80,64},{96,80},{112,96},{128,112},... | collective-permute-start | bytes 12296 | tf_op jit(solution)/shard_map/ppermute | solution.py:24
  70.7 68.2 %collective-permute-start.6 = (f32[1,8,128]{2,1,0:T(8,128)S(1)}, f32[1,8,128]{2,1,0:T(8,128)S(1)}, u32[]{:S(2)}, u32[]{:S(2)}) collective-permute-start(f32[1,8,128]{2,1,0:T(8,128)S(1)} %get-tuple-element.87), channel_id=1, source_target_pairs={{0,16},{16,32},{32,48},{48,64},{64,80},{80,96},{96,112},{112,128},... | collective-permute-start | bytes 12296 | tf_op jit(solution)/shard_map/ppermute | solution.py:21
  78.9 77.1 %all-to-all-start = ((f32[16,1,128]{2,1,0:T(1,128)}), f32[16,1,128]{2,1,0:T(1,128)S(1)}, u32[]{:S(2)}, u32[]{:S(2)}) async-start(f32[16,1,128]{2,1,0:T(1,128)} %reshape.177), calls=%async_computation | async-start | bytes 16384 | tf_op jit(solution)/shard_map/all_to_all | solution.py:83
  105.6 17.7 %collective-permute-start.43 = (f32[4,1,64]{2,1,0:T(1,128)S(1)}, f32[4,1,64]{2,1,0:T(1,128)S(1)}, u32[]{:S(2)}, u32[]{:S(2)}) collective-permute-start(f32[4,1,64]{2,1,0:T(1,128)S(1)} %get-tuple-element.132), channel_id=1, source_target_pairs={{1,0},{2,1},{3,2},{4,3},{5,4},{6,5},{7,6},{8,7},{9,8},{10,9},{11,1... | collective-permute-start | bytes 3080 | tf_op jit(solution)/shard_map/ppermute | solution.py:24
  111.3 13.8 %collective-permute-start.42 = (f32[4,1,64]{2,1,0:T(1,128)S(1)}, f32[4,1,64]{2,1,0:T(1,128)S(1)}, u32[]{:S(2)}, u32[]{:S(2)}) collective-permute-start(f32[4,1,64]{2,1,0:T(1,128)S(1)} %get-tuple-element.131), channel_id=1, source_target_pairs={{0,1},{1,2},{2,3},{3,4},{4,5},{5,6},{6,7},{7,8},{8,9},{9,10},{10,1... | collective-permute-start | bytes 3080 | tf_op jit(solution)/shard_map/ppermute | solution.py:21
  131.5 14.9 %collective-permute-start.27 = (f32[6,1,128]{2,1,0:T(1,128)S(1)}, f32[6,1,128]{2,1,0:T(1,128)S(1)}, u32[]{:S(2)}, u32[]{:S(2)}) collective-permute-start(f32[6,1,128]{2,1,0:T(1,128)S(1)} %get-tuple-element.104), channel_id=1, source_target_pairs={{1,0},{2,1},{3,2},{4,3},{5,4},{6,5},{7,6},{8,7},{9,8},{10,9},{11,1... | collective-permute-start | bytes 9224 | tf_op jit(solution)/shard_map/ppermute | solution.py:24
  172.7 17.3 %collective-permute-start.47 = (f32[4,1,64]{2,1,0:T(1,128)S(1)}, f32[4,1,64]{2,1,0:T(1,128)S(1)}, u32[]{:S(2)}, u32[]{:S(2)}) collective-permute-start(f32[4,1,64]{2,1,0:T(1,128)S(1)} %get-tuple-element.130), channel_id=1, source_target_pairs={{1,0},{2,1},{3,2},{4,3},{5,4},{6,5},{7,6},{8,7},{9,8},{10,9},{11,1... | collective-permute-start | bytes 3080 | tf_op jit(solution)/shard_map/ppermute | solution.py:24
  174.6 15.4 %collective-permute-start.46 = (f32[4,1,64]{2,1,0:T(1,128)S(1)}, f32[4,1,64]{2,1,0:T(1,128)S(1)}, u32[]{:S(2)}, u32[]{:S(2)}) collective-permute-start(f32[4,1,64]{2,1,0:T(1,128)S(1)} %get-tuple-element.129), channel_id=1, source_target_pairs={{0,1},{1,2},{2,3},{3,4},{4,5},{5,6},{6,7},{7,8},{8,9},{9,10},{10,1... | collective-permute-start | bytes 3080 | tf_op jit(solution)/shard_map/ppermute | solution.py:21
  178.0 67.1 %collective-permute-start.13 = (f32[1,8,128]{2,1,0:T(8,128)S(1)}, f32[1,8,128]{2,1,0:T(8,128)S(1)}, u32[]{:S(2)}, u32[]{:S(2)}) collective-permute-start(f32[1,8,128]{2,1,0:T(8,128)S(1)} %get-tuple-element.86), channel_id=1, source_target_pairs={{16,0},{32,16},{48,32},{64,48},{80,64},{96,80},{112,96},{128,112},... | collective-permute-start | bytes 12296 | tf_op jit(solution)/shard_map/ppermute | solution.py:24
  187.9 59.1 %collective-permute-start.12 = (f32[1,8,128]{2,1,0:T(8,128)S(1)}, f32[1,8,128]{2,1,0:T(8,128)S(1)}, u32[]{:S(2)}, u32[]{:S(2)}) collective-permute-start(f32[1,8,128]{2,1,0:T(8,128)S(1)} %get-tuple-element.85), channel_id=1, source_target_pairs={{0,16},{16,32},{32,48},{48,64},{64,80},{80,96},{96,112},{112,128},... | collective-permute-start | bytes 12296 | tf_op jit(solution)/shard_map/ppermute | solution.py:21
  211.7 14.5 %collective-permute-start.29 = (f32[1,4,128]{2,1,0:T(4,128)S(1)}, f32[1,4,128]{2,1,0:T(4,128)S(1)}, u32[]{:S(2)}, u32[]{:S(2)}) collective-permute-start(f32[1,4,128]{2,1,0:T(4,128)S(1)} %get-tuple-element.116), channel_id=1, source_target_pairs={{16,0},{32,16},{48,32},{64,48},{80,64},{96,80},{112,96},{128,112},... | collective-permute-start | bytes 6152 | tf_op jit(solution)/shard_map/ppermute | solution.py:24
  216.8 15.3 %collective-permute-start.28 = (f32[1,4,128]{2,1,0:T(4,128)S(1)}, f32[1,4,128]{2,1,0:T(4,128)S(1)}, u32[]{:S(2)}, u32[]{:S(2)}) collective-permute-start(f32[1,4,128]{2,1,0:T(4,128)S(1)} %get-tuple-element.115), channel_id=1, source_target_pairs={{0,16},{16,32},{32,48},{48,64},{64,80},{80,96},{96,112},{112,128},... | collective-permute-start | bytes 6152 | tf_op jit(solution)/shard_map/ppermute | solution.py:21
  222.0 15.6 %collective-permute-start.53 = (f32[1,2,64]{2,1,0:T(2,128)S(1)}, f32[1,2,64]{2,1,0:T(2,128)S(1)}, u32[]{:S(2)}, u32[]{:S(2)}) collective-permute-start(f32[1,2,64]{2,1,0:T(2,128)S(1)} %get-tuple-element.140), channel_id=1, source_target_pairs={{16,0},{32,16},{48,32},{64,48},{80,64},{96,80},{112,96},{128,112},... | collective-permute-start | bytes 1544 | tf_op jit(solution)/shard_map/ppermute | solution.py:24
  232.1 22.4 %collective-permute-start.31 = (f32[6,1,128]{2,1,0:T(1,128)S(1)}, f32[6,1,128]{2,1,0:T(1,128)S(1)}, u32[]{:S(2)}, u32[]{:S(2)}) collective-permute-start(f32[6,1,128]{2,1,0:T(1,128)S(1)} %get-tuple-element.102), channel_id=1, source_target_pairs={{1,0},{2,1},{3,2},{4,3},{5,4},{6,5},{7,6},{8,7},{9,8},{10,9},{11,1... | collective-permute-start | bytes 9224 | tf_op jit(solution)/shard_map/ppermute | solution.py:24
  237.6 17.0 %collective-permute-start.30 = (f32[6,1,128]{2,1,0:T(1,128)S(1)}, f32[6,1,128]{2,1,0:T(1,128)S(1)}, u32[]{:S(2)}, u32[]{:S(2)}) collective-permute-start(f32[6,1,128]{2,1,0:T(1,128)S(1)} %get-tuple-element.101), channel_id=1, source_target_pairs={{0,1},{1,2},{2,3},{3,4},{4,5},{5,6},{6,7},{7,8},{8,9},{9,10},{10,1... | collective-permute-start | bytes 9224 | tf_op jit(solution)/shard_map/ppermute | solution.py:21
  247.0 50.1 %collective-permute-start.15 = (f32[18,1,128]{2,1,0:T(1,128)S(1)}, f32[18,1,128]{2,1,0:T(1,128)S(1)}, u32[]{:S(2)}, u32[]{:S(2)}) collective-permute-start(f32[18,1,128]{2,1,0:T(1,128)S(1)} %get-tuple-element.68), channel_id=1, source_target_pairs={{1,0},{2,1},{3,2},{4,3},{5,4},{6,5},{7,6},{8,7},{9,8},{10,9},{11,1... | collective-permute-start | bytes 27656 | tf_op jit(solution)/shard_map/ppermute | solution.py:24
  252.5 44.6 %collective-permute-start.14 = (f32[18,1,128]{2,1,0:T(1,128)S(1)}, f32[18,1,128]{2,1,0:T(1,128)S(1)}, u32[]{:S(2)}, u32[]{:S(2)}) collective-permute-start(f32[18,1,128]{2,1,0:T(1,128)S(1)} %get-tuple-element.67), channel_id=1, source_target_pairs={{0,1},{1,2},{2,3},{3,4},{4,5},{5,6},{6,7},{7,8},{8,9},{9,10},{10,1... | collective-permute-start | bytes 27656 | tf_op jit(solution)/shard_map/ppermute | solution.py:21
  285.3 14.7 %collective-permute-start.37 = (f32[1,4,128]{2,1,0:T(4,128)S(1)}, f32[1,4,128]{2,1,0:T(4,128)S(1)}, u32[]{:S(2)}, u32[]{:S(2)}) collective-permute-start(f32[1,4,128]{2,1,0:T(4,128)S(1)} %get-tuple-element.112), channel_id=1, source_target_pairs={{16,0},{32,16},{48,32},{64,48},{80,64},{96,80},{112,96},{128,112},... | collective-permute-start | bytes 6152 | tf_op jit(solution)/shard_map/ppermute | solution.py:24
  303.5 15.9 %collective-permute-start.39 = (f32[6,1,128]{2,1,0:T(1,128)S(1)}, f32[6,1,128]{2,1,0:T(1,128)S(1)}, u32[]{:S(2)}, u32[]{:S(2)}) collective-permute-start(f32[6,1,128]{2,1,0:T(1,128)S(1)} %get-tuple-element.98), channel_id=1, source_target_pairs={{1,0},{2,1},{3,2},{4,3},{5,4},{6,5},{7,6},{8,7},{9,8},{10,9},{11,1... | collective-permute-start | bytes 9224 | tf_op jit(solution)/shard_map/ppermute | solution.py:24
  305.4 14.0 %collective-permute-start.38 = (f32[6,1,128]{2,1,0:T(1,128)S(1)}, f32[6,1,128]{2,1,0:T(1,128)S(1)}, u32[]{:S(2)}, u32[]{:S(2)}) collective-permute-start(f32[6,1,128]{2,1,0:T(1,128)S(1)} %get-tuple-element.97), channel_id=1, source_target_pairs={{0,1},{1,2},{2,3},{3,4},{4,5},{5,6},{6,7},{7,8},{8,9},{9,10},{10,1... | collective-permute-start | bytes 9224 | tf_op jit(solution)/shard_map/ppermute | solution.py:21
  334.5 18.0 %collective-permute-start.23 = (f32[18,10,1]{2,1,0:T(8,128)S(1)}, f32[18,10,1]{2,1,0:T(8,128)S(1)}, u32[]{:S(2)}, u32[]{:S(2)}) collective-permute-start(f32[18,10,1]{2,1,0:T(8,128)S(1)} %get-tuple-element.48), channel_id=1, source_target_pairs={{256,0},{257,1},{258,2},{259,3},{260,4},{261,5},{262,6},{263,7},{2... | collective-permute-start | bytes 2168 | tf_op jit(solution)/shard_map/ppermute | solution.py:24
  338.2 14.3 %collective-permute-start.22 = (f32[18,10,1]{2,1,0:T(8,128)S(1)}, f32[18,10,1]{2,1,0:T(8,128)S(1)}, u32[]{:S(2)}, u32[]{:S(2)}) collective-permute-start(f32[18,10,1]{2,1,0:T(8,128)S(1)} %get-tuple-element.47), channel_id=1, source_target_pairs={{0,256},{1,257},{2,258},{3,259},{4,260},{5,261},{6,262},{7,263},{8... | collective-permute-start | bytes 2168 | tf_op jit(solution)/shard_map/ppermute | solution.py:21
  340.7 18.0 %all-to-all-start.2 = ((f32[16,1,128]{2,1,0:T(1,128)}), f32[16,1,128]{2,1,0:T(1,128)S(1)}, u32[]{:S(2)}, u32[]{:S(2)}) async-start(f32[16,1,128]{2,1,0:T(1,128)} %reshape.179), calls=%async_computation.2 | async-start | bytes 16384 | tf_op jit(solution)/shard_map/all_to_all | solution.py:98
  412.4 20.5 %collective-permute-start.65 = (f32[18,1,128]{2,1,0:T(1,128)S(1)}, f32[18,1,128]{2,1,0:T(1,128)S(1)}, u32[]{:S(2)}, u32[]{:S(2)}) collective-permute-start(f32[18,1,128]{2,1,0:T(1,128)S(1)} %get-tuple-element.62), channel_id=1, source_target_pairs={{1,0},{2,1},{3,2},{4,3},{5,4},{6,5},{7,6},{8,7},{9,8},{10,9},{11,1... | collective-permute-start | bytes 27656 | tf_op jit(solution)/shard_map/ppermute | solution.py:24
  414.3 18.6 %collective-permute-start.64 = (f32[18,1,128]{2,1,0:T(1,128)S(1)}, f32[18,1,128]{2,1,0:T(1,128)S(1)}, u32[]{:S(2)}, u32[]{:S(2)}) collective-permute-start(f32[18,1,128]{2,1,0:T(1,128)S(1)} %get-tuple-element.61), channel_id=1, source_target_pairs={{0,1},{1,2},{2,3},{3,4},{4,5},{5,6},{6,7},{7,8},{8,9},{9,10},{10,1... | collective-permute-start | bytes 27656 | tf_op jit(solution)/shard_map/ppermute | solution.py:21
  433.0 16.8 %collective-permute-start.67 = (f32[18,10,1]{2,1,0:T(8,128)S(1)}, f32[18,10,1]{2,1,0:T(8,128)S(1)}, u32[]{:S(2)}, u32[]{:S(2)}) collective-permute-start(f32[18,10,1]{2,1,0:T(8,128)S(1)} %get-tuple-element.44), channel_id=1, source_target_pairs={{256,0},{257,1},{258,2},{259,3},{260,4},{261,5},{262,6},{263,7},{2... | collective-permute-start | bytes 2168 | tf_op jit(solution)/shard_map/ppermute | solution.py:24
  439.0 17.1 %all-to-all-start.3 = ((f32[16,1,128]{2,1,0:T(1,128)}), f32[16,1,128]{2,1,0:T(1,128)S(1)}, u32[]{:S(2)}, u32[]{:S(2)}) async-start(f32[16,1,128]{2,1,0:T(1,128)} %reshape.181), calls=%async_computation.3 | async-start | bytes 16384 | tf_op jit(solution)/shard_map/all_to_all | solution.py:83
  472.4 15.9 %collective-permute-start.95 = (f32[4,1,64]{2,1,0:T(1,128)S(1)}, f32[4,1,64]{2,1,0:T(1,128)S(1)}, u32[]{:S(2)}, u32[]{:S(2)}) collective-permute-start(f32[4,1,64]{2,1,0:T(1,128)S(1)} %get-tuple-element.124), channel_id=1, source_target_pairs={{1,0},{2,1},{3,2},{4,3},{5,4},{6,5},{7,6},{8,7},{9,8},{10,9},{11,1... | collective-permute-start | bytes 3080 | tf_op jit(solution)/shard_map/ppermute | solution.py:24
  478.1 66.2 %collective-permute-start.69 = (f32[1,8,128]{2,1,0:T(8,128)S(1)}, f32[1,8,128]{2,1,0:T(8,128)S(1)}, u32[]{:S(2)}, u32[]{:S(2)}) collective-permute-start(f32[1,8,128]{2,1,0:T(8,128)S(1)} %get-tuple-element.78), channel_id=1, source_target_pairs={{16,0},{32,16},{48,32},{64,48},{80,64},{96,80},{112,96},{128,112},... | collective-permute-start | bytes 12296 | tf_op jit(solution)/shard_map/ppermute | solution.py:24
  485.4 60.8 %collective-permute-start.68 = (f32[1,8,128]{2,1,0:T(8,128)S(1)}, f32[1,8,128]{2,1,0:T(8,128)S(1)}, u32[]{:S(2)}, u32[]{:S(2)}) collective-permute-start(f32[1,8,128]{2,1,0:T(8,128)S(1)} %get-tuple-element.77), channel_id=1, source_target_pairs={{0,16},{16,32},{32,48},{48,64},{64,80},{80,96},{96,112},{112,128},... | collective-permute-start | bytes 12296 | tf_op jit(solution)/shard_map/ppermute | solution.py:21
  510.9 13.7 %collective-permute-start.81 = (f32[1,4,128]{2,1,0:T(4,128)S(1)}, f32[1,4,128]{2,1,0:T(4,128)S(1)}, u32[]{:S(2)}, u32[]{:S(2)}) collective-permute-start(f32[1,4,128]{2,1,0:T(4,128)S(1)} %get-tuple-element.110), channel_id=1, source_target_pairs={{16,0},{32,16},{48,32},{64,48},{80,64},{96,80},{112,96},{128,112},... | collective-permute-start | bytes 6152 | tf_op jit(solution)/shard_map/ppermute | solution.py:24
  515.3 16.1 %collective-permute-start.80 = (f32[1,4,128]{2,1,0:T(4,128)S(1)}, f32[1,4,128]{2,1,0:T(4,128)S(1)}, u32[]{:S(2)}, u32[]{:S(2)}) collective-permute-start(f32[1,4,128]{2,1,0:T(4,128)S(1)} %get-tuple-element.109), channel_id=1, source_target_pairs={{0,16},{16,32},{32,48},{48,64},{64,80},{80,96},{96,112},{112,128},... | collective-permute-start | bytes 6152 | tf_op jit(solution)/shard_map/ppermute | solution.py:21
  521.3 15.6 %collective-permute-start.101 = (f32[1,2,64]{2,1,0:T(2,128)S(1)}, f32[1,2,64]{2,1,0:T(2,128)S(1)}, u32[]{:S(2)}, u32[]{:S(2)}) collective-permute-start(f32[1,2,64]{2,1,0:T(2,128)S(1)} %get-tuple-element.134), channel_id=1, source_target_pairs={{16,0},{32,16},{48,32},{64,48},{80,64},{96,80},{112,96},{128,112},... | collective-permute-start | bytes 1544 | tf_op jit(solution)/shard_map/ppermute | solution.py:24
  524.7 14.1 %collective-permute-start.100 = (f32[1,2,64]{2,1,0:T(2,128)S(1)}, f32[1,2,64]{2,1,0:T(2,128)S(1)}, u32[]{:S(2)}, u32[]{:S(2)}) collective-permute-start(f32[1,2,64]{2,1,0:T(2,128)S(1)} %get-tuple-element.133), channel_id=1, source_target_pairs={{0,16},{16,32},{32,48},{48,64},{64,80},{80,96},{96,112},{112,128},... | collective-permute-start | bytes 1544 | tf_op jit(solution)/shard_map/ppermute | solution.py:21
  531.4 22.4 %collective-permute-start.83 = (f32[6,1,128]{2,1,0:T(1,128)S(1)}, f32[6,1,128]{2,1,0:T(1,128)S(1)}, u32[]{:S(2)}, u32[]{:S(2)}) collective-permute-start(f32[6,1,128]{2,1,0:T(1,128)S(1)} %get-tuple-element.96), channel_id=1, source_target_pairs={{1,0},{2,1},{3,2},{4,3},{5,4},{6,5},{7,6},{8,7},{9,8},{10,9},{11,1... | collective-permute-start | bytes 9224 | tf_op jit(solution)/shard_map/ppermute | solution.py:24
  536.9 17.0 %collective-permute-start.82 = (f32[6,1,128]{2,1,0:T(1,128)S(1)}, f32[6,1,128]{2,1,0:T(1,128)S(1)}, u32[]{:S(2)}, u32[]{:S(2)}) collective-permute-start(f32[6,1,128]{2,1,0:T(1,128)S(1)} %get-tuple-element.95), channel_id=1, source_target_pairs={{0,1},{1,2},{2,3},{3,4},{4,5},{5,6},{6,7},{7,8},{8,9},{9,10},{10,1... | collective-permute-start | bytes 9224 | tf_op jit(solution)/shard_map/ppermute | solution.py:21
  546.3 49.2 %collective-permute-start.71 = (f32[18,1,128]{2,1,0:T(1,128)S(1)}, f32[18,1,128]{2,1,0:T(1,128)S(1)}, u32[]{:S(2)}, u32[]{:S(2)}) collective-permute-start(f32[18,1,128]{2,1,0:T(1,128)S(1)} %get-tuple-element.60), channel_id=1, source_target_pairs={{1,0},{2,1},{3,2},{4,3},{5,4},{6,5},{7,6},{8,7},{9,8},{10,9},{11,1... | collective-permute-start | bytes 27656 | tf_op jit(solution)/shard_map/ppermute | solution.py:24
  551.8 43.7 %collective-permute-start.70 = (f32[18,1,128]{2,1,0:T(1,128)S(1)}, f32[18,1,128]{2,1,0:T(1,128)S(1)}, u32[]{:S(2)}, u32[]{:S(2)}) collective-permute-start(f32[18,1,128]{2,1,0:T(1,128)S(1)} %get-tuple-element.59), channel_id=1, source_target_pairs={{0,1},{1,2},{2,3},{3,4},{4,5},{5,6},{6,7},{7,8},{8,9},{9,10},{10,1... | collective-permute-start | bytes 27656 | tf_op jit(solution)/shard_map/ppermute | solution.py:21
  583.6 16.1 %collective-permute-start.89 = (f32[1,4,128]{2,1,0:T(4,128)S(1)}, f32[1,4,128]{2,1,0:T(4,128)S(1)}, u32[]{:S(2)}, u32[]{:S(2)}) collective-permute-start(f32[1,4,128]{2,1,0:T(4,128)S(1)} %get-tuple-element.106), channel_id=1, source_target_pairs={{16,0},{32,16},{48,32},{64,48},{80,64},{96,80},{112,96},{128,112},... | collective-permute-start | bytes 6152 | tf_op jit(solution)/shard_map/ppermute | solution.py:24
  601.8 15.9 %collective-permute-start.91 = (f32[6,1,128]{2,1,0:T(1,128)S(1)}, f32[6,1,128]{2,1,0:T(1,128)S(1)}, u32[]{:S(2)}, u32[]{:S(2)}) collective-permute-start(f32[6,1,128]{2,1,0:T(1,128)S(1)} %get-tuple-element.92), channel_id=1, source_target_pairs={{1,0},{2,1},{3,2},{4,3},{5,4},{6,5},{7,6},{8,7},{9,8},{10,9},{11,1... | collective-permute-start | bytes 9224 | tf_op jit(solution)/shard_map/ppermute | solution.py:24
  603.8 14.0 %collective-permute-start.90 = (f32[6,1,128]{2,1,0:T(1,128)S(1)}, f32[6,1,128]{2,1,0:T(1,128)S(1)}, u32[]{:S(2)}, u32[]{:S(2)}) collective-permute-start(f32[6,1,128]{2,1,0:T(1,128)S(1)} %get-tuple-element.91), channel_id=1, source_target_pairs={{0,1},{1,2},{2,3},{3,4},{4,5},{5,6},{6,7},{7,8},{8,9},{9,10},{10,1... | collective-permute-start | bytes 9224 | tf_op jit(solution)/shard_map/ppermute | solution.py:21
  633.7 21.0 %collective-permute-start.79 = (f32[18,10,1]{2,1,0:T(8,128)S(1)}, f32[18,10,1]{2,1,0:T(8,128)S(1)}, u32[]{:S(2)}, u32[]{:S(2)}) collective-permute-start(f32[18,10,1]{2,1,0:T(8,128)S(1)} %get-tuple-element.40), channel_id=1, source_target_pairs={{256,0},{257,1},{258,2},{259,3},{260,4},{261,5},{262,6},{263,7},{2... | collective-permute-start | bytes 2168 | tf_op jit(solution)/shard_map/ppermute | solution.py:24
  636.6 18.1 %collective-permute-start.78 = (f32[18,10,1]{2,1,0:T(8,128)S(1)}, f32[18,10,1]{2,1,0:T(8,128)S(1)}, u32[]{:S(2)}, u32[]{:S(2)}) collective-permute-start(f32[18,10,1]{2,1,0:T(8,128)S(1)} %get-tuple-element.39), channel_id=1, source_target_pairs={{0,256},{1,257},{2,258},{3,259},{4,260},{5,261},{6,262},{7,263},{8... | collective-permute-start | bytes 2168 | tf_op jit(solution)/shard_map/ppermute | solution.py:21
  639.0 21.8 %all-to-all-start.4 = ((f32[16,1,128]{2,1,0:T(1,128)}), f32[16,1,128]{2,1,0:T(1,128)S(1)}, u32[]{:S(2)}, u32[]{:S(2)}) async-start(f32[16,1,128]{2,1,0:T(1,128)} %reshape.183), calls=%async_computation.4 | async-start | bytes 16384 | tf_op jit(solution)/shard_map/all_to_all | solution.py:98
  (70 other events, 712.1 us)
where the time goes:
time: 709 us; the launch traced here: 705 us
  starting transfers between devices  502 us (71%)
  waiting for transfers between devices  122 us (17%)
  local copies, waits for them, and re-layouts  41.5 us (6%)
  other arithmetic  20.6 us (3%)
  between operations  19.2 us (3%)
    ppermute x55, starting transfers between devices, padded_2(): lax.ppermute(lax.slice_in_dim(block, 0, width, axis=dim), axis, backward)  275 us
    ppermute x55, starting transfers between devices, padded_2(): lax.ppermute(lax.slice_in_dim(block, block.shape[dim] - width, None, axis...  162 us
    ppermute x55, waiting for transfers between devices, padded_2(): lax.ppermute(lax.slice_in_dim(block, block.shape[dim] - width, None, axis...  104 us
    all_to_all x2, starting transfers between devices, on_device(): lax.all_to_all(mid_corr, 'gx', split_axis=2, concat_axis=0, tiled=True)  27.5 us
    all_to_all x2, starting transfers between devices, on_device(): lax.all_to_all(res_blocks, 'gx', split_axis=0, concat_axis=2, tiled=True)  22.3 us
    reshape x6, local copies, waits for them, and re-layouts, block_sum(): field.reshape(dims[0] // 2, 2, dims[1] // 2, 2, dims[2] // 2, 2)  18 us
    all_to_all x1, starting transfers between devices, on_device(): lax.all_to_all(metric_blocks, 'gx', split_axis=0, concat_axis=2, tiled=True)  15.1 us
  transfers between devices with their start and end apart: 115, of which 29 were waited for; matrix products, arithmetic and copies ran while one was open for 6% of the time, Pallas kernels for 0%

commit v1 on v0

v1 whole, which is shorter than its diff:
```python
import jax
import jax.numpy as jnp
import numpy as np
from jax import lax
from jax.experimental import pallas as pl
from jax.experimental.pallas import tpu as pltpu
from jax.sharding import PartitionSpec as P

CYCLES = 2
RELAXATION = 0.8
SIDE_WEIGHT = 0.05 ** (1.0 / 3.0)
SELF_WEIGHT = 3.4
SIDE_CUBE = SIDE_WEIGHT**3

KEEP = 1.0 - RELAXATION * SELF_WEIGHT / 3.0
SPREAD = RELAXATION * SIDE_CUBE / 3.0
LEVEL = [RELAXATION / (3.0 * 4.0**-level) for level in range(3)]

F32 = jnp.float32
TILE = (8, 128)

X_FIRST = dict(h0=0, w=8, h1=10, w12=12, h2=13, size=14)
X_SECOND = dict(h0=0, h1=8, h2=10, size=11)
Y_FIRST = dict(h0=0, w=24, h1=42, w1=50, h2=55, w2=58, size=60, far=60)
Y_SECOND = dict(h0=0, h1=24, h2=32, size=35, far=35)


def sums_of_pairs(rows):
    out = np.zeros((8, 8), np.float32)
    for row in range(rows):
        out[row, 2 * row] = out[row, 2 * row + 1] = 1.0
    return out


def doubling(sources):
    out = np.zeros((16, 16), np.float32)
    for target, source in sources.items():
        out[target, source] = 0.5
    return out


LANE_SUMS = (np.arange(256)[:, None] // 2 == np.arange(128)[None]).astype(np.float32)
ROW_SUMS_ONE = np.kron(np.eye(16, dtype=np.float32), sums_of_pairs(4))
ROW_SUMS_TWO = np.kron(np.eye(8, dtype=np.float32), sums_of_pairs(2))
LANE_COPIES = np.ascontiguousarray(LANE_SUMS.T)
ROW_COPIES_TWO = np.kron(
    np.eye(6, dtype=np.float32), doubling({0: 0, 1: 0, 2: 1, 3: 1, 4: 2, 15: 15})
)
ROW_COPIES_ONE = np.kron(
    np.eye(10, dtype=np.float32),
    doubling({**{row: row // 2 for row in range(8)}, 8: 4, 15: 15}),
)


def dot(a, b):
    return lax.dot_general(
        a,
        b,
        (((1,), (0,)), ((), ())),
        precision=lax.Precision.HIGHEST,
        preferred_element_type=F32,
    )


def sub_index():
    return lax.broadcasted_iota(jnp.int32, TILE, 0)


def lane_index():
    return lax.broadcasted_iota(jnp.int32, TILE, 1)


def turn(tile, by):
    by %= 8
    return pltpu.roll(tile, by, 0) if by else tile


def keep(where, tile):
    return jnp.where(where, tile, 0.0)


def inverse(tile):
    return jnp.where(tile > 0, 1.0 / jnp.where(tile > 0, tile, 1.0), 0.0)


def flags(s):
    return [s[k].astype(F32) for k in range(7, 13)]


def coarse_sides(planes, row_one, row_two, lane_sums):
    one = dot(row_one, dot(jnp.concatenate(planes, axis=0), lane_sums))
    pairs = [one[16 * k : 16 * k + 8] + one[16 * k + 8 : 16 * k + 16] for k in range(len(planes) // 2)]
    two = dot(row_two, dot(jnp.concatenate(pairs, axis=0), lane_sums[:128]))
    return one, two


def tiles_of(value):
    return value.reshape(value.shape[0] // 8, 8, 128)


def pack_x(s, h0, h1, h2, xp, at):
    core = s[6]
    fine = jnp.where(core == 0, 12, 0)
    middle = jnp.where(core == 0, 4, 0)
    for k in range(4):
        for z in range(2):
            xp[at["h0"] + 2 * k + z] = h0[fine + k, z]
    for k in range(2):
        xp[at["h1"] + k] = h1[middle + 2 * k] + turn(h1[middle + 2 * k + 1], 4)
    xp[at["h2"]] = quad([h2[k] for k in range(4)])


def quad(tiles):
    total = tiles[0]
    for k in range(1, len(tiles)):
        total = total + turn(tiles[k], 2 * k)
    return total


def first_kernel(s, mg, fg, lane_sums, row_one, row_two, xp, h0, h1, w1, h2, w2):
    for z in range(2):
        h0[:, z] = LEVEL[0] * fg[z] / mg[z]
    planes = [
        jnp.concatenate([ref[z, 2 * k] + ref[z, 2 * k + 1] for z in range(2)], axis=1)
        for ref in (mg, fg)
        for k in range(8)
    ]
    one, two = coarse_sides(planes, row_one[...], row_two[...], lane_sums[...])
    w1_own = 0.125 * one[:64]
    w2_own = 0.125 * 0.125 * two[:32]
    w1[...] = tiles_of(w1_own)
    w2[...] = tiles_of(w2_own)
    h1[...] = tiles_of(LEVEL[1] * 0.5 * one[64:] * inverse(w1_own))
    h2[...] = tiles_of(LEVEL[2] * 0.25 * two[32:] * inverse(w2_own))
    pack_x(s, h0, h1, h2, xp, X_FIRST)
    core = s[6]
    edge = jnp.where(core == 0, 15, 0)
    for z in range(2):
        xp[X_FIRST["w"] + z] = mg[z, edge]
    xp[X_FIRST["w12"]] = w1[jnp.where(core == 0, 7, 0)] + turn(w2[jnp.where(core == 0, 3, 0)], 4)


def column_h0(p, z, h0, xr, at, lo, hi):
    if p < 4:
        return xr[1, 0, at["h0"] + 2 * p + z] * lo
    if p < 20:
        return h0[p - 4, z]
    return xr[0, 1, at["h0"] + 2 * (p - 20) + z] * hi


def column_w(p, z, mg, xr, at):
    if p == 0:
        return xr[1, 0, at["w"] + z]
    if p < 17:
        return mg[z, p - 1]
    return xr[0, 1, at["w"] + z]


def column_h1(p, h1, xr, at, lo, hi):
    if 4 <= p < 12:
        return h1[p - 4]
    if p < 4:
        packed = xr[1, 0, at["h1"] + p // 2] * lo
    else:
        packed = xr[0, 1, at["h1"] + (p - 12) // 2] * hi
    return keep(sub_index() < 4, turn(packed, 4 * (p % 2)))


def column_w1(p, w1, xr, at):
    if 1 <= p < 9:
        return w1[p - 1]
    packed = xr[1, 0, at["w12"]] if p == 0 else xr[0, 1, at["w12"]]
    return keep(sub_index() < 4, packed)


def column_h2(p, h2, xr, at, lo, hi):
    if 4 <= p < 8:
        return h2[p - 4]
    packed = xr[1, 0, at["h2"]] * lo if p < 4 else xr[0, 1, at["h2"]] * hi
    return keep(sub_index() < 2, turn(packed, -2 * (p % 4)))


def column_w2(p, w2, xr, at):
    if 1 <= p < 5:
        return w2[p - 1]
    packed = xr[1, 0, at["w12"]] if p == 0 else xr[0, 1, at["w12"]]
    return keep(sub_index() < 2, turn(packed, 4))


def pack_y(s, h0, h1, h2, xr, yp, x_at, at):
    lo, hi = flags(s)[:2]
    mine = (sub_index() < 4) == (s[6] == 1)
    for k in range(12):
        for z in range(2):
            first, second = (column_h0(2 * k + i, z, h0, xr, x_at, lo, hi) for i in range(2))
            yp[at["h0"] + 2 * k + z] = jnp.where(mine, first, turn(second, 4))
    for k in range(2):
        yp[at["h1"] + k] = xr[1, 0, x_at["h1"] + k] * lo
        yp[at["h1"] + 6 + k] = xr[0, 1, x_at["h1"] + k] * hi
    for k in range(4):
        yp[at["h1"] + 2 + k] = h1[2 * k] + turn(h1[2 * k + 1], 4)
    yp[at["h2"]] = xr[1, 0, x_at["h2"]] * lo
    yp[at["h2"] + 1] = quad([h2[k] for k in range(4)])
    yp[at["h2"] + 2] = xr[0, 1, x_at["h2"]] * hi


def first_rows_kernel(s, h0, mg, h1, w1, h2, w2, xr, yp, y2p):
    at = Y_FIRST
    pack_y(s, h0, h1, h2, xr, yp, X_FIRST, at)
    mine = (sub_index() < 4) == (s[6] == 1)
    for k in range(9):
        for z in range(2):
            first, second = (column_w(2 * k + i, z, mg, xr, X_FIRST) for i in range(2))
            yp[at["w"] + 2 * k + z] = jnp.where(mine, first, turn(second, 4))
    for k in range(5):
        first, second = (column_w1(2 * k + i, w1, xr, X_FIRST) for i in range(2))
        yp[at["w1"] + k] = first + turn(second, 4)
    w2_planes = [column_w2(p, w2, xr, X_FIRST) for p in range(6)]
    yp[at["w2"]] = quad(w2_planes[:4])
    yp[at["w2"] + 1] = quad(w2_planes[4:])
    for k in range(3):
        y2p[k] = yp[at["h2"] + k]


def second_rows_kernel(s, h0, h1, h2, xr, yp, y2p):
    pack_y(s, h0, h1, h2, xr, yp, X_SECOND, Y_SECOND)
    for k in range(3):
        y2p[k] = yp[Y_SECOND["h2"] + k]


def split_rows(above, below):
    sub = sub_index()
    first = jnp.where(sub < 4, above, below)
    second = turn(jnp.where(sub < 4, below, above), 4)
    return first, second


def join_h0(s, h0, xr, yr, out, x_at, at):
    lo, hi, ylo, yhi = flags(s)[:4]
    for k in range(12):
        for z in range(2):
            tile = at["h0"] + 2 * k + z
            halos = split_rows(yr[0, tile] * yhi, yr[1, tile] * ylo)
            for i in range(2):
                out[2 * k + i, z] = column_h0(2 * k + i, z, h0, xr, x_at, lo, hi)
                out[2 * k + i, 2 + z] = halos[i]


def join_w(mg, xr, yr, out):
    for k in range(9):
        for z in range(2):
            tile = Y_FIRST["w"] + 2 * k + z
            halos = split_rows(yr[0, tile], yr[1, tile])
            for i in range(2):
                out[2 * k + i, z] = column_w(2 * k + i, z, mg, xr, X_FIRST)
                out[2 * k + i, 2 + z] = halos[i]


def join_four(own, above, below, i):
    sub = sub_index()
    turned = 4 * (1 - i)
    return own + keep(sub >= 4, turn(above, turned)), keep(sub >= 4, turn(below, turned))


def join_h1(s, h1, xr, yr, out, x_at, at):
    lo, hi, ylo, yhi = flags(s)[:4]
    for k in range(8):
        above, below = yr[0, at["h1"] + k] * yhi, yr[1, at["h1"] + k] * ylo
        for i in range(2):
            own = column_h1(2 * k + i, h1, xr, x_at, lo, hi)
            out[2 * k + i, 0], out[2 * k + i, 1] = join_four(own, above, below, i)


def join_w1(w1, xr, yr, out):
    for k in range(5):
        above, below = (yr[j, Y_FIRST["w1"] + k] for j in range(2))
        for i in range(2):
            own = column_w1(2 * k + i, w1, xr, X_FIRST)
            both = join_four(own, above, below, i)
            for j in range(2):
                out[2 * k + i, j] = inverse(both[j])


def join_h2(s, h2, xr, yr, out, x_at, at):
    lo, hi, ylo, yhi, ylo2, yhi2 = flags(s)
    sub = sub_index()
    for k in range(3):
        above, below = yr[0, at["h2"] + k] * yhi, yr[1, at["h2"] + k] * ylo
        above2, below2 = yr[0, at["far"] + k] * yhi2, yr[1, at["far"] + k] * ylo2
        for i in range(4):
            p = 4 * k + i
            own = column_h2(p, h2, xr, x_at, lo, hi)
            upper = jnp.where(
                sub < 4, turn(above, 2 - 2 * i), keep(sub < 6, turn(above2, 4 - 2 * i))
            )
            out[p, 0] = own + keep(sub >= 2, upper)
            lower = jnp.where(sub < 6, turn(below2, 4 - 2 * i), turn(below, 6 - 2 * i))
            out[p, 1] = keep(sub >= 4, lower)


def join_w2(w2, xr, yr, out):
    sub = sub_index()
    for p in range(6):
        above, below = (yr[j, Y_FIRST["w2"] + p // 4] for j in range(2))
        i = p % 4
        own = column_w2(p, w2, xr, X_FIRST)
        out[p, 0] = inverse(own + keep((sub >= 2) & (sub < 4), turn(above, 2 - 2 * i)))
        out[p, 1] = inverse(keep(sub >= 6, turn(below, 6 - 2 * i)))


def along_y(first, second):
    sub = sub_index()
    up_first, up_second = turn(first, 7), turn(second, 7)
    first = first + jnp.where(sub == 7, up_second, up_first)
    second = second + jnp.where(sub == 7, up_first, up_second)
    down_first, down_second = turn(first, 1), turn(second, 1)
    return (
        first + jnp.where(sub == 0, down_second, down_first),
        second + jnp.where(sub == 0, down_first, down_second),
    )


def along_z_fine(left, right):
    lane = lane_index()
    down_left, down_right = pltpu.roll(left, 1, 1), pltpu.roll(right, 1, 1)
    up_left, up_right = pltpu.roll(left, 127, 1), pltpu.roll(right, 127, 1)
    out_left = (left + left) + (keep(lane > 0, down_left) + jnp.where(lane < 127, up_left, up_right))
    out_right = (right + right) + (
        jnp.where(lane > 0, down_right, down_left) + keep(lane < 127, up_right)
    )
    return out_left, out_right


def along_z_coarse(tile):
    lane = lane_index()
    return (tile + tile) + (
        keep(lane > 0, pltpu.roll(tile, 1, 1)) + keep(lane < 127, pltpu.roll(tile, 127, 1))
    )


def planes_to_stencil(tiles):
    if len(tiles) == 4:
        tiles = list(tiles)
        for z in range(2):
            tiles[z], tiles[2 + z] = along_y(tiles[z], tiles[2 + z])
        for y in range(2):
            tiles[2 * y], tiles[2 * y + 1] = along_z_fine(tiles[2 * y], tiles[2 * y + 1])
        return tiles
    return [along_z_coarse(tile) for tile in along_y(*tiles)]


def relax(q, h, planes, parts, count, masks, lo, hi):
    q[...] = h[...]

    def load(x):
        return [q[x, part] for part in range(parts)]

    def sweep(k, _):
        def step(j, before):
            x = k + 2 * j
            here, after, next_after = load(x), load(x + 1), load(x + 2)
            left = [a + b for a, b in zip(before, here)]
            middle = [a + b for a, b in zip(here, after)]
            right = [a + b for a, b in zip(after, next_after)]
            for place, olds, low, high in ((x, here, left, middle), (x + 1, after, middle, right)):
                spread = SPREAD * jnp.where(place < 4, lo, jnp.where(place >= planes - 4, hi, 1.0))
                summed = planes_to_stencil([a + b for a, b in zip(low, high)])
                for part in range(parts):
                    mask = spread * masks[part // (parts // 2)]
                    q[place, part] = KEEP * olds[part] + mask * summed[part] + h[place, part]
            return tuple(after)

        lax.fori_loop(0, planes // 2 - k, step, tuple(load(k - 1)))
        return 0

    lax.fori_loop(1, count, sweep, 0)


def relax_levels(s, cycle, h0, q0, h1, q1, h2, q2):
    lo, hi, ylo, yhi, ylo2, yhi2 = flags(s)
    sub, lane = sub_index(), lane_index()
    ones = jnp.ones(TILE, F32)
    masks0 = (ones, jnp.where(sub < 4, yhi, ylo) * ones)
    masks1 = (jnp.where(sub < 4, 1.0, yhi) * ones, jnp.where(sub < 4, 0.0, ylo) * ones)
    above = jnp.where(sub < 2, 1.0, jnp.where(sub < 4, yhi, jnp.where(sub < 6, yhi2, 0.0)))
    below = jnp.where(sub < 4, 0.0, jnp.where(sub < 6, ylo2, ylo))
    masks2 = (keep(lane < 64, above * ones), keep(lane < 64, below * ones))
    relax(q2, h2, 12, 2, s[3 * cycle + 2], masks2, lo, hi)
    relax(q1, h1, 16, 2, s[3 * cycle + 1], masks1, lo, hi)
    relax(q0, h0, 24, 4, s[3 * cycle], masks0, lo, hi)


def corrections(q1, iw1, q2, iw2, lane_copies, rows_two, rows_one):
    two = [q2[p + 3, part] * iw2[p, part] for p in range(6) for part in range(2)]
    spread = dot(rows_two[...], dot(jnp.concatenate(two, axis=0), lane_copies[:, :128]))
    one = []
    for p in range(10):
        for part in range(2):
            row = 16 * ((p + 1) // 2) + 8 * part
            one.append(q1[p + 3, part] * iw1[p, part] + spread[row : row + 8])
    return dot(rows_one[...], dot(jnp.concatenate(one, axis=0), lane_copies[...]))


def correction_tile(coarse, p, part):
    row, lane = 16 * ((p + 1) // 2) + 8 * (part // 2), 128 * (part % 2)
    return coarse[row : row + 8, lane : lane + 128]


def operator_rows(pf, x):
    planes = [[pf[x + i, part] for part in range(4)] for i in range(3)]
    summed = planes_to_stencil([a + (b + b) + c for a, b, c in zip(*planes)])
    return planes[1][:2], summed[:2]


def middle_kernel(
    s, h0, mg, fg, h1, w1, h2, w2, xr, yr,
    lane_sums, row_one, row_two, lane_copies, rows_two, rows_one,
    xp, pf, w, iw1, iw2, h0_next, h1_next, h2_next,
    h0_all, q0, h1_all, q1, h2_all, q2, g,
):
    join_h0(s, h0, xr, yr, h0_all, X_FIRST, Y_FIRST)
    join_w(mg, xr, yr, w)
    join_h1(s, h1, xr, yr, h1_all, X_FIRST, Y_FIRST)
    join_w1(w1, xr, yr, iw1)
    join_h2(s, h2, xr, yr, h2_all, X_FIRST, Y_FIRST)
    join_w2(w2, xr, yr, iw2)
    relax_levels(s, 0, h0_all, q0, h1_all, q1, h2_all, q2)
    coarse = corrections(q1, iw1, q2, iw2, lane_copies, rows_two, rows_one)
    for p in range(18):
        for part in range(4):
            pf[p, part] = q0[p + 3, part] + w[p, part] * correction_tile(coarse, p, part)

    def residual(x, _):
        iterate, summed = operator_rows(pf, x)
        for z in range(2):
            weight = mg[z, x]
            rest = fg[z, x] - weight * (SELF_WEIGHT * iterate[z] - SIDE_CUBE * summed[z])
            g[x, z] = rest
            h0_next[x, z] = LEVEL[0] * rest / weight
        return 0

    lax.fori_loop(0, 16, residual, 0)
    planes = [
        jnp.concatenate([g[2 * k, z] + g[2 * k + 1, z] for z in range(2)], axis=1)
        for k in range(8)
    ]
    one, two = coarse_sides(planes, row_one[:64, :64], row_two[:32, :32], lane_sums[...])
    w1_own, w2_own = w1[...], w2[...]
    h1_next[...] = LEVEL[1] * 0.5 * tiles_of(one) * inverse(w1_own)
    h2_next[...] = LEVEL[2] * 0.25 * tiles_of(two) * inverse(w2_own)
    pack_x(s, h0_next, h1_next, h2_next, xp, X_SECOND)


def last_kernel(
    s, h0, mg, fg, h1, h2, xr, yr, pf, w, iw1, iw2, lane_copies, rows_two, rows_one,
    solution_out, residual_out,
    h0_all, q0, h1_all, q1, h2_all, q2, pl_all,
):
    join_h0(s, h0, xr, yr, h0_all, X_SECOND, Y_SECOND)
    join_h1(s, h1, xr, yr, h1_all, X_SECOND, Y_SECOND)
    join_h2(s, h2, xr, yr, h2_all, X_SECOND, Y_SECOND)
    relax_levels(s, 1, h0_all, q0, h1_all, q1, h2_all, q2)
    coarse = corrections(q1, iw1, q2, iw2, lane_copies, rows_two, rows_one)
    for p in range(18):
        for part in range(4):
            pl_all[p, part] = (
                pf[p, part] + q0[p + 3, part] + w[p, part] * correction_tile(coarse, p, part)
            )
    first = s[6] == 0

    def finish(x, _):
        iterate, summed = operator_rows(pl_all, x)
        mine, spread = (jnp.where(first, both[0], both[1]) for both in (iterate, summed))
        weight = jnp.where(first, mg[0, x], mg[1, x])
        force = jnp.where(first, fg[0, x], fg[1, x])
        solution_out[x] = mine / weight
        residual_out[x] = force - weight * (SELF_WEIGHT * mine - SIDE_CUBE * spread)
        return 0

    lax.fori_loop(0, 16, finish, 0)


def call(kernel, outs, scratch, name, *operands):
    smem = pl.BlockSpec(memory_space=pltpu.SMEM)
    vmem = pl.BlockSpec(memory_space=pltpu.VMEM)
    return pl.pallas_call(
        kernel,
        out_shape=[jax.ShapeDtypeStruct(shape, F32) for shape in outs],
        in_specs=[smem] + [vmem] * (len(operands) - 1),
        out_specs=[vmem] * len(outs),
        scratch_shapes=[pltpu.VMEM(shape, F32) for shape in scratch],
        compiler_params=pltpu.CompilerParams(vmem_limit_bytes=32 * 2**20),
        name=name,
    )(*operands)


def tiles(*dims):
    return (*dims, *TILE)


def pairs(axis, distance):
    size = lax.axis_size(axis)
    return [[i, size + (i + distance) % size] for i in range(size)]


def share(value):
    return lax.all_gather(value, "group", axis=0)


def trade_x(packed):
    both = lax.all_gather(packed, ("group", "gx"), axis=0, axis_index_groups=pairs("gx", 1))
    return share(both)


def swap(packed, distance):
    moves = [move for a, b in pairs("gy", distance) for move in ((a, b), (b, a))]
    return lax.ppermute(packed, ("group", "gy"), moves)


def trade_y(packed, packed_far):
    far = swap(packed_far, 2)
    near = swap(packed, 1)
    return share(jnp.concatenate([near, far], axis=0))


def on_device(forcing, metric, sweeps):
    gx, gy = lax.axis_index("gx"), lax.axis_index("gy")
    x_last, y_last = lax.axis_size("gx") - 1, lax.axis_size("gy") - 1
    places = [gx > 0, gx < x_last, gy > 0, gy < y_last, gy > 1, gy < y_last - 1]
    s = jnp.concatenate(
        [sweeps.reshape(-1), jnp.stack([lax.axis_index("group"), *places]).astype(jnp.int32)]
    )
    mg, fg = share(metric), share(forcing)
    down = [jnp.asarray(LANE_SUMS), jnp.asarray(ROW_SUMS_ONE), jnp.asarray(ROW_SUMS_TWO)]
    up = [jnp.asarray(LANE_COPIES), jnp.asarray(ROW_COPIES_TWO), jnp.asarray(ROW_COPIES_ONE)]
    own = [tiles(16, 2), tiles(8), tiles(4)]
    spaces = [tiles(24, 4)] * 2 + [tiles(16, 2)] * 2 + [tiles(12, 2)] * 2

    xp, h0, h1, w1, h2, w2 = call(
        first_kernel,
        [tiles(X_FIRST["size"]), own[0], own[1], own[1], own[2], own[2]],
        [],
        "first_sides",
        *(s, mg, fg, *down),
    )
    xr = trade_x(xp)
    yp, y2p = call(
        first_rows_kernel,
        [tiles(Y_FIRST["size"]), tiles(3)],
        [],
        "first_rows",
        *(s, h0, mg, h1, w1, h2, w2, xr),
    )
    yr = trade_y(yp, y2p)
    xp, pf, w, iw1, iw2, h0, h1, h2 = call(
        middle_kernel,
        [tiles(X_SECOND["size"]), tiles(18, 4), tiles(18, 4), tiles(10, 2), tiles(6, 2), *own],
        [*spaces, tiles(16, 2)],
        "first_cycle",
        *(s, h0, mg, fg, h1, w1, h2, w2, xr, yr, *down, *up),
    )
    xr = trade_x(xp)
    yp, y2p = call(
        second_rows_kernel,
        [tiles(Y_SECOND["size"]), tiles(3)],
        [],
        "second_rows",
        *(s, h0, h1, h2, xr),
    )
    yr = trade_y(yp, y2p)
    return call(
        last_kernel,
        [tiles(16), tiles(16)],
        [*spaces, tiles(18, 4)],
        "second_cycle",
        *(s, h0, mg, fg, h1, h2, xr, yr, pf, w, iw1, iw2, *up),
    )


def solution(mesh):
    def program(forcing, metric, sweeps):
        return tuple(on_device(forcing, metric, sweeps))

    return jax.shard_map(
        program,
        mesh=mesh,
        in_specs=(P("gx", "gy", "group"), P("gx", "gy", "group"), P()),
        out_specs=(P("gx", "gy", "group"), P("gx", "gy", "group")),
        check_vma=False,
    )
```

time: 709 us -> 87.6 us (0.12)
  the two profiles are of different devices: /device:TPU:57 before, /device:TPU:1 now
where the time goes in v1:
time: 87.6 us; the launch traced here: 87.2 us
  blocking collectives  40.9 us (47%)
  Pallas kernels  16.6 us (19%)
  starting transfers between devices  16.4 us (19%)
  waiting for transfers between devices  11.8 us (13%)
    all_gather x2, blocking collectives, trade_x(): lax.all_gather(packed, ('group', 'gx'), axis=0, axis_index_groups=pairs('...  21.9 us
    all_gather x6, blocking collectives, share(): return lax.all_gather(value, 'group', axis=0)  19 us
    pallas_call x5, Pallas kernels, call(): pl.pallas_call(kernel, out_shape=[jax.ShapeDtypeStruct(shape, F32) for sh...  16.6 us
    ppermute x4, starting transfers between devices, swap(): return lax.ppermute(packed, ('group', 'gy'), moves)  16.4 us
    ppermute x4, waiting for transfers between devices, swap(): return lax.ppermute(packed, ('group', 'gy'), moves)  11.8 us
  transfers between devices with their start and end apart: 4, of which 2 were waited for; matrix products, arithmetic and copies ran while one was open for 0% of the time, Pallas kernels for 0%

profile of v1, /device:TPU:1, one launch (start us, length us, event | category | flops | bytes accessed | tf_op | source)
XLA Modules:
  0.0 87.2 jit_solution(7025280817758395721)
XLA Ops:
  0.6 0.0 copy-start.7
  0.7 0.7 copy-done.7
  1.3 0.1 reshape.7
  1.4 0.0 copy-start.6
  1.4 0.0 copy-start.5
  1.4 8.8 %all-gather.1 = f32[32,8,128]{2,1,0:T(8,128)S(1)} all-gather(f32[16,8,128]{2,1,0:T(8,128)} %param.9), channel_id=3, replica_groups=mesh['group'=2,'gx'=16,'gy'=16] {'group'}, dimensions={0}, use_global_device_ids=true | all-gather | bytes 196608 | tf_op jit(solution)/shard_map/all_gather | solution.py:507
  10.2 0.0 copy-done.6
  10.2 0.0 copy-start.2
  10.2 0.0 copy-start.3
  10.2 2.0 %all-gather = f32[32,8,128]{2,1,0:T(8,128)S(1)} all-gather(f32[16,8,128]{2,1,0:T(8,128)S(1)} %copy-done.6), channel_id=2, replica_groups=mesh['group'=2,'gx'=16,'gy'=16] {'group'}, dimensions={0}, use_global_device_ids=true | all-gather | bytes 196608 | tf_op jit(solution)/shard_map/all_gather | solution.py:507
  12.2 0.1 concatenate.9.s
  12.3 0.0 copy-done.5
  12.3 0.0 copy-done.2
  12.3 0.0 copy-done.3
  12.3 1.4 %first_sides.1 = (f32[14,8,128]{2,1,0:T(8,128)S(1)}, f32[16,2,8,128]{3,2,1,0:T(8,128)S(1)}, f32[8,8,128]{2,1,0:T(8,128)S(1)}, f32[8,8,128]{2,1,0:T(8,128)S(1)}, ...) custom-call(s32[13]{0:T(128)S(1)} %concatenate.9.s, f32[2,16,8,128]{3,2,1,0:T(8,128)S(1)} %bitcast.15, ...), custom_call_target="tpu_custom_call" | custom-call | tf_op jit(solution)/shard_map/first_sides/pallas_call | solution.py:486
  13.7 11.7 %all-gather.2 = f32[28,8,128]{2,1,0:T(8,128)S(1)} all-gather(f32[14,8,128]{2,1,0:T(8,128)S(1)} %get-tuple-element.25), channel_id=4, replica_groups={{0,272},{16,288},{32,304},{48,320},{64,336},{80,352},{96,368},{112,384}..., dimensions={0}, use_global_device_ids=true | all-gather | bytes 172032 | tf_op jit(solution)/shard_map/all_gather | solution.py:511
  25.4 2.0 %all-gather.3 = f32[4,14,8,128]{3,2,1,0:T(8,128)S(1)} all-gather(f32[2,14,8,128]{3,2,1,0:T(8,128)S(1)} %bitcast.28), channel_id=5, replica_groups=mesh['group'=2,'gx'=16,'gy'=16] {'group'}, dimensions={0}, use_global_device_ids=true | all-gather | bytes 344064 | tf_op jit(solution)/shard_map/all_gather | solution.py:507
  27.4 0.6 first_rows.1
  27.9 4.6 %collective-permute-start = (f32[60,8,128]{2,1,0:T(8,128)S(1)}, f32[60,8,128]{2,1,0:T(8,128)S(1)}, u32[]{:S(2)}, u32[]{:S(2)}) collective-permute-start(f32[60,8,128]{2,1,0:T(8,128)S(1)} %get-tuple-element.26), channel_id=1, source_target_pairs={{0,257},{257,0},{1,258},{258,1},{2,259},{259,2},{3,260},{260,3},{4... | collective-permute-start | bytes 737288 | tf_op jit(solution)/shard_map/ppermute | solution.py:517
  32.5 3.3 %collective-permute-start.1 = (f32[3,8,128]{2,1,0:T(8,128)S(1)}, f32[3,8,128]{2,1,0:T(8,128)S(1)}, u32[]{:S(2)}, u32[]{:S(2)}) collective-permute-start(f32[3,8,128]{2,1,0:T(8,128)S(1)} %get-tuple-element.27), channel_id=1, source_target_pairs={{0,258},{258,0},{1,259},{259,1},{2,260},{260,2},{3,261},{261,3},{4... | collective-permute-start | bytes 36872 | tf_op jit(solution)/shard_map/ppermute | solution.py:517
  35.9 5.9 %collective-permute-done.1 = f32[3,8,128]{2,1,0:T(8,128)S(1)} collective-permute-done((f32[3,8,128]{2,1,0:T(8,128)S(1)}, f32[3,8,128]{2,1,0:T(8,128)S(1)}, u32[]{:S(2)}, u32[]{:S(2)}) %collective-permute-start.1) | collective-permute-done | bytes 12320 | tf_op jit(solution)/shard_map/ppermute | solution.py:517
  41.8 0.0 collective-permute-done
  41.8 0.0 copy-start
  41.8 0.0 copy-start.1
  41.8 0.0 copy-start.4
  41.8 2.3 %all-gather.4 = f32[126,8,128]{2,1,0:T(8,128)S(1)} all-gather(f32[63,8,128]{2,1,0:T(8,128)S(1)} %pad_maximum_fusion), channel_id=6, replica_groups=mesh['group'=2,'gx'=16,'gy'=16] {'group'}, dimensions={0}, use_global_device_ids=true | all-gather | bytes 774144 | tf_op jit(solution)/shard_map/all_gather | solution.py:507
  44.1 0.0 copy-done
  44.1 0.0 copy-done.1
  44.1 0.0 copy-done.4
  44.1 7.5 %first_cycle.1 = (f32[11,8,128]{2,1,0:T(8,128)S(1)}, f32[18,4,8,128]{3,2,1,0:T(8,128)S(1)}, f32[18,4,8,128]{3,2,1,0:T(8,128)S(1)}, f32[10,2,8,128]{3,2,1,0:T(8,1...) custom-call(s32[13]{0:T(128)S(1)} %concatenate.9.s, ...), custom_call_target="tpu_custom_call" | custom-call | tf_op jit(solution)/shard_map/first_cycle/pallas_call | solution.py:486
  51.7 10.2 %all-gather.5 = f32[22,8,128]{2,1,0:T(8,128)S(1)} all-gather(f32[11,8,128]{2,1,0:T(8,128)S(1)} %get-tuple-element.31), channel_id=7, replica_groups={{0,272},{16,288},{32,304},{48,320},{64,336},{80,352},{96,368},{112,384}..., dimensions={0}, use_global_device_ids=true | all-gather | bytes 135168 | tf_op jit(solution)/shard_map/all_gather | solution.py:511
  61.8 1.9 %all-gather.6 = f32[4,11,8,128]{3,2,1,0:T(8,128)S(1)} all-gather(f32[2,11,8,128]{3,2,1,0:T(8,128)S(1)} %bitcast.29), channel_id=8, replica_groups=mesh['group'=2,'gx'=16,'gy'=16] {'group'}, dimensions={0}, use_global_device_ids=true | all-gather | bytes 270336 | tf_op jit(solution)/shard_map/all_gather | solution.py:507
  63.8 0.6 second_rows.1
  64.3 5.1 %collective-permute-start.2 = (f32[35,8,128]{2,1,0:T(8,128)S(1)}, f32[35,8,128]{2,1,0:T(8,128)S(1)}, u32[]{:S(2)}, u32[]{:S(2)}) collective-permute-start(f32[35,8,128]{2,1,0:T(8,128)S(1)} %get-tuple-element.32), channel_id=1, source_target_pairs={{0,257},{257,0},{1,258},{258,1},{2,259},{259,2},{3,260},{260,3},{4... | collective-permute-start | bytes 430088 | tf_op jit(solution)/shard_map/ppermute | solution.py:517
  69.5 3.3 %collective-permute-start.3 = (f32[3,8,128]{2,1,0:T(8,128)S(1)}, f32[3,8,128]{2,1,0:T(8,128)S(1)}, u32[]{:S(2)}, u32[]{:S(2)}) collective-permute-start(f32[3,8,128]{2,1,0:T(8,128)S(1)} %get-tuple-element.33), channel_id=1, source_target_pairs={{0,258},{258,0},{1,259},{259,1},{2,260},{260,2},{3,261},{261,3},{4... | collective-permute-start | bytes 36872 | tf_op jit(solution)/shard_map/ppermute | solution.py:517
  72.8 5.9 %collective-permute-done.3 = f32[3,8,128]{2,1,0:T(8,128)S(1)} collective-permute-done((f32[3,8,128]{2,1,0:T(8,128)S(1)}, f32[3,8,128]{2,1,0:T(8,128)S(1)}, u32[]{:S(2)}, u32[]{:S(2)}) %collective-permute-start.3) | collective-permute-done | bytes 12320 | tf_op jit(solution)/shard_map/ppermute | solution.py:517
  78.7 0.0 collective-permute-done.2
  78.7 2.0 %all-gather.7 = f32[76,8,128]{2,1,0:T(8,128)S(1)} all-gather(f32[38,8,128]{2,1,0:T(8,128)S(1)} %pad_maximum_fusion.1), channel_id=9, replica_groups=mesh['group'=2,'gx'=16,'gy'=16] {'group'}, dimensions={0}, use_global_device_ids=true | all-gather | bytes 466944 | tf_op jit(solution)/shard_map/all_gather | solution.py:507
  80.7 6.5 %second_cycle.1 = (f32[16,8,128]{2,1,0:T(8,128)}, f32[16,8,128]{2,1,0:T(8,128)}) custom-call(s32[13]{0:T(128)S(1)} %concatenate.9.s, f32[16,2,8,128]{3,2,1,0:T(8,128)S(1)} %get-tuple-element.28.h0, f32[2,16,8,128]{3,2,1,0:T(8,128)S(1)} %bitcast.18, f32[2,16,8,128]{3,2,1,0:T(8,128)S(1)} %bitcast.21, f32[8,8,128]{2,1,0:T(8,128)S(1)} %get-tuple-element.29.h1, ...), custom_call_target="tpu_custom_call" | custom-call | tf_op jit(solution)/shard_map/second_cycle/pallas_call | solution.py:486
  (2 shorter events, 0.0 us)
Async XLA Ops:
  0.6 0.7 copy-start.7
  1.4 8.8 %copy-start.6 = (f32[16,8,128]{2,1,0:T(8,128)S(1)}, f32[16,8,128]{2,1,0:T(8,128)}, u32[]{:S(2)}) copy-start(f32[16,8,128]{2,1,0:T(8,128)} %param.10) | copy-start | bytes 196612
  1.4 10.9 %copy-start.5 = (f32[64,64]{1,0:T(8,128)S(1)}, f32[64,64]{1,0:T(8,128)}, u32[]{:S(2)}) copy-start(f32[64,64]{1,0:T(8,128)} %constant.35.clone.row_two) | copy-start | bytes 49156
  10.2 2.1 %copy-start.2 = (f32[256,128]{1,0:T(8,128)S(1)}, f32[256,128]{1,0:T(8,128)}, u32[]{:S(2)}) copy-start(f32[256,128]{1,0:T(8,128)} %constant.33.clone.lane_sums) | copy-start | bytes 393220
  10.2 2.1 %copy-start.3 = (f32[128,128]{1,0:T(8,128)S(1)}, f32[128,128]{1,0:T(8,128)}, u32[]{:S(2)}) copy-start(f32[128,128]{1,0:T(8,128)} %constant.34.clone.row_one) | copy-start | bytes 196612
  27.9 13.8 %collective-permute-start = (f32[60,8,128]{2,1,0:T(8,128)S(1)}, f32[60,8,128]{2,1,0:T(8,128)S(1)}, u32[]{:S(2)}, u32[]{:S(2)}) collective-permute-start(f32[60,8,128]{2,1,0:T(8,128)S(1)} %get-tuple-element.26), channel_id=1, source_target_pairs={{0,257},{257,0},{1,258},{258,1},{2,259},{259,2},{3,260},{260,3},{4... | collective-permute-start | bytes 737288 | tf_op jit(solution)/shard_map/ppermute | solution.py:517
  32.5 9.2 %collective-permute-start.1 = (f32[3,8,128]{2,1,0:T(8,128)S(1)}, f32[3,8,128]{2,1,0:T(8,128)S(1)}, u32[]{:S(2)}, u32[]{:S(2)}) collective-permute-start(f32[3,8,128]{2,1,0:T(8,128)S(1)} %get-tuple-element.27), channel_id=1, source_target_pairs={{0,258},{258,0},{1,259},{259,1},{2,260},{260,2},{3,261},{261,3},{4... | collective-permute-start | bytes 36872 | tf_op jit(solution)/shard_map/ppermute | solution.py:517
  41.8 2.3 %copy-start = (f32[160,160]{1,0:T(8,128)S(1)}, f32[160,160]{1,0:T(8,128)}, u32[]{:S(2)}) copy-start(f32[160,160]{1,0:T(8,128)} %constant.38.clone.rows_one) | copy-start | bytes 307204
  41.8 2.3 %copy-start.1 = (f32[128,256]{1,0:T(8,128)S(1)}, f32[128,256]{1,0:T(8,128)}, u32[]{:S(2)}) copy-start(f32[128,256]{1,0:T(8,128)} %constant.36.clone.lane_copies) | copy-start | bytes 393220
  41.8 2.3 %copy-start.4 = (f32[96,96]{1,0:T(8,128)S(1)}, f32[96,96]{1,0:T(8,128)}, u32[]{:S(2)}) copy-start(f32[96,96]{1,0:T(8,128)} %constant.37.clone.rows_two) | copy-start | bytes 110596
  64.3 14.3 %collective-permute-start.2 = (f32[35,8,128]{2,1,0:T(8,128)S(1)}, f32[35,8,128]{2,1,0:T(8,128)S(1)}, u32[]{:S(2)}, u32[]{:S(2)}) collective-permute-start(f32[35,8,128]{2,1,0:T(8,128)S(1)} %get-tuple-element.32), channel_id=1, source_target_pairs={{0,257},{257,0},{1,258},{258,1},{2,259},{259,2},{3,260},{260,3},{4... | collective-permute-start | bytes 430088 | tf_op jit(solution)/shard_map/ppermute | solution.py:517
  69.5 9.2 %collective-permute-start.3 = (f32[3,8,128]{2,1,0:T(8,128)S(1)}, f32[3,8,128]{2,1,0:T(8,128)S(1)}, u32[]{:S(2)}, u32[]{:S(2)}) collective-permute-start(f32[3,8,128]{2,1,0:T(8,128)S(1)} %get-tuple-element.33), channel_id=1, source_target_pairs={{0,258},{258,0},{1,259},{259,1},{2,260},{260,2},{3,261},{261,3},{4... | collective-permute-start | bytes 36872 | tf_op jit(solution)/shard_map/ppermute | solution.py:517

commit v2 on v0

v2 whole, which is shorter than its diff:
```python
import jax
import jax.numpy as jnp
import numpy as np
from jax import lax
from jax.experimental import pallas as pl
from jax.experimental.pallas import tpu as pltpu
from jax.sharding import PartitionSpec as P

RELAXATION = 0.8
SIDE_WEIGHT = 0.05 ** (1.0 / 3.0)
SELF_WEIGHT = 3.4
SIDE_CUBE = SIDE_WEIGHT**3

KEEP = 1.0 - RELAXATION * SELF_WEIGHT / 3.0
SPREAD = RELAXATION * SIDE_CUBE / 3.0
LEVEL = [RELAXATION / (3.0 * 4.0**-level) for level in range(3)]

F32 = jnp.float32
TILE = (8, 128)

OWN = dict(h0=0, w=16, h1=32, w1=36, h2=40, w2=41, size=42)
COARSE = dict(h1=0, w1=4, h2=8, w2=9, size=10)
X_FIRST = dict(h0=0, h1=8, h2=10, w=11, w12=13, size=14)
X_SECOND = dict(h0=0, h1=8, h2=10, size=11)
Y_FIRST = dict(h0=0, h1=24, h2=32, w=35, w1=53, w2=58, size=60, far=60)
Y_SECOND = dict(h0=0, h1=24, h2=32, size=35, far=35)

LANES = np.arange(256)
HALF_SUMS = np.concatenate(
    [LANES[:128, None] // 2 == LANES[None, :128], LANES[:128, None] // 4 == LANES[None, :128]], axis=1
).astype(np.float32)
WHOLE_SUMS = np.concatenate(
    [LANES[:, None] // 2 == LANES[None, :128], LANES[:, None] // 4 == LANES[None, :128]], axis=1
).astype(np.float32)
COPIES = WHOLE_SUMS.T * np.where(LANES[:, None] < 128, 0.5, 0.25).astype(np.float32)


def exact_dot(rows, matrix):
    parts = []
    rest = rows
    for _ in range(3):
        parts.append(rest.astype(jnp.bfloat16))
        rest = rest - parts[-1].astype(F32)
    out = lax.dot_general(
        jnp.concatenate(parts, axis=0),
        matrix,
        (((1,), (0,)), ((), ())),
        preferred_element_type=F32,
    )
    count = rows.shape[0]
    return out[:count] + (out[count : 2 * count] + out[2 * count :])


def sub_index():
    return lax.broadcasted_iota(jnp.int32, TILE, 0)


def lane_index():
    return lax.broadcasted_iota(jnp.int32, TILE, 1)


def turn(tile, by):
    by %= 8
    return pltpu.roll(tile, by, 0) if by else tile


def keep(where, tile):
    return jnp.where(where, tile, 0.0)


def inverse(tile):
    return jnp.where(tile > 0, 1.0 / jnp.where(tile > 0, tile, 1.0), 0.0)


def flags(s):
    return [s[k].astype(F32) for k in range(7, 13)]


def pair_rows(first, second):
    sub = sub_index()
    first, second = (tile + turn(tile, 7) for tile in (first, second))
    low = jnp.where(sub == 0, first, turn(first, 7))
    low = jnp.where(sub < 2, low, jnp.where(sub == 2, turn(first, 6), turn(first, 5)))
    high = jnp.where(sub == 4, turn(second, 4), turn(second, 3))
    high = jnp.where(sub < 6, high, jnp.where(sub == 6, turn(second, 2), turn(second, 1)))
    return jnp.where(sub < 4, low, high)


def plane_sums(fine):
    sub = sub_index()
    sums = [fine[2 * k] + fine[2 * k + 1] for k in range(8)]
    one = [pair_rows(sums[2 * k], sums[2 * k + 1]) for k in range(4)]
    two = None
    for k in range(4):
        both = one[k] + turn(one[k], 4)
        both = both + turn(both, 7)
        placed = jnp.where(sub == 2 * k, turn(both, 2 * k), turn(both, 2 * k - 1))
        two = placed if k == 0 else jnp.where(sub < 2 * k, two, placed)
    return one + [two]


def first_kernel(s, m, f, sums, out):
    m_tiles, f_tiles = ([ref[x] for x in range(16)] for ref in (m, f))
    for x in range(16):
        out[OWN["h0"] + x] = LEVEL[0] * f_tiles[x] / m_tiles[x]
        out[OWN["w"] + x] = m_tiles[x]
    rows = jnp.concatenate(plane_sums(m_tiles) + plane_sums(f_tiles), axis=0)
    total = exact_dot(rows, sums[...])
    upper = s[6] == 1
    for k in range(5):
        left, width = (0, 64) if k < 4 else (128, 32)
        weight, force = (
            total[row : row + 8, left : left + 128] for row in (8 * k, 40 + 8 * k)
        )
        weight = (0.125 if k < 4 else 0.125 * 0.125) * weight
        force = (0.5 * LEVEL[1] if k < 4 else 0.25 * LEVEL[2]) * force * inverse(weight)
        weight, force = (
            jnp.where(upper, pltpu.roll(tile, width, 1), tile) for tile in (weight, force)
        )
        out[(OWN["w1"] + k) if k < 4 else OWN["w2"]] = weight
        out[(OWN["h1"] + k) if k < 4 else OWN["h2"]] = force


def pack_x(s, fine, h1, h2, xp, at):
    upward = s[6] == 0
    start = jnp.where(upward, 12, 0)
    for k in range(4):
        for z in range(2):
            xp[at["h0"] + 2 * k + z] = fine(start + k, z)
    for k in range(2):
        xp[at["h1"] + k] = jnp.where(upward, h1[2 + k], h1[k])
    xp[at["h2"]] = h2


def first_sides_kernel(s, own, xp, coarse):
    total = [own[0, k] + own[1, k] for k in range(OWN["h1"], OWN["size"])]
    for k in range(COARSE["size"]):
        coarse[k] = total[k]
    h1, w1 = total[:4], total[4:8]
    h2, w2 = total[8:]
    pack_x(s, lambda x, z: own[z, x], h1, h2, xp, X_FIRST)
    upward = s[6] == 0
    edge = OWN["w"] + jnp.where(upward, 15, 0)
    for z in range(2):
        xp[X_FIRST["w"] + z] = own[z, edge]
    sub = sub_index()
    edge_one = jnp.where(upward, turn(w1[3], 4), w1[0])
    edge_two = jnp.where(upward, turn(w2, 6), turn(w2, 4))
    xp[X_FIRST["w12"]] = jnp.where(sub < 4, edge_one, edge_two)


def column_fine(own, planes, xr, at, lo, hi):
    def load(p, z):
        if p < planes:
            return xr[1, 0, at + 2 * p + z] * lo
        if p < 16 + planes:
            return own(p - planes, z)
        return xr[0, 1, at + 2 * (p - 16 - planes) + z] * hi

    return load


def pack_fine(load, planes, mine, yp, at):
    for k in range(planes // 2):
        for z in range(2):
            yp[at + 2 * k + z] = jnp.where(mine, load(2 * k, z), turn(load(2 * k + 1, z), 4))


def pack_y(s, own, h1, h2, xr, yp, y2p, x_at, at):
    lo, hi = flags(s)[:2]
    mine = (sub_index() < 4) == (s[6] == 1)
    pack_fine(column_fine(own, 4, xr, x_at["h0"], lo, hi), 24, mine, yp, at["h0"])
    for k in range(2):
        yp[at["h1"] + k] = xr[1, 0, x_at["h1"] + k] * lo
        yp[at["h1"] + 6 + k] = xr[0, 1, x_at["h1"] + k] * hi
    for k in range(4):
        yp[at["h1"] + 2 + k] = h1(k)
    two = [xr[1, 0, x_at["h2"]] * lo, h2(), xr[0, 1, x_at["h2"]] * hi]
    for k in range(3):
        yp[at["h2"] + k] = two[k]
        y2p[k] = two[k]


def first_rows_kernel(s, own, coarse, xr, yp, y2p):
    at = Y_FIRST
    pack_y(
        s,
        lambda x, z: own[z, x],
        lambda k: coarse[k],
        lambda: coarse[COARSE["h2"]],
        *(xr, yp, y2p, X_FIRST, at),
    )
    sub = sub_index()
    mine = (sub < 4) == (s[6] == 1)
    weights = column_fine(lambda x, z: own[z, OWN["w"] + x], 1, xr, X_FIRST["w"], 1.0, 1.0)
    pack_fine(weights, 18, mine, yp, at["w"])
    low, high = xr[1, 0, X_FIRST["w12"]], xr[0, 1, X_FIRST["w12"]]
    for k in range(4):
        yp[at["w1"] + k] = coarse[COARSE["w1"] + k]
    yp[at["w1"] + 4] = jnp.where(sub < 4, low, turn(high, 4))
    yp[at["w2"]] = coarse[COARSE["w2"]]
    yp[at["w2"] + 1] = jnp.where(sub < 2, turn(low, 4), turn(high, 6))


def second_rows_kernel(s, h0, h12, xr, yp, y2p):
    pack_y(
        s,
        lambda x, z: h0[x, z],
        lambda k: h12[k],
        lambda: h12[4],
        *(xr, yp, y2p, X_SECOND, Y_SECOND),
    )


def join_fine(load, planes, yr, at, ylo, yhi, out):
    sub = sub_index()
    for k in range(planes // 2):
        for z in range(2):
            above, below = yr[0, at + 2 * k + z] * yhi, yr[1, at + 2 * k + z] * ylo
            halos = (
                jnp.where(sub < 4, above, below),
                turn(jnp.where(sub < 4, below, above), 4),
            )
            for i in range(2):
                out[2 * k + i, z] = load(2 * k + i, z)
                out[2 * k + i, 2 + z] = halos[i]


def four_rows(own, above, below, i):
    sub = sub_index()
    turned = 4 * (1 - i)
    first = jnp.where(sub < 4, turn(own, 4 * i), turn(above, turned))
    return first, keep(sub >= 4, turn(below, turned))


def join_h1(s, yp, yr, at, out):
    ylo, yhi = flags(s)[2:4]
    for k in range(8):
        tile = at + k
        own, above, below = yp[tile], yr[0, tile] * yhi, yr[1, tile] * ylo
        for i in range(2):
            out[2 * k + i, 0], out[2 * k + i, 1] = four_rows(own, above, below, i)


def join_w1(yp, yr, out):
    for k in range(5):
        tile = Y_FIRST["w1"] + k
        own, above, below = yp[tile], yr[0, tile], yr[1, tile]
        for i in range(2):
            p = 9 * i if k == 4 else 1 + 2 * k + i
            first, second = four_rows(own, above, below, i)
            out[p, 0], out[p, 1] = 1.0 / first, inverse(second)


def join_h2(s, yp, yr, at, out):
    ylo, yhi, ylo2, yhi2 = flags(s)[2:]
    sub = sub_index()
    for k in range(3):
        tile, far = at["h2"] + k, at["far"] + k
        own, above, below = yp[tile], yr[0, tile] * yhi, yr[1, tile] * ylo
        above2, below2 = yr[0, far] * yhi2, yr[1, far] * ylo2
        for i in range(4):
            first = jnp.where(sub < 2, turn(own, -2 * i), turn(above, 2 - 2 * i))
            upper = keep(sub < 6, turn(above2, 4 - 2 * i))
            out[4 * k + i, 0] = jnp.where(sub < 4, first, upper)
            lower = jnp.where(sub < 6, turn(below2, 4 - 2 * i), turn(below, 6 - 2 * i))
            out[4 * k + i, 1] = keep(sub >= 4, lower)


def join_w2(yp, yr, out):
    sub = sub_index()
    for p in range(6):
        k, i = (1, p // 5) if p in (0, 5) else (0, p - 1)
        tile = Y_FIRST["w2"] + k
        own, above, below = yp[tile], yr[0, tile], yr[1, tile]
        first = jnp.where(sub < 2, turn(own, -2 * i), turn(above, 2 - 2 * i))
        out[p, 0] = inverse(keep(sub < 4, first))
        out[p, 1] = inverse(keep(sub >= 6, turn(below, 6 - 2 * i)))


def along_y(first, second):
    sub = sub_index()
    up_first, up_second = turn(first, 7), turn(second, 7)
    first = first + jnp.where(sub == 7, up_second, up_first)
    second = second + jnp.where(sub == 7, up_first, up_second)
    down_first, down_second = turn(first, 1), turn(second, 1)
    return (
        first + jnp.where(sub == 0, down_second, down_first),
        second + jnp.where(sub == 0, down_first, down_second),
    )


def along_z_fine(left, right):
    lane = lane_index()
    up_left, up_right = pltpu.roll(left, 127, 1), pltpu.roll(right, 127, 1)
    sum_left = left + jnp.where(lane < 127, up_left, up_right)
    sum_right = right + keep(lane < 127, up_right)
    down_left, down_right = pltpu.roll(sum_left, 1, 1), pltpu.roll(sum_right, 1, 1)
    return (
        sum_left + jnp.where(lane > 0, down_left, left),
        sum_right + jnp.where(lane > 0, down_right, down_left),
    )


def along_z_coarse(tile):
    lane = lane_index()
    summed = tile + keep(lane < 127, pltpu.roll(tile, 127, 1))
    return summed + jnp.where(lane > 0, pltpu.roll(summed, 1, 1), tile)


def along_yz(tiles):
    tiles = list(tiles)
    if len(tiles) == 4:
        for z in range(2):
            tiles[z], tiles[2 + z] = along_y(tiles[z], tiles[2 + z])
        for y in range(2):
            tiles[2 * y], tiles[2 * y + 1] = along_z_fine(tiles[2 * y], tiles[2 * y + 1])
        return tiles
    return [along_z_coarse(tile) for tile in along_y(*tiles)]


def added(first, second):
    return [a + b for a, b in zip(first, second)]


def relax(q, h, planes, parts, count, masks, lo, hi):
    sides = [[mask * factor for mask in masks] for factor in (lo, 1.0, hi)]

    def sweep(k, source):
        def load(x):
            return [source[x, part] for part in range(parts)]

        here = load(k)
        below = added(load(k - 1), here)
        for x in range(k, planes - k):
            after = load(x + 1)
            above = added(here, after)
            summed = along_yz(added(below, above))
            side = sides[0 if x < 4 else 2 if x >= planes - 4 else 1]
            for part in range(parts):
                spread = side[part // (parts // 2)] * summed[part]
                q[x, part] = (KEEP * here[part] + spread) + h[x, part]
            here, below = after, above

    @pl.when(count == 1)
    def _():
        q[...] = h[...]

    for k in range(1, 4):

        @pl.when(count > k)
        def _():
            sweep(k, h if k == 1 else q)


def relax_levels(s, cycle, h0, q0, h1, q1, h2, q2):
    lo, hi, ylo, yhi, ylo2, yhi2 = [flag * 1.0 for flag in flags(s)]
    sub, lane = sub_index(), lane_index()
    spread = jnp.full(TILE, SPREAD, F32)
    above = jnp.where(sub < 2, 1.0, jnp.where(sub < 4, yhi, jnp.where(sub < 6, yhi2, 0.0)))
    below = jnp.where(sub < 4, 0.0, jnp.where(sub < 6, ylo2, ylo))
    masks2 = (keep(lane < 64, above * spread), keep(lane < 64, below * spread))
    masks1 = (jnp.where(sub < 4, 1.0, yhi) * spread, jnp.where(sub < 4, 0.0, ylo) * spread)
    masks0 = (spread, jnp.where(sub < 4, yhi, ylo) * spread)
    relax(q2, h2, 12, 2, s[3 * cycle + 2], masks2, lo, hi)
    relax(q1, h1, 16, 2, s[3 * cycle + 1], masks1, lo, hi)
    relax(q0, h0, 24, 4, s[3 * cycle], masks0, lo, hi)


def corrections(q1, iw1, q2, iw2, copies):
    sub = sub_index()
    one, two = (
        [
            jnp.where(sub < 7, q[p + 3, 0] * iw[p, 0], q[p + 3, 1] * iw[p, 1])
            for p in range(planes)
        ]
        for q, iw, planes in ((q1, iw1, 10), (q2, iw2, 6))
    )
    spread = []
    for tile in two:
        inner = jnp.where(sub < 3, turn(tile, 1), turn(tile, 2))
        spread.append(jnp.where((sub == 0) | (sub == 7), tile, inner))
    rows = [jnp.concatenate([one[p], spread[(p + 1) // 2]], axis=1) for p in range(10)]
    return exact_dot(jnp.concatenate(rows, axis=0), copies[...])


def iterate(coarse, q0, w, before, out):
    sub = sub_index()
    for k in range(10):
        for z in range(2):
            tile = coarse[8 * k : 8 * k + 8, 128 * z : 128 * z + 128]
            turned = [tile] + [turn(tile, by) for by in range(1, 5)]
            rows = turned[4]
            for by, last in ((3, 6), (2, 4), (1, 2), (0, 0)):
                rows = jnp.where(sub <= last, turned[by], rows)
            halo = jnp.where(sub < 7, turned[4], tile)
            for p in (2 * k - 1, 2 * k):
                if 0 <= p < 18:
                    for part, value in ((z, rows), (2 + z, halo)):
                        total = q0[p + 3, part] + w[p, part] * value
                        if before is not None:
                            total = before[p, part] + total
                        out[p, part] = total


def defects(pf):
    def load(p):
        return [pf[p, part] for part in range(4)]

    here = load(1)
    below = added(load(0), here)
    for x in range(16):
        after = load(x + 2)
        above = added(here, after)
        summed = along_yz(added(below, above))
        yield here[:2], [SELF_WEIGHT * here[z] - SIDE_CUBE * summed[z] for z in range(2)]
        here, below = after, above


def middle_kernel(
    s, own, coarse, xr, yp, yr, sums, copies,
    xp, pf, w, iw1, iw2, h0_next, h12_next,
    h0_all, q0, h1_all, q1, h2_all, q2,
):
    lo, hi, ylo, yhi = flags(s)[:4]
    load = column_fine(lambda x, z: own[z, x], 4, xr, X_FIRST["h0"], lo, hi)
    join_fine(load, 24, yr, Y_FIRST["h0"], ylo, yhi, h0_all)
    load = column_fine(lambda x, z: own[z, OWN["w"] + x], 1, xr, X_FIRST["w"], 1.0, 1.0)
    join_fine(load, 18, yr, Y_FIRST["w"], 1.0, 1.0, w)
    join_h1(s, yp, yr, Y_FIRST["h1"], h1_all)
    join_w1(yp, yr, iw1)
    join_h2(s, yp, yr, Y_FIRST, h2_all)
    join_w2(yp, yr, iw2)
    relax_levels(s, 0, h0_all, q0, h1_all, q1, h2_all, q2)
    iterate(corrections(q1, iw1, q2, iw2, copies), q0, w, None, pf)

    rests = [[], []]
    for x, (_, defect) in enumerate(defects(pf)):
        for z in range(2):
            h0 = own[z, x] - LEVEL[0] * defect[z]
            h0_next[x, z] = h0
            rests[z].append(own[z, OWN["w"] + x] * h0)
    summed = [plane_sums(rest) for rest in rests]
    rows = [jnp.concatenate([summed[0][k], summed[1][k]], axis=1) for k in range(5)]
    total = exact_dot(jnp.concatenate(rows, axis=0), sums[...])
    h1 = []
    for k in range(4):
        weight = coarse[COARSE["w1"] + k]
        h1.append(0.5 * LEVEL[1] / LEVEL[0] * total[8 * k : 8 * k + 8, :128] / weight)
        h12_next[k] = h1[k]
    weight = inverse(coarse[COARSE["w2"]])
    h2 = 0.25 * LEVEL[2] / LEVEL[0] * total[32:40, 128:] * weight
    h12_next[4] = h2
    pack_x(s, lambda x, z: h0_next[x, z], h1, h2, xp, X_SECOND)


def last_kernel(
    s, m, f, h0, xr, yp, yr, pf, w, iw1, iw2, copies,
    solution_out, residual_out,
    h0_all, q0, h1_all, q1, h2_all, q2, pf_all,
):
    lo, hi, ylo, yhi = flags(s)[:4]
    load = column_fine(lambda x, z: h0[x, z], 4, xr, X_SECOND["h0"], lo, hi)
    join_fine(load, 24, yr, Y_SECOND["h0"], ylo, yhi, h0_all)
    join_h1(s, yp, yr, Y_SECOND["h1"], h1_all)
    join_h2(s, yp, yr, Y_SECOND, h2_all)
    relax_levels(s, 1, h0_all, q0, h1_all, q1, h2_all, q2)
    iterate(corrections(q1, iw1, q2, iw2, copies), q0, w, pf, pf_all)
    first = s[6] == 0
    for x, (here, defect) in enumerate(defects(pf_all)):
        mine, rest = (jnp.where(first, both[0], both[1]) for both in (here, defect))
        weight = m[x]
        solution_out[x] = mine / weight
        residual_out[x] = f[x] - weight * rest


def call(kernel, outs, scratch, name, *operands):
    smem = pl.BlockSpec(memory_space=pltpu.SMEM)
    vmem = pl.BlockSpec(memory_space=pltpu.VMEM)
    return pl.pallas_call(
        kernel,
        out_shape=[jax.ShapeDtypeStruct(shape, F32) for shape in outs],
        in_specs=[smem] + [vmem] * (len(operands) - 1),
        out_specs=[vmem] * len(outs),
        scratch_shapes=[pltpu.VMEM(shape, F32) for shape in scratch],
        compiler_params=pltpu.CompilerParams(vmem_limit_bytes=32 * 2**20),
        name=name,
    )(*operands)


def tiles(*dims):
    return (*dims, *TILE)


def pairs(axis, distance):
    size = lax.axis_size(axis)
    return [[i, size + (i + distance) % size] for i in range(size)]


def share(value):
    return lax.all_gather(value, "group", axis=0)


def trade_x(packed):
    both = lax.all_gather(packed, ("group", "gx"), axis=0, axis_index_groups=pairs("gx", 1))
    return share(both)


def swap(packed, distance):
    moves = [move for a, b in pairs("gy", distance) for move in ((a, b), (b, a))]
    return lax.ppermute(packed, ("group", "gy"), moves)


def trade_y(packed, packed_far):
    far = swap(packed_far, 2)
    near = swap(packed, 1)
    return share(jnp.concatenate([near, far], axis=0))


def on_device(forcing, metric, sweeps):
    gx, gy = lax.axis_index("gx"), lax.axis_index("gy")
    x_last, y_last = lax.axis_size("gx") - 1, lax.axis_size("gy") - 1
    places = [gx > 0, gx < x_last, gy > 0, gy < y_last, gy > 1, gy < y_last - 1]
    s = jnp.concatenate(
        [sweeps.reshape(-1), jnp.stack([lax.axis_index("group"), *places]).astype(jnp.int32)]
    )
    half_sums, sums, copies = (
        jnp.asarray(matrix, jnp.bfloat16) for matrix in (HALF_SUMS, WHOLE_SUMS, COPIES)
    )
    spaces = [tiles(24, 4)] * 2 + [tiles(16, 2)] * 2 + [tiles(12, 2)] * 2

    (own,) = call(
        first_kernel, [tiles(OWN["size"])], [], "block_sums", *(s, metric, forcing, half_sums)
    )
    own = share(own)
    xp, coarse = call(
        first_sides_kernel,
        [tiles(X_FIRST["size"]), tiles(COARSE["size"])],
        [],
        "first_sides",
        *(s, own),
    )
    xr = trade_x(xp)
    yp, y2p = call(
        first_rows_kernel,
        [tiles(Y_FIRST["size"]), tiles(3)],
        [],
        "first_rows",
        *(s, own, coarse, xr),
    )
    yr = trade_y(yp, y2p)
    xp, pf, w, iw1, iw2, h0, h12 = call(
        middle_kernel,
        [
            *(tiles(X_SECOND["size"]), tiles(18, 4), tiles(18, 4), tiles(10, 2), tiles(6, 2)),
            *(tiles(16, 2), tiles(5)),
        ],
        spaces,
        "first_cycle",
        *(s, own, coarse, xr, yp, yr, sums, copies),
    )
    xr = trade_x(xp)
    yp, y2p = call(
        second_rows_kernel,
        [tiles(Y_SECOND["size"]), tiles(3)],
        [],
        "second_rows",
        *(s, h0, h12, xr),
    )
    yr = trade_y(yp, y2p)
    return call(
        last_kernel,
        [tiles(16), tiles(16)],
        [*spaces, tiles(18, 4)],
        "second_cycle",
        *(s, metric, forcing, h0, xr, yp, yr, pf, w, iw1, iw2, copies),
    )


def solution(mesh):
    def program(forcing, metric, sweeps):
        return tuple(on_device(forcing, metric, sweeps))

    return jax.shard_map(
        program,
        mesh=mesh,
        in_specs=(P("gx", "gy", "group"), P("gx", "gy", "group"), P()),
        out_specs=(P("gx", "gy", "group"), P("gx", "gy", "group")),
        check_vma=False,
    )
```

time: 709 us -> 79.5 us (0.11)
  the two profiles are of different devices: /device:TPU:57 before, /device:TPU:1 now
where the time goes in v2:
time: 79.5 us; the launch traced here: 79.1 us
  blocking collectives  38.8 us (49%)
  starting transfers between devices  16.4 us (21%)
  waiting for transfers between devices  11.8 us (15%)
  Pallas kernels  7.98 us (10%)
  local copies, waits for them, and re-layouts  3.39 us (4%)
    all_gather x2, blocking collectives, trade_x(): lax.all_gather(packed, ('group', 'gx'), axis=0, axis_index_groups=pairs('...  21.8 us
    all_gather x5, blocking collectives, share(): return lax.all_gather(value, 'group', axis=0)  16.9 us
    ppermute x4, starting transfers between devices, swap(): return lax.ppermute(packed, ('group', 'gy'), moves)  16.4 us
    ppermute x4, waiting for transfers between devices, swap(): return lax.ppermute(packed, ('group', 'gy'), moves)  11.8 us
    pallas_call x6, Pallas kernels, call(): pl.pallas_call(kernel, out_shape=[jax.ShapeDtypeStruct(shape, F32) for sh...  7.98 us
    unnamed x16, local copies, waits for them, and re-layouts  3.22 us
  transfers between devices with their start and end apart: 4, of which 2 were waited for; matrix products, arithmetic and copies ran while one was open for 0% of the time, Pallas kernels for 0%

profile of v2, /device:TPU:1, one launch (start us, length us, event | category | flops | bytes accessed | tf_op | source)
XLA Modules:
  0.0 79.1 jit_solution(16455451823003547068)
XLA Ops:
  0.6 0.0 copy-start.7
  0.7 0.7 copy-done.7
  1.3 0.1 reshape.7
  1.4 0.1 concatenate.9.s
  1.5 0.0 copy-start.1
  1.5 0.8 %copy-done.1 = f32[16,8,128]{2,1,0:T(8,128)S(1)} copy-done((f32[16,8,128]{2,1,0:T(8,128)S(1)}, f32[16,8,128]{2,1,0:T(8,128)}, u32[]{:S(2)}) %copy-start.1) | copy-done | bytes 65560
  2.3 0.0 copy-start.3
  2.3 0.8 %copy-done.3 = f32[16,8,128]{2,1,0:T(8,128)S(1)} copy-done((f32[16,8,128]{2,1,0:T(8,128)S(1)}, f32[16,8,128]{2,1,0:T(8,128)}, u32[]{:S(2)}) %copy-start.3) | copy-done | bytes 65560
  3.2 0.0 copy-start.6
  3.2 0.8 %copy-done.6 = bf16[128,256]{1,0:T(8,128)(2,1)S(1)} copy-done((bf16[128,256]{1,0:T(8,128)(2,1)S(1)}, bf16[128,256]{1,0:T(8,128)(2,1)}, u32[]{:S(2)}) %copy-start.6) | copy-done | bytes 65560
  4.0 0.8 %block_sums.1 = f32[42,8,128]{2,1,0:T(8,128)S(1)} custom-call(s32[13]{0:T(128)S(1)} %concatenate.9.s, f32[16,8,128]{2,1,0:T(8,128)S(1)} %copy-done.1, f32[16,8,128]{2,1,0:T(8,128)S(1)} %copy-done.3, bf16[128,256]{1,0:T(8,128)(2,1)S(1)} %copy-done.6), custom_call_target="tpu_custom_call" | custom-call | tf_op jit(solution)/shard_map/block_sums/pallas_call | solution.py:480
  4.8 8.6 %all-gather = f32[84,8,128]{2,1,0:T(8,128)S(1)} all-gather(f32[42,8,128]{2,1,0:T(8,128)S(1)} %block_sums.1), channel_id=2, replica_groups=mesh['group'=2,'gx'=16,'gy'=16] {'group'}, dimensions={0}, use_global_device_ids=true | all-gather | bytes 516096 | tf_op jit(solution)/shard_map/all_gather | solution.py:501
  13.4 0.6 first_sides.1
  13.9 11.7 %all-gather.1 = f32[28,8,128]{2,1,0:T(8,128)S(1)} all-gather(f32[14,8,128]{2,1,0:T(8,128)S(1)} %get-tuple-element.16), channel_id=3, replica_groups={{0,272},{16,288},{32,304},{48,320},{64,336},{80,352},{96,368},{112,384}..., dimensions={0}, use_global_device_ids=true | all-gather | bytes 172032 | tf_op jit(solution)/shard_map/all_gather | solution.py:505
  25.6 2.0 %all-gather.2 = f32[4,14,8,128]{3,2,1,0:T(8,128)S(1)} all-gather(f32[2,14,8,128]{3,2,1,0:T(8,128)S(1)} %bitcast.23), channel_id=4, replica_groups=mesh['group'=2,'gx'=16,'gy'=16] {'group'}, dimensions={0}, use_global_device_ids=true | all-gather | bytes 344064 | tf_op jit(solution)/shard_map/all_gather | solution.py:501
  27.6 0.6 first_rows.1
  28.2 4.6 %collective-permute-start = (f32[60,8,128]{2,1,0:T(8,128)S(1)}, f32[60,8,128]{2,1,0:T(8,128)S(1)}, u32[]{:S(2)}, u32[]{:S(2)}) collective-permute-start(f32[60,8,128]{2,1,0:T(8,128)S(1)} %get-tuple-element.17.yp), channel_id=1, source_target_pairs={{0,257},{257,0},{1,258},{258,1},{2,259},{259,2},{3,260},{260,3},{4... | collective-permute-start | bytes 737288 | tf_op jit(solution)/shard_map/ppermute | solution.py:511
  32.8 3.3 %collective-permute-start.1 = (f32[3,8,128]{2,1,0:T(8,128)S(1)}, f32[3,8,128]{2,1,0:T(8,128)S(1)}, u32[]{:S(2)}, u32[]{:S(2)}) collective-permute-start(f32[3,8,128]{2,1,0:T(8,128)S(1)} %get-tuple-element.18), channel_id=1, source_target_pairs={{0,258},{258,0},{1,259},{259,1},{2,260},{260,2},{3,261},{261,3},{4... | collective-permute-start | bytes 36872 | tf_op jit(solution)/shard_map/ppermute | solution.py:511
  36.1 5.9 %collective-permute-done.1 = f32[3,8,128]{2,1,0:T(8,128)S(1)} collective-permute-done((f32[3,8,128]{2,1,0:T(8,128)S(1)}, f32[3,8,128]{2,1,0:T(8,128)S(1)}, u32[]{:S(2)}, u32[]{:S(2)}) %collective-permute-start.1) | collective-permute-done | bytes 12320 | tf_op jit(solution)/shard_map/ppermute | solution.py:511
  42.0 0.0 collective-permute-done
  42.0 0.0 copy-start
  42.0 0.0 copy-start.5
  42.0 2.3 %all-gather.3 = f32[126,8,128]{2,1,0:T(8,128)S(1)} all-gather(f32[63,8,128]{2,1,0:T(8,128)S(1)} %pad_maximum_fusion), channel_id=5, replica_groups=mesh['group'=2,'gx'=16,'gy'=16] {'group'}, dimensions={0}, use_global_device_ids=true | all-gather | bytes 774144 | tf_op jit(solution)/shard_map/all_gather | solution.py:501
  44.3 0.0 copy-done
  44.3 0.0 copy-done.5
  44.3 3.1 %first_cycle.1 = (f32[11,8,128]{2,1,0:T(8,128)S(1)}, f32[18,4,8,128]{3,2,1,0:T(8,128)S(1)}, f32[18,4,8,128]{3,2,1,0:T(8,128)S(1)}, f32[10,2,8,128]{3,2,1,0:T(8,1...) custom-call(s32[13]{0:T(128)S(1)} %concatenate.9.s, ...), custom_call_target="tpu_custom_call" | custom-call | tf_op jit(solution)/shard_map/first_cycle/pallas_call | solution.py:480
  47.4 10.2 %all-gather.4 = f32[22,8,128]{2,1,0:T(8,128)S(1)} all-gather(f32[11,8,128]{2,1,0:T(8,128)S(1)} %get-tuple-element.20), channel_id=6, replica_groups={{0,272},{16,288},{32,304},{48,320},{64,336},{80,352},{96,368},{112,384}..., dimensions={0}, use_global_device_ids=true | all-gather | bytes 135168 | tf_op jit(solution)/shard_map/all_gather | solution.py:505
  57.6 1.9 %all-gather.5 = f32[4,11,8,128]{3,2,1,0:T(8,128)S(1)} all-gather(f32[2,11,8,128]{3,2,1,0:T(8,128)S(1)} %bitcast.24), channel_id=7, replica_groups=mesh['group'=2,'gx'=16,'gy'=16] {'group'}, dimensions={0}, use_global_device_ids=true | all-gather | bytes 270336 | tf_op jit(solution)/shard_map/all_gather | solution.py:501
  59.5 0.6 second_rows.1
  60.1 5.1 %collective-permute-start.2 = (f32[35,8,128]{2,1,0:T(8,128)S(1)}, f32[35,8,128]{2,1,0:T(8,128)S(1)}, u32[]{:S(2)}, u32[]{:S(2)}) collective-permute-start(f32[35,8,128]{2,1,0:T(8,128)S(1)} %get-tuple-element.22.yp), channel_id=1, source_target_pairs={{0,257},{257,0},{1,258},{258,1},{2,259},{259,2},{3,260},{260,3},{4... | collective-permute-start | bytes 430088 | tf_op jit(solution)/shard_map/ppermute | solution.py:511
  65.2 3.3 %collective-permute-start.3 = (f32[3,8,128]{2,1,0:T(8,128)S(1)}, f32[3,8,128]{2,1,0:T(8,128)S(1)}, u32[]{:S(2)}, u32[]{:S(2)}) collective-permute-start(f32[3,8,128]{2,1,0:T(8,128)S(1)} %get-tuple-element.23), channel_id=1, source_target_pairs={{0,258},{258,0},{1,259},{259,1},{2,260},{260,2},{3,261},{261,3},{4... | collective-permute-start | bytes 36872 | tf_op jit(solution)/shard_map/ppermute | solution.py:511
  68.6 5.9 %collective-permute-done.3 = f32[3,8,128]{2,1,0:T(8,128)S(1)} collective-permute-done((f32[3,8,128]{2,1,0:T(8,128)S(1)}, f32[3,8,128]{2,1,0:T(8,128)S(1)}, u32[]{:S(2)}, u32[]{:S(2)}) %collective-permute-start.3) | collective-permute-done | bytes 12320 | tf_op jit(solution)/shard_map/ppermute | solution.py:511
  74.5 0.0 collective-permute-done.2
  74.5 0.0 copy-start.2
  74.5 0.0 copy-start.4
  74.5 2.2 %all-gather.6 = f32[76,8,128]{2,1,0:T(8,128)S(1)} all-gather(f32[38,8,128]{2,1,0:T(8,128)S(1)} %pad_maximum_fusion.1), channel_id=8, replica_groups=mesh['group'=2,'gx'=16,'gy'=16] {'group'}, dimensions={0}, use_global_device_ids=true | all-gather | bytes 466944 | tf_op jit(solution)/shard_map/all_gather | solution.py:501
  76.7 0.0 copy-done.2
  76.7 0.0 copy-done.4
  76.7 2.4 %second_cycle.1 = (f32[16,8,128]{2,1,0:T(8,128)}, f32[16,8,128]{2,1,0:T(8,128)}) custom-call(s32[13]{0:T(128)S(1)} %concatenate.9.s, f32[16,8,128]{2,1,0:T(8,128)S(1)} %copy-done.2, f32[16,8,128]{2,1,0:T(8,128)S(1)} %copy-done.4, f32[16,2,8,128]{3,2,1,0:T(8,128)S(1)} %get-tuple-element.19.h0, f32[2,2,11,8,128]{4,3,2,1,0:T(8,128)S(1)} %bitcast.21, ...), custom_call_target="tpu_custom_call" | custom-call | tf_op jit(solution)/shard_map/second_cycle/pallas_call | solution.py:480
  (2 shorter events, 0.0 us)
Async XLA Ops:
  0.6 0.7 copy-start.7
  1.5 0.8 %copy-start.1 = (f32[16,8,128]{2,1,0:T(8,128)S(1)}, f32[16,8,128]{2,1,0:T(8,128)}, u32[]{:S(2)}) copy-start(f32[16,8,128]{2,1,0:T(8,128)} %m.3) | copy-start | bytes 196612
  2.3 0.8 %copy-start.3 = (f32[16,8,128]{2,1,0:T(8,128)S(1)}, f32[16,8,128]{2,1,0:T(8,128)}, u32[]{:S(2)}) copy-start(f32[16,8,128]{2,1,0:T(8,128)} %f.3) | copy-start | bytes 196612
  3.2 0.8 %copy-start.6 = (bf16[128,256]{1,0:T(8,128)(2,1)S(1)}, bf16[128,256]{1,0:T(8,128)(2,1)}, u32[]{:S(2)}) copy-start(bf16[128,256]{1,0:T(8,128)(2,1)} %constant.27.clone.sums) | copy-start | bytes 196612
  28.2 13.8 %collective-permute-start = (f32[60,8,128]{2,1,0:T(8,128)S(1)}, f32[60,8,128]{2,1,0:T(8,128)S(1)}, u32[]{:S(2)}, u32[]{:S(2)}) collective-permute-start(f32[60,8,128]{2,1,0:T(8,128)S(1)} %get-tuple-element.17.yp), channel_id=1, source_target_pairs={{0,257},{257,0},{1,258},{258,1},{2,259},{259,2},{3,260},{260,3},{4... | collective-permute-start | bytes 737288 | tf_op jit(solution)/shard_map/ppermute | solution.py:511
  32.8 9.2 %collective-permute-start.1 = (f32[3,8,128]{2,1,0:T(8,128)S(1)}, f32[3,8,128]{2,1,0:T(8,128)S(1)}, u32[]{:S(2)}, u32[]{:S(2)}) collective-permute-start(f32[3,8,128]{2,1,0:T(8,128)S(1)} %get-tuple-element.18), channel_id=1, source_target_pairs={{0,258},{258,0},{1,259},{259,1},{2,260},{260,2},{3,261},{261,3},{4... | collective-permute-start | bytes 36872 | tf_op jit(solution)/shard_map/ppermute | solution.py:511
  42.0 2.3 %copy-start = (bf16[256,256]{1,0:T(8,128)(2,1)S(1)}, bf16[256,256]{1,0:T(8,128)(2,1)}, u32[]{:S(2)}) copy-start(bf16[256,256]{1,0:T(8,128)(2,1)} %constant.29.clone.copies) | copy-start | bytes 393220
  42.0 2.3 %copy-start.5 = (bf16[256,256]{1,0:T(8,128)(2,1)S(1)}, bf16[256,256]{1,0:T(8,128)(2,1)}, u32[]{:S(2)}) copy-start(bf16[256,256]{1,0:T(8,128)(2,1)} %constant.28.clone.sums) | copy-start | bytes 393220
  60.1 14.4 %collective-permute-start.2 = (f32[35,8,128]{2,1,0:T(8,128)S(1)}, f32[35,8,128]{2,1,0:T(8,128)S(1)}, u32[]{:S(2)}, u32[]{:S(2)}) collective-permute-start(f32[35,8,128]{2,1,0:T(8,128)S(1)} %get-tuple-element.22.yp), channel_id=1, source_target_pairs={{0,257},{257,0},{1,258},{258,1},{2,259},{259,2},{3,260},{260,3},{4... | collective-permute-start | bytes 430088 | tf_op jit(solution)/shard_map/ppermute | solution.py:511
  65.2 9.2 %collective-permute-start.3 = (f32[3,8,128]{2,1,0:T(8,128)S(1)}, f32[3,8,128]{2,1,0:T(8,128)S(1)}, u32[]{:S(2)}, u32[]{:S(2)}) collective-permute-start(f32[3,8,128]{2,1,0:T(8,128)S(1)} %get-tuple-element.23), channel_id=1, source_target_pairs={{0,258},{258,0},{1,259},{259,1},{2,260},{260,2},{3,261},{261,3},{4... | collective-permute-start | bytes 36872 | tf_op jit(solution)/shard_map/ppermute | solution.py:511
  74.5 2.2 %copy-start.2 = (f32[16,8,128]{2,1,0:T(8,128)S(1)}, f32[16,8,128]{2,1,0:T(8,128)}, u32[]{:S(2)}) copy-start(f32[16,8,128]{2,1,0:T(8,128)} %m.3) | copy-start | bytes 196612
  74.5 2.2 %copy-start.4 = (f32[16,8,128]{2,1,0:T(8,128)S(1)}, f32[16,8,128]{2,1,0:T(8,128)}, u32[]{:S(2)}) copy-start(f32[16,8,128]{2,1,0:T(8,128)} %f.3) | copy-start | bytes 196612

commit v3 on v2

--- a/solution.py
+++ b/solution.py
@@ -26,9 +26,6 @@
 Y_SECOND = dict(h0=0, h1=24, h2=32, size=35, far=35)
 
 LANES = np.arange(256)
-HALF_SUMS = np.concatenate(
-    [LANES[:128, None] // 2 == LANES[None, :128], LANES[:128, None] // 4 == LANES[None, :128]], axis=1
-).astype(np.float32)
 WHOLE_SUMS = np.concatenate(
     [LANES[:, None] // 2 == LANES[None, :128], LANES[:, None] // 4 == LANES[None, :128]], axis=1
 ).astype(np.float32)
@@ -72,8 +69,15 @@
     return jnp.where(tile > 0, 1.0 / jnp.where(tile > 0, tile, 1.0), 0.0)
 
 
-def flags(s):
-    return [s[k].astype(F32) for k in range(7, 13)]
+def core():
+    return lax.axis_index("group")
+
+
+def flags():
+    gx, gy = lax.axis_index("gx"), lax.axis_index("gy")
+    x_last, y_last = lax.axis_size("gx") - 1, lax.axis_size("gy") - 1
+    places = [gx > 0, gx < x_last, gy > 0, gy < y_last, gy > 1, gy < y_last - 1]
+    return [place.astype(F32) for place in places]
 
 
 def pair_rows(first, second):
@@ -99,14 +103,30 @@
     return one + [two]
 
 
-def first_kernel(s, m, f, sums, out):
+def half_sums():
+    row = lax.broadcasted_iota(jnp.int32, (128, 128), 0)
+    column = lax.broadcasted_iota(jnp.int32, (128, 128), 1)
+    matrix = jnp.concatenate([row >> 1 == column, row >> 2 == column], axis=1)
+    return jnp.where(matrix, 1.0, 0.0).astype(jnp.bfloat16)
+
+
+def first_kernel(m_whole, f_whole, out, m, f, arrived):
+    copies = [
+        pltpu.make_async_copy(source, target, arrived.at[k])
+        for k, (source, target) in enumerate(((m_whole, m), (f_whole, f)))
+    ]
+    for copy in copies:
+        copy.start()
+    sums = half_sums()
+    for copy in copies:
+        copy.wait()
     m_tiles, f_tiles = ([ref[x] for x in range(16)] for ref in (m, f))
     for x in range(16):
         out[OWN["h0"] + x] = LEVEL[0] * f_tiles[x] / m_tiles[x]
         out[OWN["w"] + x] = m_tiles[x]
     rows = jnp.concatenate(plane_sums(m_tiles) + plane_sums(f_tiles), axis=0)
-    total = exact_dot(rows, sums[...])
-    upper = s[6] == 1
+    total = exact_dot(rows, sums)
+    upper = core() == 1
     for k in range(5):
         left, width = (0, 64) if k < 4 else (128, 32)
         weight, force = (
@@ -121,8 +141,8 @@
         out[(OWN["h1"] + k) if k < 4 else OWN["h2"]] = force
 
 
-def pack_x(s, fine, h1, h2, xp, at):
-    upward = s[6] == 0
+def pack_x(fine, h1, h2, xp, at):
+    upward = core() == 0
     start = jnp.where(upward, 12, 0)
     for k in range(4):
         for z in range(2):
@@ -132,14 +152,14 @@
     xp[at["h2"]] = h2
 
 
-def first_sides_kernel(s, own, xp, coarse):
+def first_sides_kernel(own, xp, coarse):
     total = [own[0, k] + own[1, k] for k in range(OWN["h1"], OWN["size"])]
     for k in range(COARSE["size"]):
         coarse[k] = total[k]
     h1, w1 = total[:4], total[4:8]
     h2, w2 = total[8:]
-    pack_x(s, lambda x, z: own[z, x], h1, h2, xp, X_FIRST)
-    upward = s[6] == 0
+    pack_x(lambda x, z: own[z, x], h1, h2, xp, X_FIRST)
+    upward = core() == 0
     edge = OWN["w"] + jnp.where(upward, 15, 0)
     for z in range(2):
         xp[X_FIRST["w"] + z] = own[z, edge]
@@ -166,9 +186,9 @@
             yp[at + 2 * k + z] = jnp.where(mine, load(2 * k, z), turn(load(2 * k + 1, z), 4))
 
 
-def pack_y(s, own, h1, h2, xr, yp, y2p, x_at, at):
-    lo, hi = flags(s)[:2]
-    mine = (sub_index() < 4) == (s[6] == 1)
+def pack_y(own, h1, h2, xr, yp, y2p, x_at, at):
+    lo, hi = flags()[:2]
+    mine = (sub_index() < 4) == (core() == 1)
     pack_fine(column_fine(own, 4, xr, x_at["h0"], lo, hi), 24, mine, yp, at["h0"])
     for k in range(2):
         yp[at["h1"] + k] = xr[1, 0, x_at["h1"] + k] * lo
@@ -181,17 +201,16 @@
         y2p[k] = two[k]
 
 
-def first_rows_kernel(s, own, coarse, xr, yp, y2p):
+def first_rows_kernel(own, coarse, xr, yp, y2p):
     at = Y_FIRST
     pack_y(
-        s,
         lambda x, z: own[z, x],
         lambda k: coarse[k],
         lambda: coarse[COARSE["h2"]],
         *(xr, yp, y2p, X_FIRST, at),
     )
     sub = sub_index()
-    mine = (sub < 4) == (s[6] == 1)
+    mine = (sub < 4) == (core() == 1)
     weights = column_fine(lambda x, z: own[z, OWN["w"] + x], 1, xr, X_FIRST["w"], 1.0, 1.0)
     pack_fine(weights, 18, mine, yp, at["w"])
     low, high = xr[1, 0, X_FIRST["w12"]], xr[0, 1, X_FIRST["w12"]]
@@ -202,9 +221,8 @@
     yp[at["w2"] + 1] = jnp.where(sub < 2, turn(low, 4), turn(high, 6))
 
 
-def second_rows_kernel(s, h0, h12, xr, yp, y2p):
+def second_rows_kernel(h0, h12, xr, yp, y2p):
     pack_y(
-        s,
         lambda x, z: h0[x, z],
         lambda k: h12[k],
         lambda: h12[4],
@@ -233,8 +251,8 @@
     return first, keep(sub >= 4, turn(below, turned))
 
 
-def join_h1(s, yp, yr, at, out):
-    ylo, yhi = flags(s)[2:4]
+def join_h1(yp, yr, at, out):
+    ylo, yhi = flags()[2:4]
     for k in range(8):
         tile = at + k
         own, above, below = yp[tile], yr[0, tile] * yhi, yr[1, tile] * ylo
@@ -252,8 +270,8 @@
             out[p, 0], out[p, 1] = 1.0 / first, inverse(second)
 
 
-def join_h2(s, yp, yr, at, out):
-    ylo, yhi, ylo2, yhi2 = flags(s)[2:]
+def join_h2(yp, yr, at, out):
+    ylo, yhi, ylo2, yhi2 = flags()[2:]
     sub = sub_index()
     for k in range(3):
         tile, far = at["h2"] + k, at["far"] + k
@@ -353,8 +371,8 @@
             sweep(k, h if k == 1 else q)
 
 
-def relax_levels(s, cycle, h0, q0, h1, q1, h2, q2):
-    lo, hi, ylo, yhi, ylo2, yhi2 = [flag * 1.0 for flag in flags(s)]
+def relax_levels(counts, cycle, h0, q0, h1, q1, h2, q2):
+    lo, hi, ylo, yhi, ylo2, yhi2 = [flag * 1.0 for flag in flags()]
     sub, lane = sub_index(), lane_index()
     spread = jnp.full(TILE, SPREAD, F32)
     above = jnp.where(sub < 2, 1.0, jnp.where(sub < 4, yhi, jnp.where(sub < 6, yhi2, 0.0)))
@@ -362,9 +380,9 @@
     masks2 = (keep(lane < 64, above * spread), keep(lane < 64, below * spread))
     masks1 = (jnp.where(sub < 4, 1.0, yhi) * spread, jnp.where(sub < 4, 0.0, ylo) * spread)
     masks0 = (spread, jnp.where(sub < 4, yhi, ylo) * spread)
-    relax(q2, h2, 12, 2, s[3 * cycle + 2], masks2, lo, hi)
-    relax(q1, h1, 16, 2, s[3 * cycle + 1], masks1, lo, hi)
-    relax(q0, h0, 24, 4, s[3 * cycle], masks0, lo, hi)
+    relax(q2, h2, 12, 2, counts[cycle, 2], masks2, lo, hi)
+    relax(q1, h1, 16, 2, counts[cycle, 1], masks1, lo, hi)
+    relax(q0, h0, 24, 4, counts[cycle, 0], masks0, lo, hi)
 
 
 def corrections(q1, iw1, q2, iw2, copies):
@@ -418,20 +436,23 @@
 
 
 def middle_kernel(
-    s, own, coarse, xr, yp, yr, sums, copies,
+    sweeps, own, coarse, xr, yp, yr, sums, copies,
     xp, pf, w, iw1, iw2, h0_next, h12_next,
-    h0_all, q0, h1_all, q1, h2_all, q2,
+    h0_all, q0, h1_all, q1, h2_all, q2, counts, arrived,
 ):
-    lo, hi, ylo, yhi = flags(s)[:4]
+    counting = pltpu.make_async_copy(sweeps, counts, arrived)
+    counting.start()
+    lo, hi, ylo, yhi = flags()[:4]
     load = column_fine(lambda x, z: own[z, x], 4, xr, X_FIRST["h0"], lo, hi)
     join_fine(load, 24, yr, Y_FIRST["h0"], ylo, yhi, h0_all)
     load = column_fine(lambda x, z: own[z, OWN["w"] + x], 1, xr, X_FIRST["w"], 1.0, 1.0)
     join_fine(load, 18, yr, Y_FIRST["w"], 1.0, 1.0, w)
-    join_h1(s, yp, yr, Y_FIRST["h1"], h1_all)
+    join_h1(yp, yr, Y_FIRST["h1"], h1_all)
     join_w1(yp, yr, iw1)
-    join_h2(s, yp, yr, Y_FIRST, h2_all)
+    join_h2(yp, yr, Y_FIRST, h2_all)
     join_w2(yp, yr, iw2)
-    relax_levels(s, 0, h0_all, q0, h1_all, q1, h2_all, q2)
+    counting.wait()
+    relax_levels(counts, 0, h0_all, q0, h1_all, q1, h2_all, q2)
     iterate(corrections(q1, iw1, q2, iw2, copies), q0, w, None, pf)
 
     rests = [[], []]
@@ -451,22 +472,25 @@
     weight = inverse(coarse[COARSE["w2"]])
     h2 = 0.25 * LEVEL[2] / LEVEL[0] * total[32:40, 128:] * weight
     h12_next[4] = h2
-    pack_x(s, lambda x, z: h0_next[x, z], h1, h2, xp, X_SECOND)
+    pack_x(lambda x, z: h0_next[x, z], h1, h2, xp, X_SECOND)
 
 
 def last_kernel(
-    s, m, f, h0, xr, yp, yr, pf, w, iw1, iw2, copies,
+    sweeps, m, f, h0, xr, yp, yr, pf, w, iw1, iw2, copies,
     solution_out, residual_out,
-    h0_all, q0, h1_all, q1, h2_all, q2, pf_all,
+    h0_all, q0, h1_all, q1, h2_all, q2, counts, arrived, pf_all,
 ):
-    lo, hi, ylo, yhi = flags(s)[:4]
+    counting = pltpu.make_async_copy(sweeps, counts, arrived)
+    counting.start()
+    lo, hi, ylo, yhi = flags()[:4]
     load = column_fine(lambda x, z: h0[x, z], 4, xr, X_SECOND["h0"], lo, hi)
     join_fine(load, 24, yr, Y_SECOND["h0"], ylo, yhi, h0_all)
-    join_h1(s, yp, yr, Y_SECOND["h1"], h1_all)
-    join_h2(s, yp, yr, Y_SECOND, h2_all)
-    relax_levels(s, 1, h0_all, q0, h1_all, q1, h2_all, q2)
+    join_h1(yp, yr, Y_SECOND["h1"], h1_all)
+    join_h2(yp, yr, Y_SECOND, h2_all)
+    counting.wait()
+    relax_levels(counts, 1, h0_all, q0, h1_all, q1, h2_all, q2)
     iterate(corrections(q1, iw1, q2, iw2, copies), q0, w, pf, pf_all)
-    first = s[6] == 0
+    first = core() == 0
     for x, (here, defect) in enumerate(defects(pf_all)):
         mine, rest = (jnp.where(first, both[0], both[1]) for both in (here, defect))
         weight = m[x]
@@ -474,18 +498,22 @@
         residual_out[x] = f[x] - weight * rest
 
 
-def call(kernel, outs, scratch, name, *operands):
-    smem = pl.BlockSpec(memory_space=pltpu.SMEM)
+def call(kernel, outs, scratch, name, *operands, outside=0):
+    whole = pl.BlockSpec(memory_space=pltpu.HBM)
     vmem = pl.BlockSpec(memory_space=pltpu.VMEM)
     return pl.pallas_call(
         kernel,
         out_shape=[jax.ShapeDtypeStruct(shape, F32) for shape in outs],
-        in_specs=[smem] + [vmem] * (len(operands) - 1),
+        in_specs=[whole] * outside + [vmem] * (len(operands) - outside),
         out_specs=[vmem] * len(outs),
-        scratch_shapes=[pltpu.VMEM(shape, F32) for shape in scratch],
+        scratch_shapes=scratch,
         compiler_params=pltpu.CompilerParams(vmem_limit_bytes=32 * 2**20),
         name=name,
     )(*operands)
+
+
+def space(*dims):
+    return pltpu.VMEM(tiles(*dims), F32)
 
 
 def tiles(*dims):
@@ -518,19 +546,17 @@
 
 
 def on_device(forcing, metric, sweeps):
-    gx, gy = lax.axis_index("gx"), lax.axis_index("gy")
-    x_last, y_last = lax.axis_size("gx") - 1, lax.axis_size("gy") - 1
-    places = [gx > 0, gx < x_last, gy > 0, gy < y_last, gy > 1, gy < y_last - 1]
-    s = jnp.concatenate(
-        [sweeps.reshape(-1), jnp.stack([lax.axis_index("group"), *places]).astype(jnp.int32)]
-    )
-    half_sums, sums, copies = (
-        jnp.asarray(matrix, jnp.bfloat16) for matrix in (HALF_SUMS, WHOLE_SUMS, COPIES)
-    )
-    spaces = [tiles(24, 4)] * 2 + [tiles(16, 2)] * 2 + [tiles(12, 2)] * 2
+    sums, copies = (jnp.asarray(matrix, jnp.bfloat16) for matrix in (WHOLE_SUMS, COPIES))
+    spaces = [space(24, 4)] * 2 + [space(16, 2)] * 2 + [space(12, 2)] * 2
+    spaces += [pltpu.SMEM(sweeps.shape, jnp.int32), pltpu.SemaphoreType.DMA]
 
     (own,) = call(
-        first_kernel, [tiles(OWN["size"])], [], "block_sums", *(s, metric, forcing, half_sums)
+        first_kernel,
+        [tiles(OWN["size"])],
+        [space(16), space(16), pltpu.SemaphoreType.DMA((2,))],
+        "block_sums",
+        *(metric, forcing),
+        outside=2,
     )
     own = share(own)
     xp, coarse = call(
@@ -538,7 +564,7 @@
         [tiles(X_FIRST["size"]), tiles(COARSE["size"])],
         [],
         "first_sides",
-        *(s, own),
+        own,
     )
     xr = trade_x(xp)
     yp, y2p = call(
@@ -546,7 +572,7 @@
         [tiles(Y_FIRST["size"]), tiles(3)],
         [],
         "first_rows",
-        *(s, own, coarse, xr),
+        *(own, coarse, xr),
     )
     yr = trade_y(yp, y2p)
     xp, pf, w, iw1, iw2, h0, h12 = call(
@@ -557,7 +583,8 @@
         ],
         spaces,
         "first_cycle",
-        *(s, own, coarse, xr, yp, yr, sums, copies),
+        *(sweeps, own, coarse, xr, yp, yr, sums, copies),
+        outside=1,
     )
     xr = trade_x(xp)
     yp, y2p = call(
@@ -565,15 +592,16 @@
         [tiles(Y_SECOND["size"]), tiles(3)],
         [],
         "second_rows",
-        *(s, h0, h12, xr),
+        *(h0, h12, xr),
     )
     yr = trade_y(yp, y2p)
     return call(
         last_kernel,
         [tiles(16), tiles(16)],
-        [*spaces, tiles(18, 4)],
+        [*spaces, space(18, 4)],
         "second_cycle",
-        *(s, metric, forcing, h0, xr, yp, yr, pf, w, iw1, iw2, copies),
+        *(sweeps, metric, forcing, h0, xr, yp, yr, pf, w, iw1, iw2, copies),
+        outside=1,
     )
 
 

time: 79.5 us -> 75.9 us (0.955)
  Pallas kernels: 7.98 us -> 5.4 us
  local copies, waits for them, and re-layouts: 3.39 us -> 2.37 us
    pallas_call x6, Pallas kernels: 7.98 us -> 5.4 us  [call(): pl.pallas_call(kernel, out_shape=[jax.ShapeDtypeStruct(shape, F32) for sh...]
    unnamed x16 -> x14, local copies, waits for them, and re-layouts: 3.22 us -> 2.37 us
where the time goes in v3:
time: 75.9 us; the launch traced here: 75.5 us
  blocking collectives  38.8 us (51%)
  starting transfers between devices  16.4 us (22%)
  waiting for transfers between devices  11.8 us (16%)
  Pallas kernels  5.4 us (7%)
  local copies, waits for them, and re-layouts  2.37 us (3%)
    all_gather x2, blocking collectives, trade_x(): lax.all_gather(packed, ('group', 'gx'), axis=0, axis_index_groups=pairs('...  21.8 us
    all_gather x5, blocking collectives, share(): return lax.all_gather(value, 'group', axis=0)  16.9 us
    ppermute x4, starting transfers between devices, swap(): return lax.ppermute(packed, ('group', 'gy'), moves)  16.4 us
    ppermute x4, waiting for transfers between devices, swap(): return lax.ppermute(packed, ('group', 'gy'), moves)  11.8 us
    pallas_call x6, Pallas kernels, call(): pl.pallas_call(kernel, out_shape=[jax.ShapeDtypeStruct(shape, F32) for sh...  5.4 us
    unnamed x14, local copies, waits for them, and re-layouts  2.37 us
  transfers between devices with their start and end apart: 4, of which 2 were waited for; matrix products, arithmetic and copies ran while one was open for 0% of the time, Pallas kernels for 0%

profile of v3, /device:TPU:1, one launch (start us, length us, event | category | flops | bytes accessed | tf_op | source)
XLA Modules:
  0.0 75.5 jit_solution(15429637140598250037)
XLA Ops:
  0.6 0.0 copy-start.1
  0.6 0.8 %copy-done.1 = f32[16,8,128]{2,1,0:T(8,128)S(1)} copy-done((f32[16,8,128]{2,1,0:T(8,128)S(1)}, f32[16,8,128]{2,1,0:T(8,128)}, u32[]{:S(2)}) %copy-start.1) | copy-done | bytes 65560
  1.5 0.0 copy-start.3
  1.5 0.8 %copy-done.3 = f32[16,8,128]{2,1,0:T(8,128)S(1)} copy-done((f32[16,8,128]{2,1,0:T(8,128)S(1)}, f32[16,8,128]{2,1,0:T(8,128)}, u32[]{:S(2)}) %copy-start.3) | copy-done | bytes 65560
  2.3 0.4 block_sums.1
  2.7 8.6 %all-gather = f32[84,8,128]{2,1,0:T(8,128)S(1)} all-gather(f32[42,8,128]{2,1,0:T(8,128)S(1)} %block_sums.1), channel_id=2, replica_groups=mesh['group'=2,'gx'=16,'gy'=16] {'group'}, dimensions={0}, use_global_device_ids=true | all-gather | bytes 516096 | tf_op jit(solution)/shard_map/all_gather | solution.py:529
  11.3 11.7 %all-gather.1 = f32[28,8,128]{2,1,0:T(8,128)S(1)} all-gather(f32[14,8,128]{2,1,0:T(8,128)S(1)} %get-tuple-element.16), channel_id=3, replica_groups={{0,272},{16,288},{32,304},{48,320},{64,336},{80,352},{96,368},{112,384}..., dimensions={0}, use_global_device_ids=true | all-gather | bytes 172032 | tf_op jit(solution)/shard_map/all_gather | solution.py:533
  23.0 2.0 %all-gather.2 = f32[4,14,8,128]{3,2,1,0:T(8,128)S(1)} all-gather(f32[2,14,8,128]{3,2,1,0:T(8,128)S(1)} %bitcast.16), channel_id=4, replica_groups=mesh['group'=2,'gx'=16,'gy'=16] {'group'}, dimensions={0}, use_global_device_ids=true | all-gather | bytes 344064 | tf_op jit(solution)/shard_map/all_gather | solution.py:529
  25.0 4.6 %collective-permute-start = (f32[60,8,128]{2,1,0:T(8,128)S(1)}, f32[60,8,128]{2,1,0:T(8,128)S(1)}, u32[]{:S(2)}, u32[]{:S(2)}) collective-permute-start(f32[60,8,128]{2,1,0:T(8,128)S(1)} %get-tuple-element.17.yp), channel_id=1, source_target_pairs={{0,257},{257,0},{1,258},{258,1},{2,259},{259,2},{3,260},{260,3},{4... | collective-permute-start | bytes 737288 | tf_op jit(solution)/shard_map/ppermute | solution.py:539
  29.6 3.3 %collective-permute-start.1 = (f32[3,8,128]{2,1,0:T(8,128)S(1)}, f32[3,8,128]{2,1,0:T(8,128)S(1)}, u32[]{:S(2)}, u32[]{:S(2)}) collective-permute-start(f32[3,8,128]{2,1,0:T(8,128)S(1)} %get-tuple-element.18), channel_id=1, source_target_pairs={{0,258},{258,0},{1,259},{259,1},{2,260},{260,2},{3,261},{261,3},{4... | collective-permute-start | bytes 36872 | tf_op jit(solution)/shard_map/ppermute | solution.py:539
  33.0 5.9 %collective-permute-done.1 = f32[3,8,128]{2,1,0:T(8,128)S(1)} collective-permute-done((f32[3,8,128]{2,1,0:T(8,128)S(1)}, f32[3,8,128]{2,1,0:T(8,128)S(1)}, u32[]{:S(2)}, u32[]{:S(2)}) %collective-permute-start.1) | collective-permute-done | bytes 12320 | tf_op jit(solution)/shard_map/ppermute | solution.py:539
  38.8 0.0 collective-permute-done
  38.9 0.0 copy-start
  38.9 0.0 copy-start.5
  38.9 2.3 %all-gather.3 = f32[126,8,128]{2,1,0:T(8,128)S(1)} all-gather(f32[63,8,128]{2,1,0:T(8,128)S(1)} %pad_maximum_fusion), channel_id=5, replica_groups=mesh['group'=2,'gx'=16,'gy'=16] {'group'}, dimensions={0}, use_global_device_ids=true | all-gather | bytes 774144 | tf_op jit(solution)/shard_map/all_gather | solution.py:529
  41.2 0.0 copy-start.6
  41.2 0.0 copy-done
  41.2 0.0 copy-done.5
  41.2 0.7 copy-done.6
  41.9 1.7 %first_cycle.1 = (f32[11,8,128]{2,1,0:T(8,128)S(1)}, f32[18,4,8,128]{3,2,1,0:T(8,128)S(1)}, f32[18,4,8,128]{3,2,1,0:T(8,128)S(1)}, f32[10,2,8,128]{3,2,1,0:T(8,1...) custom-call(s32[2,3]{1,0:T(2,128)S(1)} %copy-done.6, ...), custom_call_target="tpu_custom_call" | custom-call | tf_op jit(solution)/shard_map/first_cycle/pallas_call | solution.py:504
  43.6 10.2 %all-gather.4 = f32[22,8,128]{2,1,0:T(8,128)S(1)} all-gather(f32[11,8,128]{2,1,0:T(8,128)S(1)} %get-tuple-element.20), channel_id=6, replica_groups={{0,272},{16,288},{32,304},{48,320},{64,336},{80,352},{96,368},{112,384}..., dimensions={0}, use_global_device_ids=true | all-gather | bytes 135168 | tf_op jit(solution)/shard_map/all_gather | solution.py:533
  53.8 1.9 %all-gather.5 = f32[4,11,8,128]{3,2,1,0:T(8,128)S(1)} all-gather(f32[2,11,8,128]{3,2,1,0:T(8,128)S(1)} %bitcast.17), channel_id=7, replica_groups=mesh['group'=2,'gx'=16,'gy'=16] {'group'}, dimensions={0}, use_global_device_ids=true | all-gather | bytes 270336 | tf_op jit(solution)/shard_map/all_gather | solution.py:529
  55.7 5.1 %collective-permute-start.2 = (f32[35,8,128]{2,1,0:T(8,128)S(1)}, f32[35,8,128]{2,1,0:T(8,128)S(1)}, u32[]{:S(2)}, u32[]{:S(2)}) collective-permute-start(f32[35,8,128]{2,1,0:T(8,128)S(1)} %get-tuple-element.22.yp), channel_id=1, source_target_pairs={{0,257},{257,0},{1,258},{258,1},{2,259},{259,2},{3,260},{260,3},{4... | collective-permute-start | bytes 430088 | tf_op jit(solution)/shard_map/ppermute | solution.py:539
  60.9 3.3 %collective-permute-start.3 = (f32[3,8,128]{2,1,0:T(8,128)S(1)}, f32[3,8,128]{2,1,0:T(8,128)S(1)}, u32[]{:S(2)}, u32[]{:S(2)}) collective-permute-start(f32[3,8,128]{2,1,0:T(8,128)S(1)} %get-tuple-element.23), channel_id=1, source_target_pairs={{0,258},{258,0},{1,259},{259,1},{2,260},{260,2},{3,261},{261,3},{4... | collective-permute-start | bytes 36872 | tf_op jit(solution)/shard_map/ppermute | solution.py:539
  64.2 5.9 %collective-permute-done.3 = f32[3,8,128]{2,1,0:T(8,128)S(1)} collective-permute-done((f32[3,8,128]{2,1,0:T(8,128)S(1)}, f32[3,8,128]{2,1,0:T(8,128)S(1)}, u32[]{:S(2)}, u32[]{:S(2)}) %collective-permute-start.3) | collective-permute-done | bytes 12320 | tf_op jit(solution)/shard_map/ppermute | solution.py:539
  70.1 0.0 collective-permute-done.2
  70.1 0.0 copy-start.2
  70.1 0.0 copy-start.4
  70.1 2.2 %all-gather.6 = f32[76,8,128]{2,1,0:T(8,128)S(1)} all-gather(f32[38,8,128]{2,1,0:T(8,128)S(1)} %pad_maximum_fusion.1), channel_id=8, replica_groups=mesh['group'=2,'gx'=16,'gy'=16] {'group'}, dimensions={0}, use_global_device_ids=true | all-gather | bytes 466944 | tf_op jit(solution)/shard_map/all_gather | solution.py:529
  72.3 0.0 copy-done.2
  72.3 0.0 copy-done.4
  72.3 3.2 %second_cycle.1 = (f32[16,8,128]{2,1,0:T(8,128)}, f32[16,8,128]{2,1,0:T(8,128)}) custom-call(s32[2,3]{1,0:T(2,128)S(1)} %copy-done.6, f32[16,8,128]{2,1,0:T(8,128)S(1)} %copy-done.2, f32[16,8,128]{2,1,0:T(8,128)S(1)} %copy-done.4, f32[16,2,8,128]{3,2,1,0:T(8,128)S(1)} %get-tuple-element.19.h0, f32[2,2,11,8,128]{4,3,2,1,0:T(8,128)S(1)} %bitcast.14, ...), custom_call_target="tpu_custom_call" | custom-call | tf_op jit(solution)/shard_map/second_cycle/pallas_call | solution.py:504
  (5 shorter events, 0.1 us)
Async XLA Ops:
  0.6 0.8 %copy-start.1 = (f32[16,8,128]{2,1,0:T(8,128)S(1)}, f32[16,8,128]{2,1,0:T(8,128)}, u32[]{:S(2)}) copy-start(f32[16,8,128]{2,1,0:T(8,128)} %m.1) | copy-start | bytes 196612
  1.5 0.8 %copy-start.3 = (f32[16,8,128]{2,1,0:T(8,128)S(1)}, f32[16,8,128]{2,1,0:T(8,128)}, u32[]{:S(2)}) copy-start(f32[16,8,128]{2,1,0:T(8,128)} %f.1) | copy-start | bytes 196612
  25.0 13.8 %collective-permute-start = (f32[60,8,128]{2,1,0:T(8,128)S(1)}, f32[60,8,128]{2,1,0:T(8,128)S(1)}, u32[]{:S(2)}, u32[]{:S(2)}) collective-permute-start(f32[60,8,128]{2,1,0:T(8,128)S(1)} %get-tuple-element.17.yp), channel_id=1, source_target_pairs={{0,257},{257,0},{1,258},{258,1},{2,259},{259,2},{3,260},{260,3},{4... | collective-permute-start | bytes 737288 | tf_op jit(solution)/shard_map/ppermute | solution.py:539
  29.6 9.2 %collective-permute-start.1 = (f32[3,8,128]{2,1,0:T(8,128)S(1)}, f32[3,8,128]{2,1,0:T(8,128)S(1)}, u32[]{:S(2)}, u32[]{:S(2)}) collective-permute-start(f32[3,8,128]{2,1,0:T(8,128)S(1)} %get-tuple-element.18), channel_id=1, source_target_pairs={{0,258},{258,0},{1,259},{259,1},{2,260},{260,2},{3,261},{261,3},{4... | collective-permute-start | bytes 36872 | tf_op jit(solution)/shard_map/ppermute | solution.py:539
  38.9 2.3 %copy-start = (bf16[256,256]{1,0:T(8,128)(2,1)S(1)}, bf16[256,256]{1,0:T(8,128)(2,1)}, u32[]{:S(2)}) copy-start(bf16[256,256]{1,0:T(8,128)(2,1)} %constant.5.clone.copies) | copy-start | bytes 393220
  38.9 2.3 %copy-start.5 = (bf16[256,256]{1,0:T(8,128)(2,1)S(1)}, bf16[256,256]{1,0:T(8,128)(2,1)}, u32[]{:S(2)}) copy-start(bf16[256,256]{1,0:T(8,128)(2,1)} %constant.4.clone.sums) | copy-start | bytes 393220
  41.2 0.7 copy-start.6
  55.7 14.4 %collective-permute-start.2 = (f32[35,8,128]{2,1,0:T(8,128)S(1)}, f32[35,8,128]{2,1,0:T(8,128)S(1)}, u32[]{:S(2)}, u32[]{:S(2)}) collective-permute-start(f32[35,8,128]{2,1,0:T(8,128)S(1)} %get-tuple-element.22.yp), channel_id=1, source_target_pairs={{0,257},{257,0},{1,258},{258,1},{2,259},{259,2},{3,260},{260,3},{4... | collective-permute-start | bytes 430088 | tf_op jit(solution)/shard_map/ppermute | solution.py:539
  60.9 9.2 %collective-permute-start.3 = (f32[3,8,128]{2,1,0:T(8,128)S(1)}, f32[3,8,128]{2,1,0:T(8,128)S(1)}, u32[]{:S(2)}, u32[]{:S(2)}) collective-permute-start(f32[3,8,128]{2,1,0:T(8,128)S(1)} %get-tuple-element.23), channel_id=1, source_target_pairs={{0,258},{258,0},{1,259},{259,1},{2,260},{260,2},{3,261},{261,3},{4... | collective-permute-start | bytes 36872 | tf_op jit(solution)/shard_map/ppermute | solution.py:539
  70.1 2.2 %copy-start.2 = (f32[16,8,128]{2,1,0:T(8,128)S(1)}, f32[16,8,128]{2,1,0:T(8,128)}, u32[]{:S(2)}) copy-start(f32[16,8,128]{2,1,0:T(8,128)} %m.1) | copy-start | bytes 196612
  70.1 2.2 %copy-start.4 = (f32[16,8,128]{2,1,0:T(8,128)S(1)}, f32[16,8,128]{2,1,0:T(8,128)}, u32[]{:S(2)}) copy-start(f32[16,8,128]{2,1,0:T(8,128)} %f.1) | copy-start | bytes 196612

commit v4 on v3

--- a/solution.py
+++ b/solution.py
@@ -172,10 +172,10 @@
 def column_fine(own, planes, xr, at, lo, hi):
     def load(p, z):
         if p < planes:
-            return xr[1, 0, at + 2 * p + z] * lo
+            return xr[1, at + 2 * p + z] * lo
         if p < 16 + planes:
             return own(p - planes, z)
-        return xr[0, 1, at + 2 * (p - 16 - planes) + z] * hi
+        return xr[0, at + 2 * (p - 16 - planes) + z] * hi
 
     return load
 
@@ -191,11 +191,11 @@
     mine = (sub_index() < 4) == (core() == 1)
     pack_fine(column_fine(own, 4, xr, x_at["h0"], lo, hi), 24, mine, yp, at["h0"])
     for k in range(2):
-        yp[at["h1"] + k] = xr[1, 0, x_at["h1"] + k] * lo
-        yp[at["h1"] + 6 + k] = xr[0, 1, x_at["h1"] + k] * hi
+        yp[at["h1"] + k] = xr[1, x_at["h1"] + k] * lo
+        yp[at["h1"] + 6 + k] = xr[0, x_at["h1"] + k] * hi
     for k in range(4):
         yp[at["h1"] + 2 + k] = h1(k)
-    two = [xr[1, 0, x_at["h2"]] * lo, h2(), xr[0, 1, x_at["h2"]] * hi]
+    two = [xr[1, x_at["h2"]] * lo, h2(), xr[0, x_at["h2"]] * hi]
     for k in range(3):
         yp[at["h2"] + k] = two[k]
         y2p[k] = two[k]
@@ -213,7 +213,7 @@
     mine = (sub < 4) == (core() == 1)
     weights = column_fine(lambda x, z: own[z, OWN["w"] + x], 1, xr, X_FIRST["w"], 1.0, 1.0)
     pack_fine(weights, 18, mine, yp, at["w"])
-    low, high = xr[1, 0, X_FIRST["w12"]], xr[0, 1, X_FIRST["w12"]]
+    low, high = xr[1, X_FIRST["w12"]], xr[0, X_FIRST["w12"]]
     for k in range(4):
         yp[at["w1"] + k] = coarse[COARSE["w1"] + k]
     yp[at["w1"] + 4] = jnp.where(sub < 4, low, turn(high, 4))
@@ -267,7 +267,7 @@
         for i in range(2):
             p = 9 * i if k == 4 else 1 + 2 * k + i
             first, second = four_rows(own, above, below, i)
-            out[p, 0], out[p, 1] = 1.0 / first, inverse(second)
+            out[p, 0], out[p, 1] = inverse(first), inverse(second)
 
 
 def join_h2(yp, yr, at, out):
@@ -276,7 +276,7 @@
     for k in range(3):
         tile, far = at["h2"] + k, at["far"] + k
         own, above, below = yp[tile], yr[0, tile] * yhi, yr[1, tile] * ylo
-        above2, below2 = yr[0, far] * yhi2, yr[1, far] * ylo2
+        above2, below2 = yr[0, far + 3] * yhi2, yr[1, far] * ylo2
         for i in range(4):
             first = jnp.where(sub < 2, turn(own, -2 * i), turn(above, 2 - 2 * i))
             upper = keep(sub < 6, turn(above2, 4 - 2 * i))
@@ -509,7 +509,7 @@
         scratch_shapes=scratch,
         compiler_params=pltpu.CompilerParams(vmem_limit_bytes=32 * 2**20),
         name=name,
-    )(*operands)
+    )(*(pltpu.with_memory_space_constraint(x, pltpu.HBM) for x in operands[:outside]), *operands[outside:])
 
 
 def space(*dims):
@@ -522,26 +522,27 @@
 
 def pairs(axis, distance):
     size = lax.axis_size(axis)
-    return [[i, size + (i + distance) % size] for i in range(size)]
+    return [[i, size + i + distance] for i in range(size - distance)]
 
 
 def share(value):
     return lax.all_gather(value, "group", axis=0)
 
 
+def swap(packed, axis):
+    moves = [move for a, b in pairs(axis, 1) for move in ((a, b), (b, a))]
+    return lax.ppermute(packed, ("group", axis), moves)
+
+
 def trade_x(packed):
-    both = lax.all_gather(packed, ("group", "gx"), axis=0, axis_index_groups=pairs("gx", 1))
-    return share(both)
-
-
-def swap(packed, distance):
-    moves = [move for a, b in pairs("gy", distance) for move in ((a, b), (b, a))]
-    return lax.ppermute(packed, ("group", "gy"), moves)
+    return share(swap(packed, "gx"))
 
 
 def trade_y(packed, packed_far):
-    far = swap(packed_far, 2)
-    near = swap(packed, 1)
+    near = swap(packed, "gy")
+    size = lax.axis_size("gy")
+    groups = [*pairs("gy", 2), [size - 2, size - 1], [size, size + 1]]
+    far = lax.all_gather(packed_far, ("group", "gy"), axis=0, tiled=True, axis_index_groups=groups)
     return share(jnp.concatenate([near, far], axis=0))
 
 

time: 75.9 us -> 65.7 us (0.87)
  the two profiles are of different devices: /device:TPU:1 before, /device:TPU:241 now
where the time goes in v4:
time: 65.7 us; the launch traced here: 65.4 us
  blocking collectives  27 us (41%)
  starting transfers between devices  15.5 us (24%)
  waiting for transfers between devices  13.6 us (21%)
  Pallas kernels  8.49 us (13%)
  between operations  0.73 us (1%)
    ppermute x4, starting transfers between devices, swap(): return lax.ppermute(packed, ('group', axis), moves)  15.5 us
    all_gather x5, blocking collectives, share(): return lax.all_gather(value, 'group', axis=0)  14.5 us
    ppermute x4, waiting for transfers between devices, swap(): return lax.ppermute(packed, ('group', axis), moves)  13.6 us
    all_gather x2, blocking collectives, trade_y(): lax.all_gather(packed_far, ('group', 'gy'), axis=0, tiled=True, axis_inde...  12.5 us
    pallas_call x6, Pallas kernels, call(): pl.pallas_call(kernel, out_shape=[jax.ShapeDtypeStruct(shape, F32) for sh...  8.49 us
  transfers between devices with their start and end apart: 4, of which 2 were waited for; matrix products, arithmetic and copies ran while one was open for 0% of the time, Pallas kernels for 0%

profile of v4, /device:TPU:241, one launch (start us, length us, event | category | flops | bytes accessed | tf_op | source)
XLA Modules:
  0.0 65.4 jit_solution(7321066173958219546)
XLA Ops:
  0.6 1.2 %block_sums.1 = f32[42,8,128]{2,1,0:T(8,128)S(1)} custom-call(f32[16,8,128]{2,1,0:T(8,128)} %m.1, f32[16,8,128]{2,1,0:T(8,128)} %f.1), custom_call_target="tpu_custom_call" | custom-call | tf_op jit(solution)/shard_map/block_sums/pallas_call | solution.py:504
  1.8 2.4 %all-gather = f32[84,8,128]{2,1,0:T(8,128)S(1)} all-gather(f32[42,8,128]{2,1,0:T(8,128)S(1)} %block_sums.1), channel_id=2, replica_groups=mesh['group'=2,'gx'=16,'gy'=16] {'group'}, dimensions={0}, use_global_device_ids=true | all-gather | bytes 516096 | tf_op jit(solution)/shard_map/all_gather | solution.py:529
  4.2 3.8 %collective-permute-start = (f32[14,8,128]{2,1,0:T(8,128)S(1)}, f32[14,8,128]{2,1,0:T(8,128)S(1)}, u32[]{:S(2)}, u32[]{:S(2)}) collective-permute-start(f32[14,8,128]{2,1,0:T(8,128)S(1)} %get-tuple-element.16), channel_id=1, source_target_pairs={{0,272},{272,0},{16,288},{288,16},{32,304},{304,32},{48,320},{320,... | collective-permute-start | bytes 172040 | tf_op jit(solution)/shard_map/ppermute | solution.py:534
  8.0 6.2 %collective-permute-done = f32[14,8,128]{2,1,0:T(8,128)S(1)} collective-permute-done((f32[14,8,128]{2,1,0:T(8,128)S(1)}, f32[14,8,128]{2,1,0:T(8,128)S(1)}, u32[]{:S(2)}, u32[]{:S(2)}) %collective-permute-start) | collective-permute-done | bytes 57376 | tf_op jit(solution)/shard_map/ppermute | solution.py:534
  14.2 3.4 %all-gather.1 = f32[28,8,128]{2,1,0:T(8,128)S(1)} all-gather(f32[14,8,128]{2,1,0:T(8,128)S(1)} %collective-permute-done), channel_id=3, replica_groups=mesh['group'=2,'gx'=16,'gy'=16] {'group'}, dimensions={0}, use_global_device_ids=true | all-gather | bytes 172032 | tf_op jit(solution)/shard_map/all_gather | solution.py:529
  17.6 6.0 %collective-permute-start.1 = (f32[60,8,128]{2,1,0:T(8,128)S(1)}, f32[60,8,128]{2,1,0:T(8,128)S(1)}, u32[]{:S(2)}, u32[]{:S(2)}) collective-permute-start(f32[60,8,128]{2,1,0:T(8,128)S(1)} %get-tuple-element.17.yp), channel_id=1, source_target_pairs={{0,257},{257,0},{1,258},{258,1},{2,259},{259,2},{3,260},{260,3},{4... | collective-permute-start | bytes 737288 | tf_op jit(solution)/shard_map/ppermute | solution.py:534
  23.6 6.2 %all_gather.40 = f32[6,8,128]{2,1,0:T(8,128)S(1)} all-gather(f32[3,8,128]{2,1,0:T(8,128)S(1)} %get-tuple-element.18), channel_id=1, replica_groups={{0,258},{1,259},{2,260},{3,261},{4,262},{5,263},{6,264},{7,265},{8,266}..., dimensions={0}, use_global_device_ids=true | all-gather | bytes 36864 | tf_op jit(solution)/shard_map/all_gather | solution.py:545
  29.9 0.0 collective-permute-done.1
  29.9 0.0 copy-start
  29.9 0.0 copy-start.3
  29.9 2.3 %all-gather.2 = f32[132,8,128]{2,1,0:T(8,128)S(1)} all-gather(f32[66,8,128]{2,1,0:T(8,128)S(1)} %pad_maximum_fusion), channel_id=4, replica_groups=mesh['group'=2,'gx'=16,'gy'=16] {'group'}, dimensions={0}, use_global_device_ids=true | all-gather | bytes 811008 | tf_op jit(solution)/shard_map/all_gather | solution.py:529
  32.2 0.0 copy-done
  32.2 0.0 copy-done.3
  32.3 3.6 %first_cycle.1 = (f32[11,8,128]{2,1,0:T(8,128)S(1)}, f32[18,4,8,128]{3,2,1,0:T(8,128)S(1)}, f32[18,4,8,128]{3,2,1,0:T(8,128)S(1)}, f32[10,2,8,128]{3,2,1,0:T(8,1...) custom-call(s32[2,3]{1,0:T(2,128)} %sweeps.3, ...), custom_call_target="tpu_custom_call" | custom-call | tf_op jit(solution)/shard_map/first_cycle/pallas_call | solution.py:504
  35.9 1.9 %collective-permute-start.2 = (f32[11,8,128]{2,1,0:T(8,128)S(1)}, f32[11,8,128]{2,1,0:T(8,128)S(1)}, u32[]{:S(2)}, u32[]{:S(2)}) collective-permute-start(f32[11,8,128]{2,1,0:T(8,128)S(1)} %get-tuple-element.20), channel_id=1, source_target_pairs={{0,272},{272,0},{16,288},{288,16},{32,304},{304,32},{48,320},{320,... | collective-permute-start | bytes 135176 | tf_op jit(solution)/shard_map/ppermute | solution.py:534
  37.8 7.3 %collective-permute-done.2 = f32[11,8,128]{2,1,0:T(8,128)S(1)} collective-permute-done((f32[11,8,128]{2,1,0:T(8,128)S(1)}, f32[11,8,128]{2,1,0:T(8,128)S(1)}, u32[]{:S(2)}, u32[]{:S(2)}) %collective-permute-start.2) | collective-permute-done | bytes 45088 | tf_op jit(solution)/shard_map/ppermute | solution.py:534
  45.2 4.3 %all-gather.3 = f32[22,8,128]{2,1,0:T(8,128)S(1)} all-gather(f32[11,8,128]{2,1,0:T(8,128)S(1)} %collective-permute-done.2), channel_id=5, replica_groups=mesh['group'=2,'gx'=16,'gy'=16] {'group'}, dimensions={0}, use_global_device_ids=true | all-gather | bytes 135168 | tf_op jit(solution)/shard_map/all_gather | solution.py:529
  49.5 3.8 %collective-permute-start.3 = (f32[35,8,128]{2,1,0:T(8,128)S(1)}, f32[35,8,128]{2,1,0:T(8,128)S(1)}, u32[]{:S(2)}, u32[]{:S(2)}) collective-permute-start(f32[35,8,128]{2,1,0:T(8,128)S(1)} %get-tuple-element.22.yp), channel_id=1, source_target_pairs={{0,257},{257,0},{1,258},{258,1},{2,259},{259,2},{3,260},{260,3},{4... | collective-permute-start | bytes 430088 | tf_op jit(solution)/shard_map/ppermute | solution.py:534
  53.3 6.2 %all_gather.45 = f32[6,8,128]{2,1,0:T(8,128)S(1)} all-gather(f32[3,8,128]{2,1,0:T(8,128)S(1)} %get-tuple-element.23), channel_id=1, replica_groups={{0,258},{1,259},{2,260},{3,261},{4,262},{5,263},{6,264},{7,265},{8,266}..., dimensions={0}, use_global_device_ids=true | all-gather | bytes 36864 | tf_op jit(solution)/shard_map/all_gather | solution.py:545
  59.5 0.0 collective-permute-done.3
  59.5 0.0 copy-start.1
  59.5 0.0 copy-start.2
  59.6 2.2 %all-gather.4 = f32[82,8,128]{2,1,0:T(8,128)S(1)} all-gather(f32[41,8,128]{2,1,0:T(8,128)S(1)} %pad_maximum_fusion.1), channel_id=6, replica_groups=mesh['group'=2,'gx'=16,'gy'=16] {'group'}, dimensions={0}, use_global_device_ids=true | all-gather | bytes 503808 | tf_op jit(solution)/shard_map/all_gather | solution.py:529
  61.7 0.0 copy-done.1
  61.7 0.0 copy-done.2
  61.7 3.6 %second_cycle.1 = (f32[16,8,128]{2,1,0:T(8,128)}, f32[16,8,128]{2,1,0:T(8,128)}) custom-call(s32[2,3]{1,0:T(2,128)} %sweeps.3, f32[16,8,128]{2,1,0:T(8,128)S(1)} %copy-done.1, f32[16,8,128]{2,1,0:T(8,128)S(1)} %copy-done.2, f32[16,2,8,128]{3,2,1,0:T(8,128)S(1)} %get-tuple-element.19.h0, f32[2,11,8,128]{3,2,1,0:T(8,128)S(1)} %bitcast.13, ...), custom_call_target="tpu_custom_call" | custom-call | tf_op jit(solution)/shard_map/second_cycle/pallas_call | solution.py:504
  (5 shorter events, 0.1 us)
Async XLA Ops:
  4.2 10.0 %collective-permute-start = (f32[14,8,128]{2,1,0:T(8,128)S(1)}, f32[14,8,128]{2,1,0:T(8,128)S(1)}, u32[]{:S(2)}, u32[]{:S(2)}) collective-permute-start(f32[14,8,128]{2,1,0:T(8,128)S(1)} %get-tuple-element.16), channel_id=1, source_target_pairs={{0,272},{272,0},{16,288},{288,16},{32,304},{304,32},{48,320},{320,... | collective-permute-start | bytes 172040 | tf_op jit(solution)/shard_map/ppermute | solution.py:534
  17.6 12.3 %collective-permute-start.1 = (f32[60,8,128]{2,1,0:T(8,128)S(1)}, f32[60,8,128]{2,1,0:T(8,128)S(1)}, u32[]{:S(2)}, u32[]{:S(2)}) collective-permute-start(f32[60,8,128]{2,1,0:T(8,128)S(1)} %get-tuple-element.17.yp), channel_id=1, source_target_pairs={{0,257},{257,0},{1,258},{258,1},{2,259},{259,2},{3,260},{260,3},{4... | collective-permute-start | bytes 737288 | tf_op jit(solution)/shard_map/ppermute | solution.py:534
  29.9 2.4 %copy-start = (bf16[256,256]{1,0:T(8,128)(2,1)S(1)}, bf16[256,256]{1,0:T(8,128)(2,1)}, u32[]{:S(2)}) copy-start(bf16[256,256]{1,0:T(8,128)(2,1)} %constant.5.clone.copies) | copy-start | bytes 393220
  29.9 2.3 %copy-start.3 = (bf16[256,256]{1,0:T(8,128)(2,1)S(1)}, bf16[256,256]{1,0:T(8,128)(2,1)}, u32[]{:S(2)}) copy-start(bf16[256,256]{1,0:T(8,128)(2,1)} %constant.4.clone.sums) | copy-start | bytes 393220
  35.9 9.3 %collective-permute-start.2 = (f32[11,8,128]{2,1,0:T(8,128)S(1)}, f32[11,8,128]{2,1,0:T(8,128)S(1)}, u32[]{:S(2)}, u32[]{:S(2)}) collective-permute-start(f32[11,8,128]{2,1,0:T(8,128)S(1)} %get-tuple-element.20), channel_id=1, source_target_pairs={{0,272},{272,0},{16,288},{288,16},{32,304},{304,32},{48,320},{320,... | collective-permute-start | bytes 135176 | tf_op jit(solution)/shard_map/ppermute | solution.py:534
  49.5 10.0 %collective-permute-start.3 = (f32[35,8,128]{2,1,0:T(8,128)S(1)}, f32[35,8,128]{2,1,0:T(8,128)S(1)}, u32[]{:S(2)}, u32[]{:S(2)}) collective-permute-start(f32[35,8,128]{2,1,0:T(8,128)S(1)} %get-tuple-element.22.yp), channel_id=1, source_target_pairs={{0,257},{257,0},{1,258},{258,1},{2,259},{259,2},{3,260},{260,3},{4... | collective-permute-start | bytes 430088 | tf_op jit(solution)/shard_map/ppermute | solution.py:534
  59.5 2.2 %copy-start.1 = (f32[16,8,128]{2,1,0:T(8,128)S(1)}, f32[16,8,128]{2,1,0:T(8,128)}, u32[]{:S(2)}) copy-start(f32[16,8,128]{2,1,0:T(8,128)} %m.1) | copy-start | bytes 196612
  59.5 2.2 %copy-start.2 = (f32[16,8,128]{2,1,0:T(8,128)S(1)}, f32[16,8,128]{2,1,0:T(8,128)}, u32[]{:S(2)}) copy-start(f32[16,8,128]{2,1,0:T(8,128)} %f.1) | copy-start | bytes 196612

commit v5 on v4

--- a/solution.py
+++ b/solution.py
@@ -18,7 +18,7 @@
 F32 = jnp.float32
 TILE = (8, 128)
 
-OWN = dict(h0=0, w=16, h1=32, w1=36, h2=40, w2=41, size=42)
+OWN = dict(h0=0, w=16, h1=32, w1=36, h2=40, w2=41, counts=42, size=43)
 COARSE = dict(h1=0, w1=4, h2=8, w2=9, size=10)
 X_FIRST = dict(h0=0, h1=8, h2=10, w=11, w12=13, size=14)
 X_SECOND = dict(h0=0, h1=8, h2=10, size=11)
@@ -110,10 +110,11 @@
     return jnp.where(matrix, 1.0, 0.0).astype(jnp.bfloat16)
 
 
-def first_kernel(m_whole, f_whole, out, m, f, arrived):
+def first_kernel(m_whole, f_whole, sweeps_whole, out, m, f, sweeps, arrived):
+    moves = ((m_whole, m), (f_whole, f), (sweeps_whole, sweeps))
     copies = [
         pltpu.make_async_copy(source, target, arrived.at[k])
-        for k, (source, target) in enumerate(((m_whole, m), (f_whole, f)))
+        for k, (source, target) in enumerate(moves)
     ]
     for copy in copies:
         copy.start()
@@ -126,6 +127,8 @@
         out[OWN["w"] + x] = m_tiles[x]
     rows = jnp.concatenate(plane_sums(m_tiles) + plane_sums(f_tiles), axis=0)
     total = exact_dot(rows, sums)
+    out[OWN["counts"]] = jnp.zeros(TILE, F32)
+    out[OWN["counts"], : sweeps.shape[0], : sweeps.shape[1]] = sweeps[...].astype(F32)
     upper = core() == 1
     for k in range(5):
         left, width = (0, 64) if k < 4 else (128, 32)
@@ -153,7 +156,7 @@
 
 
 def first_sides_kernel(own, xp, coarse):
-    total = [own[0, k] + own[1, k] for k in range(OWN["h1"], OWN["size"])]
+    total = [own[0, k] + own[1, k] for k in range(OWN["h1"], OWN["counts"])]
     for k in range(COARSE["size"]):
         coarse[k] = total[k]
     h1, w1 = total[:4], total[4:8]
@@ -230,7 +233,7 @@
     )
 
 
-def join_fine(load, planes, yr, at, ylo, yhi, out):
+def join_fine(load, planes, yr, at, ylo, yhi, *outs):
     sub = sub_index()
     for k in range(planes // 2):
         for z in range(2):
@@ -240,8 +243,10 @@
                 turn(jnp.where(sub < 4, below, above), 4),
             )
             for i in range(2):
-                out[2 * k + i, z] = load(2 * k + i, z)
-                out[2 * k + i, 2 + z] = halos[i]
+                own = load(2 * k + i, z)
+                for out in outs:
+                    out[2 * k + i, z] = own
+                    out[2 * k + i, 2 + z] = halos[i]
 
 
 def four_rows(own, above, below, i):
@@ -251,13 +256,15 @@
     return first, keep(sub >= 4, turn(below, turned))
 
 
-def join_h1(yp, yr, at, out):
+def join_h1(yp, yr, at, *outs):
     ylo, yhi = flags()[2:4]
     for k in range(8):
         tile = at + k
         own, above, below = yp[tile], yr[0, tile] * yhi, yr[1, tile] * ylo
         for i in range(2):
-            out[2 * k + i, 0], out[2 * k + i, 1] = four_rows(own, above, below, i)
+            both = four_rows(own, above, below, i)
+            for out in outs:
+                out[2 * k + i, 0], out[2 * k + i, 1] = both
 
 
 def join_w1(yp, yr, out):
@@ -270,7 +277,7 @@
             out[p, 0], out[p, 1] = inverse(first), inverse(second)
 
 
-def join_h2(yp, yr, at, out):
+def join_h2(yp, yr, at, *outs):
     ylo, yhi, ylo2, yhi2 = flags()[2:]
     sub = sub_index()
     for k in range(3):
@@ -280,9 +287,10 @@
         for i in range(4):
             first = jnp.where(sub < 2, turn(own, -2 * i), turn(above, 2 - 2 * i))
             upper = keep(sub < 6, turn(above2, 4 - 2 * i))
-            out[4 * k + i, 0] = jnp.where(sub < 4, first, upper)
             lower = jnp.where(sub < 6, turn(below2, 4 - 2 * i), turn(below, 6 - 2 * i))
-            out[4 * k + i, 1] = keep(sub >= 4, lower)
+            for out in outs:
+                out[4 * k + i, 0] = jnp.where(sub < 4, first, upper)
+                out[4 * k + i, 1] = keep(sub >= 4, lower)
 
 
 def join_w2(yp, yr, out):
@@ -299,31 +307,25 @@
 def along_y(first, second):
     sub = sub_index()
     up_first, up_second = turn(first, 7), turn(second, 7)
-    first = first + jnp.where(sub == 7, up_second, up_first)
-    second = second + jnp.where(sub == 7, up_first, up_second)
     down_first, down_second = turn(first, 1), turn(second, 1)
-    return (
-        first + jnp.where(sub == 0, down_second, down_first),
-        second + jnp.where(sub == 0, down_first, down_second),
-    )
+    sides_first = jnp.where(sub == 7, up_second, up_first) + jnp.where(sub == 0, down_second, down_first)
+    sides_second = jnp.where(sub == 7, up_first, up_second) + jnp.where(sub == 0, down_first, down_second)
+    return (first + first) + sides_first, (second + second) + sides_second
 
 
 def along_z_fine(left, right):
     lane = lane_index()
     up_left, up_right = pltpu.roll(left, 127, 1), pltpu.roll(right, 127, 1)
-    sum_left = left + jnp.where(lane < 127, up_left, up_right)
-    sum_right = right + keep(lane < 127, up_right)
-    down_left, down_right = pltpu.roll(sum_left, 1, 1), pltpu.roll(sum_right, 1, 1)
-    return (
-        sum_left + jnp.where(lane > 0, down_left, left),
-        sum_right + jnp.where(lane > 0, down_right, down_left),
-    )
+    down_left, down_right = pltpu.roll(left, 1, 1), pltpu.roll(right, 1, 1)
+    sides_left = jnp.where(lane < 127, up_left, up_right) + keep(lane > 0, down_left)
+    sides_right = keep(lane < 127, up_right) + jnp.where(lane > 0, down_right, down_left)
+    return (left + left) + sides_left, (right + right) + sides_right
 
 
 def along_z_coarse(tile):
     lane = lane_index()
-    summed = tile + keep(lane < 127, pltpu.roll(tile, 127, 1))
-    return summed + jnp.where(lane > 0, pltpu.roll(summed, 1, 1), tile)
+    sides = keep(lane < 127, pltpu.roll(tile, 127, 1)) + keep(lane > 0, pltpu.roll(tile, 1, 1))
+    return (tile + tile) + sides
 
 
 def along_yz(tiles):
@@ -341,38 +343,28 @@
     return [a + b for a, b in zip(first, second)]
 
 
-def relax(q, h, planes, parts, count, masks, lo, hi):
-    sides = [[mask * factor for mask in masks] for factor in (lo, 1.0, hi)]
-
-    def sweep(k, source):
-        def load(x):
-            return [source[x, part] for part in range(parts)]
-
-        here = load(k)
-        below = added(load(k - 1), here)
-        for x in range(k, planes - k):
-            after = load(x + 1)
-            above = added(here, after)
-            summed = along_yz(added(below, above))
-            side = sides[0 if x < 4 else 2 if x >= planes - 4 else 1]
-            for part in range(parts):
-                spread = side[part // (parts // 2)] * summed[part]
-                q[x, part] = (KEEP * here[part] + spread) + h[x, part]
-            here, below = after, above
-
-    @pl.when(count == 1)
-    def _():
-        q[...] = h[...]
-
-    for k in range(1, 4):
-
-        @pl.when(count > k)
-        def _():
-            sweep(k, h if k == 1 else q)
-
-
-def relax_levels(counts, cycle, h0, q0, h1, q1, h2, q2):
-    lo, hi, ylo, yhi, ylo2, yhi2 = [flag * 1.0 for flag in flags()]
+def relax_planes(q, h, start, planes, parts, before, masks, factors, active):
+    def load(x):
+        return [q[x, part] for part in range(parts)]
+
+    kept = KEEP if active is None else 1.0 + active * (KEEP - 1.0)
+    here = load(start)
+    below = added(before, here)
+    for i in range(planes):
+        x = start + i
+        after = load(x + 1)
+        above = added(here, after)
+        summed = along_yz(added(below, above))
+        for part in range(parts):
+            spread = (masks[part // (parts // 2)] * factors[i]) * summed[part]
+            source = h[x, part] if active is None else active * h[x, part]
+            q[x, part] = (kept * here[part] + spread) + source
+        last, here, below = here, after, above
+    return last
+
+
+def relax_levels(counts, h0, q0, h1, q1, h2, q2):
+    lo, hi, ylo, yhi, ylo2, yhi2 = flags()
     sub, lane = sub_index(), lane_index()
     spread = jnp.full(TILE, SPREAD, F32)
     above = jnp.where(sub < 2, 1.0, jnp.where(sub < 4, yhi, jnp.where(sub < 6, yhi2, 0.0)))
@@ -380,9 +372,35 @@
     masks2 = (keep(lane < 64, above * spread), keep(lane < 64, below * spread))
     masks1 = (jnp.where(sub < 4, 1.0, yhi) * spread, jnp.where(sub < 4, 0.0, ylo) * spread)
     masks0 = (spread, jnp.where(sub < 4, yhi, ylo) * spread)
-    relax(q2, h2, 12, 2, counts[cycle, 2], masks2, lo, hi)
-    relax(q1, h1, 16, 2, counts[cycle, 1], masks1, lo, hi)
-    relax(q0, h0, 24, 4, counts[cycle, 0], masks0, lo, hi)
+
+    def coarse_sweep(k, _):
+        for q, h, planes, masks, count in ((q2, h2, 12, masks2, counts[2]), (q1, h1, 16, masks1, counts[1])):
+            active = jnp.where(count > k, 1.0, 0.0)
+            factors = [active * lo] * 3 + [active] * (planes - 8) + [active * hi] * 3
+            before = [q[0, part] for part in range(2)]
+            relax_planes(q, h, 1, planes - 2, 2, before, masks, factors, active)
+        return 0
+
+    def fine_sweep(_, __):
+        def half(j, before):
+            start = 1 + 11 * j
+            factors = [
+                jnp.where(start + i < 4, lo, jnp.where(start + i >= 20, hi, 1.0)) for i in range(11)
+            ]
+            return tuple(relax_planes(q0, h0, start, 11, 4, list(before), masks0, factors, None))
+
+        lax.fori_loop(0, 2, half, tuple(q0[0, part] for part in range(4)))
+        return 0
+
+    lax.fori_loop(1, jnp.maximum(counts[1], counts[2]), coarse_sweep, 0)
+    lax.fori_loop(1, counts[0], fine_sweep, 0)
+
+
+def sweep_counts(own, cycle):
+    held, sub, lane = own[0, OWN["counts"]], sub_index(), lane_index()
+    return [
+        jnp.max(keep((sub == cycle) & (lane == level), held)).astype(jnp.int32) for level in range(3)
+    ]
 
 
 def corrections(q1, iw1, q2, iw2, copies):
@@ -436,23 +454,21 @@
 
 
 def middle_kernel(
-    sweeps, own, coarse, xr, yp, yr, sums, copies,
+    own, coarse, xr, yp, yr, sums, copies,
     xp, pf, w, iw1, iw2, h0_next, h12_next,
-    h0_all, q0, h1_all, q1, h2_all, q2, counts, arrived,
+    h0_all, q0, h1_all, q1, h2_all, q2,
 ):
-    counting = pltpu.make_async_copy(sweeps, counts, arrived)
-    counting.start()
+    counts = sweep_counts(own, 0)
     lo, hi, ylo, yhi = flags()[:4]
     load = column_fine(lambda x, z: own[z, x], 4, xr, X_FIRST["h0"], lo, hi)
-    join_fine(load, 24, yr, Y_FIRST["h0"], ylo, yhi, h0_all)
+    join_fine(load, 24, yr, Y_FIRST["h0"], ylo, yhi, h0_all, q0)
     load = column_fine(lambda x, z: own[z, OWN["w"] + x], 1, xr, X_FIRST["w"], 1.0, 1.0)
     join_fine(load, 18, yr, Y_FIRST["w"], 1.0, 1.0, w)
-    join_h1(yp, yr, Y_FIRST["h1"], h1_all)
+    join_h1(yp, yr, Y_FIRST["h1"], h1_all, q1)
     join_w1(yp, yr, iw1)
-    join_h2(yp, yr, Y_FIRST, h2_all)
+    join_h2(yp, yr, Y_FIRST, h2_all, q2)
     join_w2(yp, yr, iw2)
-    counting.wait()
-    relax_levels(counts, 0, h0_all, q0, h1_all, q1, h2_all, q2)
+    relax_levels(counts, h0_all, q0, h1_all, q1, h2_all, q2)
     iterate(corrections(q1, iw1, q2, iw2, copies), q0, w, None, pf)
 
     rests = [[], []]
@@ -476,36 +492,45 @@
 
 
 def last_kernel(
-    sweeps, m, f, h0, xr, yp, yr, pf, w, iw1, iw2, copies,
+    own, m, f, h0, xr, yp, yr, pf, w, iw1, iw2, copies,
     solution_out, residual_out,
-    h0_all, q0, h1_all, q1, h2_all, q2, counts, arrived, pf_all,
+    h0_all, q0, h1_all, q1, h2_all, q2, pf_all, solved, left, sent,
 ):
-    counting = pltpu.make_async_copy(sweeps, counts, arrived)
-    counting.start()
+    counts = sweep_counts(own, 1)
     lo, hi, ylo, yhi = flags()[:4]
     load = column_fine(lambda x, z: h0[x, z], 4, xr, X_SECOND["h0"], lo, hi)
-    join_fine(load, 24, yr, Y_SECOND["h0"], ylo, yhi, h0_all)
-    join_h1(yp, yr, Y_SECOND["h1"], h1_all)
-    join_h2(yp, yr, Y_SECOND, h2_all)
-    counting.wait()
-    relax_levels(counts, 1, h0_all, q0, h1_all, q1, h2_all, q2)
+    join_fine(load, 24, yr, Y_SECOND["h0"], ylo, yhi, h0_all, q0)
+    join_h1(yp, yr, Y_SECOND["h1"], h1_all, q1)
+    join_h2(yp, yr, Y_SECOND, h2_all, q2)
+    relax_levels(counts, h0_all, q0, h1_all, q1, h2_all, q2)
     iterate(corrections(q1, iw1, q2, iw2, copies), q0, w, pf, pf_all)
     first = core() == 0
+    sending = []
     for x, (here, defect) in enumerate(defects(pf_all)):
         mine, rest = (jnp.where(first, both[0], both[1]) for both in (here, defect))
         weight = m[x]
-        solution_out[x] = mine / weight
-        residual_out[x] = f[x] - weight * rest
-
-
-def call(kernel, outs, scratch, name, *operands, outside=0):
+        solved[x] = mine / weight
+        left[x] = f[x] - weight * rest
+        if x % 4 == 3:
+            done = pl.ds(x - 3, 4)
+            for k, (source, target) in enumerate(((solved, solution_out), (left, residual_out))):
+                copy = pltpu.make_async_copy(
+                    source.at[done], target.at[done], sent.at[2 * (x // 4) + k]
+                )
+                copy.start()
+                sending.append(copy)
+    for copy in sending:
+        copy.wait()
+
+
+def call(kernel, outs, scratch, name, *operands, outside=0, outs_outside=False):
     whole = pl.BlockSpec(memory_space=pltpu.HBM)
     vmem = pl.BlockSpec(memory_space=pltpu.VMEM)
     return pl.pallas_call(
         kernel,
         out_shape=[jax.ShapeDtypeStruct(shape, F32) for shape in outs],
         in_specs=[whole] * outside + [vmem] * (len(operands) - outside),
-        out_specs=[vmem] * len(outs),
+        out_specs=[whole if outs_outside else vmem] * len(outs),
         scratch_shapes=scratch,
         compiler_params=pltpu.CompilerParams(vmem_limit_bytes=32 * 2**20),
         name=name,
@@ -549,15 +574,17 @@
 def on_device(forcing, metric, sweeps):
     sums, copies = (jnp.asarray(matrix, jnp.bfloat16) for matrix in (WHOLE_SUMS, COPIES))
     spaces = [space(24, 4)] * 2 + [space(16, 2)] * 2 + [space(12, 2)] * 2
-    spaces += [pltpu.SMEM(sweeps.shape, jnp.int32), pltpu.SemaphoreType.DMA]
 
     (own,) = call(
         first_kernel,
         [tiles(OWN["size"])],
-        [space(16), space(16), pltpu.SemaphoreType.DMA((2,))],
+        [
+            *(space(16), space(16), pltpu.VMEM(sweeps.shape, jnp.int32)),
+            pltpu.SemaphoreType.DMA((3,)),
+        ],
         "block_sums",
-        *(metric, forcing),
-        outside=2,
+        *(metric, forcing, sweeps),
+        outside=3,
     )
     own = share(own)
     xp, coarse = call(
@@ -584,8 +611,7 @@
         ],
         spaces,
         "first_cycle",
-        *(sweeps, own, coarse, xr, yp, yr, sums, copies),
-        outside=1,
+        *(own, coarse, xr, yp, yr, sums, copies),
     )
     xr = trade_x(xp)
     yp, y2p = call(
@@ -599,10 +625,10 @@
     return call(
         last_kernel,
         [tiles(16), tiles(16)],
-        [*spaces, space(18, 4)],
+        [*spaces, space(18, 4), space(16), space(16), pltpu.SemaphoreType.DMA((8,))],
         "second_cycle",
-        *(sweeps, metric, forcing, h0, xr, yp, yr, pf, w, iw1, iw2, copies),
-        outside=1,
+        *(own, metric, forcing, h0, xr, yp, yr, pf, w, iw1, iw2, copies),
+        outs_outside=True,
     )
 
 

time: 65.7 us -> 62.6 us (0.953)
  Pallas kernels: 8.49 us -> 5.4 us
    pallas_call x6, Pallas kernels: 8.49 us -> 5.4 us  [call(): pl.pallas_call(kernel, out_shape=[jax.ShapeDtypeStruct(shape, F32) for sh...]
where the time goes in v5:
time: 62.6 us; the launch traced here: 62.3 us
  blocking collectives  27 us (43%)
  starting transfers between devices  15.5 us (25%)
  waiting for transfers between devices  13.6 us (22%)
  Pallas kernels  5.4 us (9%)
  between operations  0.74 us (1%)
    ppermute x4, starting transfers between devices, swap(): return lax.ppermute(packed, ('group', axis), moves)  15.5 us
    all_gather x5, blocking collectives, share(): return lax.all_gather(value, 'group', axis=0)  14.5 us
    ppermute x4, waiting for transfers between devices, swap(): return lax.ppermute(packed, ('group', axis), moves)  13.6 us
    all_gather x2, blocking collectives, trade_y(): lax.all_gather(packed_far, ('group', 'gy'), axis=0, tiled=True, axis_inde...  12.5 us
    pallas_call x6, Pallas kernels, call(): pl.pallas_call(kernel, out_shape=[jax.ShapeDtypeStruct(shape, F32) for sh...  5.4 us
  transfers between devices with their start and end apart: 4, of which 2 were waited for; matrix products, arithmetic and copies ran while one was open for 0% of the time, Pallas kernels for 0%

profile of v5, /device:TPU:241, one launch (start us, length us, event | category | flops | bytes accessed | tf_op | source)
XLA Modules:
  0.0 62.3 jit_solution(5380351657235881039)
XLA Ops:
  0.6 1.2 %block_sums.1 = f32[43,8,128]{2,1,0:T(8,128)S(1)} custom-call(f32[16,8,128]{2,1,0:T(8,128)} %m.1, f32[16,8,128]{2,1,0:T(8,128)} %f.1, s32[2,3]{1,0:T(2,128)} %sweeps_whole.1), custom_call_target="tpu_custom_call" | custom-call | tf_op jit(solution)/shard_map/block_sums/pallas_call | solution.py:529
  1.8 2.4 %all-gather = f32[86,8,128]{2,1,0:T(8,128)S(1)} all-gather(f32[43,8,128]{2,1,0:T(8,128)S(1)} %block_sums.1), channel_id=2, replica_groups=mesh['group'=2,'gx'=16,'gy'=16] {'group'}, dimensions={0}, use_global_device_ids=true | all-gather | bytes 528384 | tf_op jit(solution)/shard_map/all_gather | solution.py:554
  4.2 3.8 %collective-permute-start = (f32[14,8,128]{2,1,0:T(8,128)S(1)}, f32[14,8,128]{2,1,0:T(8,128)S(1)}, u32[]{:S(2)}, u32[]{:S(2)}) collective-permute-start(f32[14,8,128]{2,1,0:T(8,128)S(1)} %get-tuple-element.16), channel_id=1, source_target_pairs={{0,272},{272,0},{16,288},{288,16},{32,304},{304,32},{48,320},{320,... | collective-permute-start | bytes 172040 | tf_op jit(solution)/shard_map/ppermute | solution.py:559
  8.0 6.2 %collective-permute-done = f32[14,8,128]{2,1,0:T(8,128)S(1)} collective-permute-done((f32[14,8,128]{2,1,0:T(8,128)S(1)}, f32[14,8,128]{2,1,0:T(8,128)S(1)}, u32[]{:S(2)}, u32[]{:S(2)}) %collective-permute-start) | collective-permute-done | bytes 57376 | tf_op jit(solution)/shard_map/ppermute | solution.py:559
  14.2 3.4 %all-gather.1 = f32[28,8,128]{2,1,0:T(8,128)S(1)} all-gather(f32[14,8,128]{2,1,0:T(8,128)S(1)} %collective-permute-done), channel_id=3, replica_groups=mesh['group'=2,'gx'=16,'gy'=16] {'group'}, dimensions={0}, use_global_device_ids=true | all-gather | bytes 172032 | tf_op jit(solution)/shard_map/all_gather | solution.py:554
  17.6 6.0 %collective-permute-start.1 = (f32[60,8,128]{2,1,0:T(8,128)S(1)}, f32[60,8,128]{2,1,0:T(8,128)S(1)}, u32[]{:S(2)}, u32[]{:S(2)}) collective-permute-start(f32[60,8,128]{2,1,0:T(8,128)S(1)} %get-tuple-element.17.yp), channel_id=1, source_target_pairs={{0,257},{257,0},{1,258},{258,1},{2,259},{259,2},{3,260},{260,3},{4... | collective-permute-start | bytes 737288 | tf_op jit(solution)/shard_map/ppermute | solution.py:559
  23.7 6.2 %all_gather.40 = f32[6,8,128]{2,1,0:T(8,128)S(1)} all-gather(f32[3,8,128]{2,1,0:T(8,128)S(1)} %get-tuple-element.18), channel_id=1, replica_groups={{0,258},{1,259},{2,260},{3,261},{4,262},{5,263},{6,264},{7,265},{8,266}..., dimensions={0}, use_global_device_ids=true | all-gather | bytes 36864 | tf_op jit(solution)/shard_map/all_gather | solution.py:570
  29.9 0.0 collective-permute-done.1
  29.9 0.0 copy-start
  29.9 0.0 copy-start.3
  29.9 2.3 %all-gather.2 = f32[132,8,128]{2,1,0:T(8,128)S(1)} all-gather(f32[66,8,128]{2,1,0:T(8,128)S(1)} %pad_maximum_fusion), channel_id=4, replica_groups=mesh['group'=2,'gx'=16,'gy'=16] {'group'}, dimensions={0}, use_global_device_ids=true | all-gather | bytes 811008 | tf_op jit(solution)/shard_map/all_gather | solution.py:554
  32.3 0.0 copy-done
  32.3 0.0 copy-done.3
  32.3 1.4 %first_cycle.1 = (f32[11,8,128]{2,1,0:T(8,128)S(1)}, f32[18,4,8,128]{3,2,1,0:T(8,128)S(1)}, f32[18,4,8,128]{3,2,1,0:T(8,128)S(1)}, f32[10,2,8,128]{3,2,1,0:T(8,1...) custom-call(f32[2,43,8,128]{3,2,1,0:T(8,128)S(1)} %bitcast.7, ...), custom_call_target="tpu_custom_call" | custom-call | tf_op jit(solution)/shard_map/first_cycle/pallas_call | solution.py:529
  33.7 1.9 %collective-permute-start.2 = (f32[11,8,128]{2,1,0:T(8,128)S(1)}, f32[11,8,128]{2,1,0:T(8,128)S(1)}, u32[]{:S(2)}, u32[]{:S(2)}) collective-permute-start(f32[11,8,128]{2,1,0:T(8,128)S(1)} %get-tuple-element.20), channel_id=1, source_target_pairs={{0,272},{272,0},{16,288},{288,16},{32,304},{304,32},{48,320},{320,... | collective-permute-start | bytes 135176 | tf_op jit(solution)/shard_map/ppermute | solution.py:559
  35.6 7.3 %collective-permute-done.2 = f32[11,8,128]{2,1,0:T(8,128)S(1)} collective-permute-done((f32[11,8,128]{2,1,0:T(8,128)S(1)}, f32[11,8,128]{2,1,0:T(8,128)S(1)}, u32[]{:S(2)}, u32[]{:S(2)}) %collective-permute-start.2) | collective-permute-done | bytes 45088 | tf_op jit(solution)/shard_map/ppermute | solution.py:559
  42.9 4.3 %all-gather.3 = f32[22,8,128]{2,1,0:T(8,128)S(1)} all-gather(f32[11,8,128]{2,1,0:T(8,128)S(1)} %collective-permute-done.2), channel_id=5, replica_groups=mesh['group'=2,'gx'=16,'gy'=16] {'group'}, dimensions={0}, use_global_device_ids=true | all-gather | bytes 135168 | tf_op jit(solution)/shard_map/all_gather | solution.py:554
  47.2 3.8 %collective-permute-start.3 = (f32[35,8,128]{2,1,0:T(8,128)S(1)}, f32[35,8,128]{2,1,0:T(8,128)S(1)}, u32[]{:S(2)}, u32[]{:S(2)}) collective-permute-start(f32[35,8,128]{2,1,0:T(8,128)S(1)} %get-tuple-element.22.yp), channel_id=1, source_target_pairs={{0,257},{257,0},{1,258},{258,1},{2,259},{259,2},{3,260},{260,3},{4... | collective-permute-start | bytes 430088 | tf_op jit(solution)/shard_map/ppermute | solution.py:559
  51.0 6.2 %all_gather.45 = f32[6,8,128]{2,1,0:T(8,128)S(1)} all-gather(f32[3,8,128]{2,1,0:T(8,128)S(1)} %get-tuple-element.23), channel_id=1, replica_groups={{0,258},{1,259},{2,260},{3,261},{4,262},{5,263},{6,264},{7,265},{8,266}..., dimensions={0}, use_global_device_ids=true | all-gather | bytes 36864 | tf_op jit(solution)/shard_map/all_gather | solution.py:570
  57.3 0.0 collective-permute-done.3
  57.3 0.0 copy-start.1
  57.3 0.0 copy-start.2
  57.3 2.2 %all-gather.4 = f32[82,8,128]{2,1,0:T(8,128)S(1)} all-gather(f32[41,8,128]{2,1,0:T(8,128)S(1)} %pad_maximum_fusion.1), channel_id=6, replica_groups=mesh['group'=2,'gx'=16,'gy'=16] {'group'}, dimensions={0}, use_global_device_ids=true | all-gather | bytes 503808 | tf_op jit(solution)/shard_map/all_gather | solution.py:554
  59.5 0.0 copy-done.1
  59.5 0.0 copy-done.2
  59.5 2.8 %second_cycle.1 = (f32[16,8,128]{2,1,0:T(8,128)}, f32[16,8,128]{2,1,0:T(8,128)}) custom-call(f32[2,43,8,128]{3,2,1,0:T(8,128)S(1)} %bitcast.8, f32[16,8,128]{2,1,0:T(8,128)S(1)} %copy-done.1, f32[16,8,128]{2,1,0:T(8,128)S(1)} %copy-done.2, f32[16,2,8,128]{3,2,1,0:T(8,128)S(1)} %get-tuple-element.19.h0, f32[2,11,8,128]{3,2,1,0:T(8,128)S(1)} %bitcast.14, ...), custom_call_target="tpu_custom_call" | custom-call | tf_op jit(solution)/shard_map/second_cycle/pallas_call | solution.py:529
  (5 shorter events, 0.1 us)
Async XLA Ops:
  4.2 10.0 %collective-permute-start = (f32[14,8,128]{2,1,0:T(8,128)S(1)}, f32[14,8,128]{2,1,0:T(8,128)S(1)}, u32[]{:S(2)}, u32[]{:S(2)}) collective-permute-start(f32[14,8,128]{2,1,0:T(8,128)S(1)} %get-tuple-element.16), channel_id=1, source_target_pairs={{0,272},{272,0},{16,288},{288,16},{32,304},{304,32},{48,320},{320,... | collective-permute-start | bytes 172040 | tf_op jit(solution)/shard_map/ppermute | solution.py:559
  17.6 12.3 %collective-permute-start.1 = (f32[60,8,128]{2,1,0:T(8,128)S(1)}, f32[60,8,128]{2,1,0:T(8,128)S(1)}, u32[]{:S(2)}, u32[]{:S(2)}) collective-permute-start(f32[60,8,128]{2,1,0:T(8,128)S(1)} %get-tuple-element.17.yp), channel_id=1, source_target_pairs={{0,257},{257,0},{1,258},{258,1},{2,259},{259,2},{3,260},{260,3},{4... | collective-permute-start | bytes 737288 | tf_op jit(solution)/shard_map/ppermute | solution.py:559
  29.9 2.4 %copy-start = (bf16[256,256]{1,0:T(8,128)(2,1)S(1)}, bf16[256,256]{1,0:T(8,128)(2,1)}, u32[]{:S(2)}) copy-start(bf16[256,256]{1,0:T(8,128)(2,1)} %constant.5.clone.copies) | copy-start | bytes 393220
  29.9 2.3 %copy-start.3 = (bf16[256,256]{1,0:T(8,128)(2,1)S(1)}, bf16[256,256]{1,0:T(8,128)(2,1)}, u32[]{:S(2)}) copy-start(bf16[256,256]{1,0:T(8,128)(2,1)} %constant.4.clone.sums) | copy-start | bytes 393220
  33.7 9.3 %collective-permute-start.2 = (f32[11,8,128]{2,1,0:T(8,128)S(1)}, f32[11,8,128]{2,1,0:T(8,128)S(1)}, u32[]{:S(2)}, u32[]{:S(2)}) collective-permute-start(f32[11,8,128]{2,1,0:T(8,128)S(1)} %get-tuple-element.20), channel_id=1, source_target_pairs={{0,272},{272,0},{16,288},{288,16},{32,304},{304,32},{48,320},{320,... | collective-permute-start | bytes 135176 | tf_op jit(solution)/shard_map/ppermute | solution.py:559
  47.2 10.0 %collective-permute-start.3 = (f32[35,8,128]{2,1,0:T(8,128)S(1)}, f32[35,8,128]{2,1,0:T(8,128)S(1)}, u32[]{:S(2)}, u32[]{:S(2)}) collective-permute-start(f32[35,8,128]{2,1,0:T(8,128)S(1)} %get-tuple-element.22.yp), channel_id=1, source_target_pairs={{0,257},{257,0},{1,258},{258,1},{2,259},{259,2},{3,260},{260,3},{4... | collective-permute-start | bytes 430088 | tf_op jit(solution)/shard_map/ppermute | solution.py:559
  57.3 2.2 %copy-start.1 = (f32[16,8,128]{2,1,0:T(8,128)S(1)}, f32[16,8,128]{2,1,0:T(8,128)}, u32[]{:S(2)}) copy-start(f32[16,8,128]{2,1,0:T(8,128)} %m.1) | copy-start | bytes 196612
  57.3 2.2 %copy-start.2 = (f32[16,8,128]{2,1,0:T(8,128)S(1)}, f32[16,8,128]{2,1,0:T(8,128)}, u32[]{:S(2)}) copy-start(f32[16,8,128]{2,1,0:T(8,128)} %f.1) | copy-start | bytes 196612

commit v6 on v5

--- a/solution.py
+++ b/solution.py
@@ -175,10 +175,10 @@
 def column_fine(own, planes, xr, at, lo, hi):
     def load(p, z):
         if p < planes:
-            return xr[1, at + 2 * p + z] * lo
+            return xr[1, 0, at + 2 * p + z] * lo
         if p < 16 + planes:
             return own(p - planes, z)
-        return xr[0, at + 2 * (p - 16 - planes) + z] * hi
+        return xr[0, 1, at + 2 * (p - 16 - planes) + z] * hi
 
     return load
 
@@ -194,11 +194,11 @@
     mine = (sub_index() < 4) == (core() == 1)
     pack_fine(column_fine(own, 4, xr, x_at["h0"], lo, hi), 24, mine, yp, at["h0"])
     for k in range(2):
-        yp[at["h1"] + k] = xr[1, x_at["h1"] + k] * lo
-        yp[at["h1"] + 6 + k] = xr[0, x_at["h1"] + k] * hi
+        yp[at["h1"] + k] = xr[1, 0, x_at["h1"] + k] * lo
+        yp[at["h1"] + 6 + k] = xr[0, 1, x_at["h1"] + k] * hi
     for k in range(4):
         yp[at["h1"] + 2 + k] = h1(k)
-    two = [xr[1, x_at["h2"]] * lo, h2(), xr[0, x_at["h2"]] * hi]
+    two = [xr[1, 0, x_at["h2"]] * lo, h2(), xr[0, 1, x_at["h2"]] * hi]
     for k in range(3):
         yp[at["h2"] + k] = two[k]
         y2p[k] = two[k]
@@ -216,7 +216,7 @@
     mine = (sub < 4) == (core() == 1)
     weights = column_fine(lambda x, z: own[z, OWN["w"] + x], 1, xr, X_FIRST["w"], 1.0, 1.0)
     pack_fine(weights, 18, mine, yp, at["w"])
-    low, high = xr[1, X_FIRST["w12"]], xr[0, X_FIRST["w12"]]
+    low, high = xr[1, 0, X_FIRST["w12"]], xr[0, 1, X_FIRST["w12"]]
     for k in range(4):
         yp[at["w1"] + k] = coarse[COARSE["w1"] + k]
     yp[at["w1"] + 4] = jnp.where(sub < 4, low, turn(high, 4))
@@ -283,7 +283,7 @@
     for k in range(3):
         tile, far = at["h2"] + k, at["far"] + k
         own, above, below = yp[tile], yr[0, tile] * yhi, yr[1, tile] * ylo
-        above2, below2 = yr[0, far + 3] * yhi2, yr[1, far] * ylo2
+        above2, below2 = yr[1, far + 3] * yhi2, yr[0, far] * ylo2
         for i in range(4):
             first = jnp.where(sub < 2, turn(own, -2 * i), turn(above, 2 - 2 * i))
             upper = keep(sub < 6, turn(above2, 4 - 2 * i))
@@ -545,28 +545,28 @@
     return (*dims, *TILE)
 
 
-def pairs(axis, distance):
-    size = lax.axis_size(axis)
-    return [[i, size + i + distance] for i in range(size - distance)]
-
-
 def share(value):
     return lax.all_gather(value, "group", axis=0)
 
 
-def swap(packed, axis):
-    moves = [move for a, b in pairs(axis, 1) for move in ((a, b), (b, a))]
-    return lax.ppermute(packed, ("group", axis), moves)
-
-
 def trade_x(packed):
-    return share(swap(packed, "gx"))
+    names = ("group", "gx", "gy")
+    sizes = [lax.axis_size(name) for name in names]
+    index = np.arange(np.prod(sizes)).reshape(sizes)
+    inner = np.stack([index[0, :-1], index[1, 1:]], axis=-1).reshape(-1, 2)
+    ends = np.concatenate([index[0, -1], index[1, 0]]).reshape(-1, 2)
+    groups = np.concatenate([inner, ends]).tolist()
+    return share(lax.all_gather(packed, names, axis=0, axis_index_groups=groups))
 
 
 def trade_y(packed, packed_far):
-    near = swap(packed, "gy")
     size = lax.axis_size("gy")
-    groups = [*pairs("gy", 2), [size - 2, size - 1], [size, size + 1]]
+    moves = []
+    for i in range(size - 1):
+        moves += [(i, size + i + 1), (size + i + 1, i)]
+    near = lax.ppermute(packed, ("group", "gy"), moves)
+    groups = [[size + i, i + 2] for i in range(size - 2)]
+    groups += [[0, 1], [2 * size - 2, 2 * size - 1]]
     far = lax.all_gather(packed_far, ("group", "gy"), axis=0, tiled=True, axis_index_groups=groups)
     return share(jnp.concatenate([near, far], axis=0))
 

time: 62.6 us -> 60.2 us (0.962)
  blocking collectives: 27 us -> 42.4 us
  waiting for transfers between devices: 13.6 us -> 0.01 us
  starting transfers between devices: 15.5 us -> 10.6 us
  Pallas kernels: 5.4 us -> 6.09 us
    all_gather x0 -> x2, blocking collectives: none -> 17.9 us  [trade_x(): lax.all_gather(packed, names, axis=0, axis_index_groups=groups)]
    ppermute x4 -> x2, waiting for transfers between devices: 13.6 us -> 0.01 us  [trade_y(): near = lax.ppermute(packed, ('group', 'gy'), moves)]
    ppermute x4 -> x2, starting transfers between devices: 15.5 us -> 10.6 us  [trade_y(): near = lax.ppermute(packed, ('group', 'gy'), moves)]
    all_gather x2, blocking collectives: 12.5 us -> 10.7 us  [trade_y(): lax.all_gather(packed_far, ('group', 'gy'), axis=0, tiled=True, axis_inde...]
    all_gather x5, blocking collectives: 14.5 us -> 13.8 us  [share(): return lax.all_gather(value, 'group', axis=0)]
    pallas_call x6, Pallas kernels: 5.4 us -> 6.09 us  [call(): pl.pallas_call(kernel, out_shape=[jax.ShapeDtypeStruct(shape, F32) for sh...]
  transfers between devices with their start and end apart: 4 -> 2, of which waited for: 2 -> 0; matrix products, arithmetic and copies ran while one was open for 0% -> 0% of each run, Pallas kernels for 0% -> 0%
where the time goes in v6:
time: 60.2 us; the launch traced here: 59.9 us
  blocking collectives  42.4 us (70%)
  starting transfers between devices  10.6 us (18%)
  Pallas kernels  6.09 us (10%)
  between operations  0.72 us (1%)
    all_gather x2, blocking collectives, trade_x(): lax.all_gather(packed, names, axis=0, axis_index_groups=groups)  17.9 us
    all_gather x5, blocking collectives, share(): return lax.all_gather(value, 'group', axis=0)  13.8 us
    all_gather x2, blocking collectives, trade_y(): lax.all_gather(packed_far, ('group', 'gy'), axis=0, tiled=True, axis_inde...  10.7 us
    ppermute x2, starting transfers between devices, trade_y(): near = lax.ppermute(packed, ('group', 'gy'), moves)  10.6 us
    pallas_call x6, Pallas kernels, call(): pl.pallas_call(kernel, out_shape=[jax.ShapeDtypeStruct(shape, F32) for sh...  6.09 us
  transfers between devices with their start and end apart: 2, of which 0 were waited for; matrix products, arithmetic and copies ran while one was open for 0% of the time, Pallas kernels for 0%

profile of v6, /device:TPU:241, one launch (start us, length us, event | category | flops | bytes accessed | tf_op | source)
XLA Modules:
  0.0 59.9 jit_solution(17416981434820921591)
XLA Ops:
  0.6 1.2 %block_sums.1 = f32[43,8,128]{2,1,0:T(8,128)S(1)} custom-call(f32[16,8,128]{2,1,0:T(8,128)} %m.1, f32[16,8,128]{2,1,0:T(8,128)} %f.1, s32[2,3]{1,0:T(2,128)} %sweeps_whole.1), custom_call_target="tpu_custom_call" | custom-call | tf_op jit(solution)/shard_map/block_sums/pallas_call | solution.py:529
  1.8 2.4 %all-gather = f32[86,8,128]{2,1,0:T(8,128)S(1)} all-gather(f32[43,8,128]{2,1,0:T(8,128)S(1)} %block_sums.1), channel_id=2, replica_groups=mesh['group'=2,'gx'=16,'gy'=16] {'group'}, dimensions={0}, use_global_device_ids=true | all-gather | bytes 528384 | tf_op jit(solution)/shard_map/all_gather | solution.py:549
  4.2 9.1 %all-gather.1 = f32[28,8,128]{2,1,0:T(8,128)S(1)} all-gather(f32[14,8,128]{2,1,0:T(8,128)S(1)} %get-tuple-element.16), channel_id=3, replica_groups={{0,272},{1,273},{2,274},{3,275},{4,276},{5,277},{6,278},{7,279},{8,280}..., dimensions={0}, use_global_device_ids=true | all-gather | bytes 172032 | tf_op jit(solution)/shard_map/all_gather | solution.py:559
  13.3 3.2 %all-gather.2 = f32[4,14,8,128]{3,2,1,0:T(8,128)S(1)} all-gather(f32[2,14,8,128]{3,2,1,0:T(8,128)S(1)} %bitcast.17), channel_id=4, replica_groups=mesh['group'=2,'gx'=16,'gy'=16] {'group'}, dimensions={0}, use_global_device_ids=true | all-gather | bytes 344064 | tf_op jit(solution)/shard_map/all_gather | solution.py:549
  16.5 6.0 %collective-permute-start = (f32[60,8,128]{2,1,0:T(8,128)S(1)}, f32[60,8,128]{2,1,0:T(8,128)S(1)}, u32[]{:S(2)}, u32[]{:S(2)}) collective-permute-start(f32[60,8,128]{2,1,0:T(8,128)S(1)} %get-tuple-element.17.yp), channel_id=1, source_target_pairs={{0,257},{257,0},{1,258},{258,1},{2,259},{259,2},{3,260},{260,3},{4... | collective-permute-start | bytes 737288 | tf_op jit(solution)/shard_map/ppermute | solution.py:567
  22.5 5.3 %all_gather.54 = f32[6,8,128]{2,1,0:T(8,128)S(1)} all-gather(f32[3,8,128]{2,1,0:T(8,128)S(1)} %get-tuple-element.18), channel_id=1, replica_groups={{256,2},{257,3},{258,4},{259,5},{260,6},{261,7},{262,8},{263,9},{264,10..., dimensions={0}, use_global_device_ids=true | all-gather | bytes 36864 | tf_op jit(solution)/shard_map/all_gather | solution.py:570
  27.9 0.0 collective-permute-done
  27.9 0.0 copy-start
  27.9 0.0 copy-start.3
  27.9 2.3 %all-gather.3 = f32[132,8,128]{2,1,0:T(8,128)S(1)} all-gather(f32[66,8,128]{2,1,0:T(8,128)S(1)} %pad_maximum_fusion), channel_id=5, replica_groups=mesh['group'=2,'gx'=16,'gy'=16] {'group'}, dimensions={0}, use_global_device_ids=true | all-gather | bytes 811008 | tf_op jit(solution)/shard_map/all_gather | solution.py:549
  30.2 0.0 copy-done
  30.2 0.0 copy-done.3
  30.2 2.1 %first_cycle.1 = (f32[11,8,128]{2,1,0:T(8,128)S(1)}, f32[18,4,8,128]{3,2,1,0:T(8,128)S(1)}, f32[18,4,8,128]{3,2,1,0:T(8,128)S(1)}, f32[10,2,8,128]{3,2,1,0:T(8,1...) custom-call(f32[2,43,8,128]{3,2,1,0:T(8,128)S(1)} %bitcast.9, ...), custom_call_target="tpu_custom_call" | custom-call | tf_op jit(solution)/shard_map/first_cycle/pallas_call | solution.py:529
  32.3 8.8 %all-gather.4 = f32[22,8,128]{2,1,0:T(8,128)S(1)} all-gather(f32[11,8,128]{2,1,0:T(8,128)S(1)} %get-tuple-element.20), channel_id=6, replica_groups={{0,272},{1,273},{2,274},{3,275},{4,276},{5,277},{6,278},{7,279},{8,280}..., dimensions={0}, use_global_device_ids=true | all-gather | bytes 135168 | tf_op jit(solution)/shard_map/all_gather | solution.py:559
  41.2 3.7 %all-gather.5 = f32[4,11,8,128]{3,2,1,0:T(8,128)S(1)} all-gather(f32[2,11,8,128]{3,2,1,0:T(8,128)S(1)} %bitcast.18), channel_id=7, replica_groups=mesh['group'=2,'gx'=16,'gy'=16] {'group'}, dimensions={0}, use_global_device_ids=true | all-gather | bytes 270336 | tf_op jit(solution)/shard_map/all_gather | solution.py:549
  44.9 4.6 %collective-permute-start.1 = (f32[35,8,128]{2,1,0:T(8,128)S(1)}, f32[35,8,128]{2,1,0:T(8,128)S(1)}, u32[]{:S(2)}, u32[]{:S(2)}) collective-permute-start(f32[35,8,128]{2,1,0:T(8,128)S(1)} %get-tuple-element.22.yp), channel_id=1, source_target_pairs={{0,257},{257,0},{1,258},{258,1},{2,259},{259,2},{3,260},{260,3},{4... | collective-permute-start | bytes 430088 | tf_op jit(solution)/shard_map/ppermute | solution.py:567
  49.5 5.3 %all_gather.61 = f32[6,8,128]{2,1,0:T(8,128)S(1)} all-gather(f32[3,8,128]{2,1,0:T(8,128)S(1)} %get-tuple-element.23), channel_id=1, replica_groups={{256,2},{257,3},{258,4},{259,5},{260,6},{261,7},{262,8},{263,9},{264,10..., dimensions={0}, use_global_device_ids=true | all-gather | bytes 36864 | tf_op jit(solution)/shard_map/all_gather | solution.py:570
  54.8 0.0 collective-permute-done.1
  54.9 0.0 copy-start.1
  54.9 0.0 copy-start.2
  54.9 2.2 %all-gather.6 = f32[82,8,128]{2,1,0:T(8,128)S(1)} all-gather(f32[41,8,128]{2,1,0:T(8,128)S(1)} %pad_maximum_fusion.1), channel_id=8, replica_groups=mesh['group'=2,'gx'=16,'gy'=16] {'group'}, dimensions={0}, use_global_device_ids=true | all-gather | bytes 503808 | tf_op jit(solution)/shard_map/all_gather | solution.py:549
  57.1 0.0 copy-done.1
  57.1 0.0 copy-done.2
  57.1 2.8 %second_cycle.1 = (f32[16,8,128]{2,1,0:T(8,128)}, f32[16,8,128]{2,1,0:T(8,128)}) custom-call(f32[2,43,8,128]{3,2,1,0:T(8,128)S(1)} %bitcast.10, f32[16,8,128]{2,1,0:T(8,128)S(1)} %copy-done.1, f32[16,8,128]{2,1,0:T(8,128)S(1)} %copy-done.2, f32[16,2,8,128]{3,2,1,0:T(8,128)S(1)} %get-tuple-element.19.h0, f32[2,2,11,8,128]{4,3,2,1,0:T(8,128)S(1)} %bitcast.15, ...), custom_call_target="tpu_custom_call" | custom-call | tf_op jit(solution)/shard_map/second_cycle/pallas_call | solution.py:529
  (5 shorter events, 0.1 us)
Async XLA Ops:
  16.5 11.4 %collective-permute-start = (f32[60,8,128]{2,1,0:T(8,128)S(1)}, f32[60,8,128]{2,1,0:T(8,128)S(1)}, u32[]{:S(2)}, u32[]{:S(2)}) collective-permute-start(f32[60,8,128]{2,1,0:T(8,128)S(1)} %get-tuple-element.17.yp), channel_id=1, source_target_pairs={{0,257},{257,0},{1,258},{258,1},{2,259},{259,2},{3,260},{260,3},{4... | collective-permute-start | bytes 737288 | tf_op jit(solution)/shard_map/ppermute | solution.py:567
  27.9 2.4 %copy-start = (bf16[256,256]{1,0:T(8,128)(2,1)S(1)}, bf16[256,256]{1,0:T(8,128)(2,1)}, u32[]{:S(2)}) copy-start(bf16[256,256]{1,0:T(8,128)(2,1)} %constant.5.clone.copies) | copy-start | bytes 393220
  27.9 2.3 %copy-start.3 = (bf16[256,256]{1,0:T(8,128)(2,1)S(1)}, bf16[256,256]{1,0:T(8,128)(2,1)}, u32[]{:S(2)}) copy-start(bf16[256,256]{1,0:T(8,128)(2,1)} %constant.4.clone.sums) | copy-start | bytes 393220
  44.9 9.9 %collective-permute-start.1 = (f32[35,8,128]{2,1,0:T(8,128)S(1)}, f32[35,8,128]{2,1,0:T(8,128)S(1)}, u32[]{:S(2)}, u32[]{:S(2)}) collective-permute-start(f32[35,8,128]{2,1,0:T(8,128)S(1)} %get-tuple-element.22.yp), channel_id=1, source_target_pairs={{0,257},{257,0},{1,258},{258,1},{2,259},{259,2},{3,260},{260,3},{4... | collective-permute-start | bytes 430088 | tf_op jit(solution)/shard_map/ppermute | solution.py:567
  54.9 2.2 %copy-start.1 = (f32[16,8,128]{2,1,0:T(8,128)S(1)}, f32[16,8,128]{2,1,0:T(8,128)}, u32[]{:S(2)}) copy-start(f32[16,8,128]{2,1,0:T(8,128)} %m.1) | copy-start | bytes 196612
  54.9 2.2 %copy-start.2 = (f32[16,8,128]{2,1,0:T(8,128)S(1)}, f32[16,8,128]{2,1,0:T(8,128)}, u32[]{:S(2)}) copy-start(f32[16,8,128]{2,1,0:T(8,128)} %f.1) | copy-start | bytes 196612

commit v7 on v6

--- a/solution.py
+++ b/solution.py
@@ -22,7 +22,7 @@
 COARSE = dict(h1=0, w1=4, h2=8, w2=9, size=10)
 X_FIRST = dict(h0=0, h1=8, h2=10, w=11, w12=13, size=14)
 X_SECOND = dict(h0=0, h1=8, h2=10, size=11)
-Y_FIRST = dict(h0=0, h1=24, h2=32, w=35, w1=53, w2=58, size=60, far=60)
+Y_FIRST = dict(h0=0, h1=24, h2=32, w=35, w1=41, w2=46, size=48, far=48)
 Y_SECOND = dict(h0=0, h1=24, h2=32, size=35, far=35)
 
 LANES = np.arange(256)
@@ -119,13 +119,17 @@
     for copy in copies:
         copy.start()
     sums = half_sums()
-    for copy in copies:
+    copies[0].wait()
+    m_tiles = [m[x] for x in range(16)]
+    m_sums = plane_sums(m_tiles)
+    for x in range(16):
+        out[OWN["w"] + x] = m_tiles[x]
+    for copy in copies[1:]:
         copy.wait()
-    m_tiles, f_tiles = ([ref[x] for x in range(16)] for ref in (m, f))
+    f_tiles = [f[x] for x in range(16)]
     for x in range(16):
         out[OWN["h0"] + x] = LEVEL[0] * f_tiles[x] / m_tiles[x]
-        out[OWN["w"] + x] = m_tiles[x]
-    rows = jnp.concatenate(plane_sums(m_tiles) + plane_sums(f_tiles), axis=0)
+    rows = jnp.concatenate(m_sums + plane_sums(f_tiles), axis=0)
     total = exact_dot(rows, sums)
     out[OWN["counts"]] = jnp.zeros(TILE, F32)
     out[OWN["counts"], : sweeps.shape[0], : sweeps.shape[1]] = sweeps[...].astype(F32)
@@ -213,9 +217,16 @@
         *(xr, yp, y2p, X_FIRST, at),
     )
     sub = sub_index()
-    mine = (sub < 4) == (core() == 1)
     weights = column_fine(lambda x, z: own[z, OWN["w"] + x], 1, xr, X_FIRST["w"], 1.0, 1.0)
-    pack_fine(weights, 18, mine, yp, at["w"])
+    upward = core() == 0
+    for k in range(3):
+        for z in range(2):
+            packed = None
+            for i in range(min(8, 18 - 8 * k)):
+                tile = weights(8 * k + i, z)
+                row = turn(jnp.where(upward, turn(tile, 1), tile), i)
+                packed = row if i == 0 else jnp.where(sub < i, packed, row)
+            yp[at["w"] + 2 * k + z] = packed
     low, high = xr[1, 0, X_FIRST["w12"]], xr[0, 1, X_FIRST["w12"]]
     for k in range(4):
         yp[at["w1"] + k] = coarse[COARSE["w1"] + k]
@@ -247,6 +258,16 @@
                 for out in outs:
                     out[2 * k + i, z] = own
                     out[2 * k + i, 2 + z] = halos[i]
+
+
+def join_weights(load, yr, at, out):
+    sub = sub_index()
+    for p in range(18):
+        for z in range(2):
+            tile, i = at + 2 * (p // 8) + z, p % 8
+            above, below = turn(yr[0, tile], -i), turn(yr[1, tile], 7 - i)
+            out[p, z] = load(p, z)
+            out[p, 2 + z] = jnp.where(sub < 7, above, below)
 
 
 def four_rows(own, above, below, i):
@@ -463,7 +484,7 @@
     load = column_fine(lambda x, z: own[z, x], 4, xr, X_FIRST["h0"], lo, hi)
     join_fine(load, 24, yr, Y_FIRST["h0"], ylo, yhi, h0_all, q0)
     load = column_fine(lambda x, z: own[z, OWN["w"] + x], 1, xr, X_FIRST["w"], 1.0, 1.0)
-    join_fine(load, 18, yr, Y_FIRST["w"], 1.0, 1.0, w)
+    join_weights(load, yr, Y_FIRST["w"], w)
     join_h1(yp, yr, Y_FIRST["h1"], h1_all, q1)
     join_w1(yp, yr, iw1)
     join_h2(yp, yr, Y_FIRST, h2_all, q2)

time: 60.2 us -> 58.7 us (0.975)
  Pallas kernels: 6.09 us -> 5.25 us
    pallas_call x6, Pallas kernels: 6.09 us -> 5.25 us  [call(): pl.pallas_call(kernel, out_shape=[jax.ShapeDtypeStruct(shape, F32) for sh...]
where the time goes in v7:
time: 58.7 us; the launch traced here: 58.4 us
  blocking collectives  42.1 us (72%)
  starting transfers between devices  10.3 us (18%)
  Pallas kernels  5.25 us (9%)
  between operations  0.72 us (1%)
    all_gather x2, blocking collectives, trade_x(): lax.all_gather(packed, names, axis=0, axis_index_groups=groups)  17.7 us
    all_gather x5, blocking collectives, share(): return lax.all_gather(value, 'group', axis=0)  13.7 us
    all_gather x2, blocking collectives, trade_y(): lax.all_gather(packed_far, ('group', 'gy'), axis=0, tiled=True, axis_inde...  10.7 us
    ppermute x2, starting transfers between devices, trade_y(): near = lax.ppermute(packed, ('group', 'gy'), moves)  10.3 us
    pallas_call x6, Pallas kernels, call(): pl.pallas_call(kernel, out_shape=[jax.ShapeDtypeStruct(shape, F32) for sh...  5.25 us
  transfers between devices with their start and end apart: 2, of which 0 were waited for; matrix products, arithmetic and copies ran while one was open for 0% of the time, Pallas kernels for 0%

profile of v7, /device:TPU:241, one launch (start us, length us, event | category | flops | bytes accessed | tf_op | source)
XLA Modules:
  0.0 58.4 jit_solution(4735933696955145062)
XLA Ops:
  0.6 1.2 %block_sums.1 = f32[43,8,128]{2,1,0:T(8,128)S(1)} custom-call(f32[16,8,128]{2,1,0:T(8,128)} %m.1, f32[16,8,128]{2,1,0:T(8,128)} %f.1, s32[2,3]{1,0:T(2,128)} %sweeps_whole.1), custom_call_target="tpu_custom_call" | custom-call | tf_op jit(solution)/shard_map/block_sums/pallas_call | solution.py:550
  1.8 2.4 %all-gather = f32[86,8,128]{2,1,0:T(8,128)S(1)} all-gather(f32[43,8,128]{2,1,0:T(8,128)S(1)} %block_sums.1), channel_id=2, replica_groups=mesh['group'=2,'gx'=16,'gy'=16] {'group'}, dimensions={0}, use_global_device_ids=true | all-gather | bytes 528384 | tf_op jit(solution)/shard_map/all_gather | solution.py:570
  4.2 9.1 %all-gather.1 = f32[28,8,128]{2,1,0:T(8,128)S(1)} all-gather(f32[14,8,128]{2,1,0:T(8,128)S(1)} %get-tuple-element.16), channel_id=3, replica_groups={{0,272},{1,273},{2,274},{3,275},{4,276},{5,277},{6,278},{7,279},{8,280}..., dimensions={0}, use_global_device_ids=true | all-gather | bytes 172032 | tf_op jit(solution)/shard_map/all_gather | solution.py:580
  13.3 3.2 %all-gather.2 = f32[4,14,8,128]{3,2,1,0:T(8,128)S(1)} all-gather(f32[2,14,8,128]{3,2,1,0:T(8,128)S(1)} %bitcast.17), channel_id=4, replica_groups=mesh['group'=2,'gx'=16,'gy'=16] {'group'}, dimensions={0}, use_global_device_ids=true | all-gather | bytes 344064 | tf_op jit(solution)/shard_map/all_gather | solution.py:570
  16.5 6.0 %collective-permute-start = (f32[48,8,128]{2,1,0:T(8,128)S(1)}, f32[48,8,128]{2,1,0:T(8,128)S(1)}, u32[]{:S(2)}, u32[]{:S(2)}) collective-permute-start(f32[48,8,128]{2,1,0:T(8,128)S(1)} %get-tuple-element.17.yp), channel_id=1, source_target_pairs={{0,257},{257,0},{1,258},{258,1},{2,259},{259,2},{3,260},{260,3},{4... | collective-permute-start | bytes 589832 | tf_op jit(solution)/shard_map/ppermute | solution.py:588
  22.5 5.3 %all_gather.54 = f32[6,8,128]{2,1,0:T(8,128)S(1)} all-gather(f32[3,8,128]{2,1,0:T(8,128)S(1)} %get-tuple-element.18), channel_id=1, replica_groups={{256,2},{257,3},{258,4},{259,5},{260,6},{261,7},{262,8},{263,9},{264,10..., dimensions={0}, use_global_device_ids=true | all-gather | bytes 36864 | tf_op jit(solution)/shard_map/all_gather | solution.py:591
  27.8 0.0 collective-permute-done
  27.9 0.0 copy-start
  27.9 0.0 copy-start.3
  27.9 2.3 %all-gather.3 = f32[108,8,128]{2,1,0:T(8,128)S(1)} all-gather(f32[54,8,128]{2,1,0:T(8,128)S(1)} %pad_maximum_fusion), channel_id=5, replica_groups=mesh['group'=2,'gx'=16,'gy'=16] {'group'}, dimensions={0}, use_global_device_ids=true | all-gather | bytes 663552 | tf_op jit(solution)/shard_map/all_gather | solution.py:570
  30.2 0.0 copy-done
  30.2 0.0 copy-done.3
  30.2 1.2 %first_cycle.1 = (f32[11,8,128]{2,1,0:T(8,128)S(1)}, f32[18,4,8,128]{3,2,1,0:T(8,128)S(1)}, f32[18,4,8,128]{3,2,1,0:T(8,128)S(1)}, f32[10,2,8,128]{3,2,1,0:T(8,1...) custom-call(f32[2,43,8,128]{3,2,1,0:T(8,128)S(1)} %bitcast.9, ...), custom_call_target="tpu_custom_call" | custom-call | tf_op jit(solution)/shard_map/first_cycle/pallas_call | solution.py:550
  31.4 8.6 %all-gather.4 = f32[22,8,128]{2,1,0:T(8,128)S(1)} all-gather(f32[11,8,128]{2,1,0:T(8,128)S(1)} %get-tuple-element.20), channel_id=6, replica_groups={{0,272},{1,273},{2,274},{3,275},{4,276},{5,277},{6,278},{7,279},{8,280}..., dimensions={0}, use_global_device_ids=true | all-gather | bytes 135168 | tf_op jit(solution)/shard_map/all_gather | solution.py:580
  40.0 3.8 %all-gather.5 = f32[4,11,8,128]{3,2,1,0:T(8,128)S(1)} all-gather(f32[2,11,8,128]{3,2,1,0:T(8,128)S(1)} %bitcast.18), channel_id=7, replica_groups=mesh['group'=2,'gx'=16,'gy'=16] {'group'}, dimensions={0}, use_global_device_ids=true | all-gather | bytes 270336 | tf_op jit(solution)/shard_map/all_gather | solution.py:570
  43.8 4.3 %collective-permute-start.1 = (f32[35,8,128]{2,1,0:T(8,128)S(1)}, f32[35,8,128]{2,1,0:T(8,128)S(1)}, u32[]{:S(2)}, u32[]{:S(2)}) collective-permute-start(f32[35,8,128]{2,1,0:T(8,128)S(1)} %get-tuple-element.22.yp), channel_id=1, source_target_pairs={{0,257},{257,0},{1,258},{258,1},{2,259},{259,2},{3,260},{260,3},{4... | collective-permute-start | bytes 430088 | tf_op jit(solution)/shard_map/ppermute | solution.py:588
  48.1 5.3 %all_gather.61 = f32[6,8,128]{2,1,0:T(8,128)S(1)} all-gather(f32[3,8,128]{2,1,0:T(8,128)S(1)} %get-tuple-element.23), channel_id=1, replica_groups={{256,2},{257,3},{258,4},{259,5},{260,6},{261,7},{262,8},{263,9},{264,10..., dimensions={0}, use_global_device_ids=true | all-gather | bytes 36864 | tf_op jit(solution)/shard_map/all_gather | solution.py:591
  53.4 0.0 collective-permute-done.1
  53.4 0.0 copy-start.1
  53.4 0.0 copy-start.2
  53.5 2.2 %all-gather.6 = f32[82,8,128]{2,1,0:T(8,128)S(1)} all-gather(f32[41,8,128]{2,1,0:T(8,128)S(1)} %pad_maximum_fusion.1), channel_id=8, replica_groups=mesh['group'=2,'gx'=16,'gy'=16] {'group'}, dimensions={0}, use_global_device_ids=true | all-gather | bytes 503808 | tf_op jit(solution)/shard_map/all_gather | solution.py:570
  55.6 0.0 copy-done.1
  55.6 0.0 copy-done.2
  55.6 2.8 %second_cycle.1 = (f32[16,8,128]{2,1,0:T(8,128)}, f32[16,8,128]{2,1,0:T(8,128)}) custom-call(f32[2,43,8,128]{3,2,1,0:T(8,128)S(1)} %bitcast.10, f32[16,8,128]{2,1,0:T(8,128)S(1)} %copy-done.1, f32[16,8,128]{2,1,0:T(8,128)S(1)} %copy-done.2, f32[16,2,8,128]{3,2,1,0:T(8,128)S(1)} %get-tuple-element.19.h0, f32[2,2,11,8,128]{4,3,2,1,0:T(8,128)S(1)} %bitcast.15, ...), custom_call_target="tpu_custom_call" | custom-call | tf_op jit(solution)/shard_map/second_cycle/pallas_call | solution.py:550
  (5 shorter events, 0.1 us)
Async XLA Ops:
  16.5 11.4 %collective-permute-start = (f32[48,8,128]{2,1,0:T(8,128)S(1)}, f32[48,8,128]{2,1,0:T(8,128)S(1)}, u32[]{:S(2)}, u32[]{:S(2)}) collective-permute-start(f32[48,8,128]{2,1,0:T(8,128)S(1)} %get-tuple-element.17.yp), channel_id=1, source_target_pairs={{0,257},{257,0},{1,258},{258,1},{2,259},{259,2},{3,260},{260,3},{4... | collective-permute-start | bytes 589832 | tf_op jit(solution)/shard_map/ppermute | solution.py:588
  27.9 2.3 %copy-start = (bf16[256,256]{1,0:T(8,128)(2,1)S(1)}, bf16[256,256]{1,0:T(8,128)(2,1)}, u32[]{:S(2)}) copy-start(bf16[256,256]{1,0:T(8,128)(2,1)} %constant.5.clone.copies) | copy-start | bytes 393220
  27.9 2.3 %copy-start.3 = (bf16[256,256]{1,0:T(8,128)(2,1)S(1)}, bf16[256,256]{1,0:T(8,128)(2,1)}, u32[]{:S(2)}) copy-start(bf16[256,256]{1,0:T(8,128)(2,1)} %constant.4.clone.sums) | copy-start | bytes 393220
  43.8 9.6 %collective-permute-start.1 = (f32[35,8,128]{2,1,0:T(8,128)S(1)}, f32[35,8,128]{2,1,0:T(8,128)S(1)}, u32[]{:S(2)}, u32[]{:S(2)}) collective-permute-start(f32[35,8,128]{2,1,0:T(8,128)S(1)} %get-tuple-element.22.yp), channel_id=1, source_target_pairs={{0,257},{257,0},{1,258},{258,1},{2,259},{259,2},{3,260},{260,3},{4... | collective-permute-start | bytes 430088 | tf_op jit(solution)/shard_map/ppermute | solution.py:588
  53.4 2.2 %copy-start.1 = (f32[16,8,128]{2,1,0:T(8,128)S(1)}, f32[16,8,128]{2,1,0:T(8,128)}, u32[]{:S(2)}) copy-start(f32[16,8,128]{2,1,0:T(8,128)} %m.1) | copy-start | bytes 196612
  53.4 2.2 %copy-start.2 = (f32[16,8,128]{2,1,0:T(8,128)S(1)}, f32[16,8,128]{2,1,0:T(8,128)}, u32[]{:S(2)}) copy-start(f32[16,8,128]{2,1,0:T(8,128)} %f.1) | copy-start | bytes 196612

commit v8 on v7

--- a/solution.py
+++ b/solution.py
@@ -22,7 +22,7 @@
 COARSE = dict(h1=0, w1=4, h2=8, w2=9, size=10)
 X_FIRST = dict(h0=0, h1=8, h2=10, w=11, w12=13, size=14)
 X_SECOND = dict(h0=0, h1=8, h2=10, size=11)
-Y_FIRST = dict(h0=0, h1=24, h2=32, w=35, w1=41, w2=46, size=48, far=48)
+Y_FIRST = dict(h0=0, h1=24, h2=32, w=35, w12=41, size=43, far=43)
 Y_SECOND = dict(h0=0, h1=24, h2=32, size=35, far=35)
 
 LANES = np.arange(256)
@@ -208,6 +208,18 @@
         y2p[k] = two[k]
 
 
+def column_w1(p, coarse, xr):
+    if p in (0, 9):
+        return (xr[1, 0, X_FIRST["w12"]] if p == 0 else xr[0, 1, X_FIRST["w12"]]), 0
+    return coarse[COARSE["w1"] + (p - 1) // 2], 4 * ((p - 1) % 2)
+
+
+def column_w2(p, coarse, xr):
+    if p in (0, 5):
+        return (xr[1, 0, X_FIRST["w12"]] if p == 0 else xr[0, 1, X_FIRST["w12"]]), 4
+    return coarse[COARSE["w2"]], 2 * (p - 1)
+
+
 def first_rows_kernel(own, coarse, xr, yp, y2p):
     at = Y_FIRST
     pack_y(
@@ -227,12 +239,17 @@
                 row = turn(jnp.where(upward, turn(tile, 1), tile), i)
                 packed = row if i == 0 else jnp.where(sub < i, packed, row)
             yp[at["w"] + 2 * k + z] = packed
-    low, high = xr[1, 0, X_FIRST["w12"]], xr[0, 1, X_FIRST["w12"]]
-    for k in range(4):
-        yp[at["w1"] + k] = coarse[COARSE["w1"] + k]
-    yp[at["w1"] + 4] = jnp.where(sub < 4, low, turn(high, 4))
-    yp[at["w2"]] = coarse[COARSE["w2"]]
-    yp[at["w2"] + 1] = jnp.where(sub < 2, turn(low, 4), turn(high, 6))
+    for k in range(2):
+        packed = None
+        for i in range(8):
+            p = 8 * k + i
+            if p < 10:
+                (tile, start), last = column_w1(p, coarse, xr), 3
+            else:
+                (tile, start), last = column_w2(p - 10, coarse, xr), 1
+            row = turn(jnp.where(upward, turn(tile, -start - last), turn(tile, -start)), i)
+            packed = row if i == 0 else jnp.where(sub < i, packed, row)
+        yp[at["w12"] + k] = packed
 
 
 def second_rows_kernel(h0, h12, xr, yp, y2p):
@@ -288,14 +305,18 @@
                 out[2 * k + i, 0], out[2 * k + i, 1] = both
 
 
-def join_w1(yp, yr, out):
-    for k in range(5):
-        tile = Y_FIRST["w1"] + k
-        own, above, below = yp[tile], yr[0, tile], yr[1, tile]
-        for i in range(2):
-            p = 9 * i if k == 4 else 1 + 2 * k + i
-            first, second = four_rows(own, above, below, i)
-            out[p, 0], out[p, 1] = inverse(first), inverse(second)
+def join_coarse_weights(coarse, xr, yr, iw1, iw2):
+    sub = sub_index()
+    for p in range(16):
+        packed, i = Y_FIRST["w12"] + p // 8, p % 8
+        above, below = yr[0, packed], yr[1, packed]
+        if p < 10:
+            (tile, start), rows, out, plane = column_w1(p, coarse, xr), 4, iw1, p
+        else:
+            (tile, start), rows, out, plane = column_w2(p - 10, coarse, xr), 2, iw2, p - 10
+        own = turn(tile, -start)
+        out[plane, 0] = inverse(jnp.where(sub < rows, own, keep(sub == rows, turn(above, rows - i))))
+        out[plane, 1] = inverse(keep(sub == 7, turn(below, 7 - i)))
 
 
 def join_h2(yp, yr, at, *outs):
@@ -314,17 +335,6 @@
                 out[4 * k + i, 1] = keep(sub >= 4, lower)
 
 
-def join_w2(yp, yr, out):
-    sub = sub_index()
-    for p in range(6):
-        k, i = (1, p // 5) if p in (0, 5) else (0, p - 1)
-        tile = Y_FIRST["w2"] + k
-        own, above, below = yp[tile], yr[0, tile], yr[1, tile]
-        first = jnp.where(sub < 2, turn(own, -2 * i), turn(above, 2 - 2 * i))
-        out[p, 0] = inverse(keep(sub < 4, first))
-        out[p, 1] = inverse(keep(sub >= 6, turn(below, 6 - 2 * i)))
-
-
 def along_y(first, second):
     sub = sub_index()
     up_first, up_second = turn(first, 7), turn(second, 7)
@@ -377,11 +387,11 @@
         above = added(here, after)
         summed = along_yz(added(below, above))
         for part in range(parts):
-            spread = (masks[part // (parts // 2)] * factors[i]) * summed[part]
+            mask = masks[part // (parts // 2)]
+            spread = (mask if factors[i] is None else mask * factors[i]) * summed[part]
             source = h[x, part] if active is None else active * h[x, part]
             q[x, part] = (kept * here[part] + spread) + source
-        last, here, below = here, after, above
-    return last
+        here, below = after, above
 
 
 def relax_levels(counts, h0, q0, h1, q1, h2, q2):
@@ -403,14 +413,9 @@
         return 0
 
     def fine_sweep(_, __):
-        def half(j, before):
-            start = 1 + 11 * j
-            factors = [
-                jnp.where(start + i < 4, lo, jnp.where(start + i >= 20, hi, 1.0)) for i in range(11)
-            ]
-            return tuple(relax_planes(q0, h0, start, 11, 4, list(before), masks0, factors, None))
-
-        lax.fori_loop(0, 2, half, tuple(q0[0, part] for part in range(4)))
+        factors = [lo] * 3 + [None] * 16 + [hi] * 3
+        before = [q0[0, part] for part in range(4)]
+        relax_planes(q0, h0, 1, 22, 4, before, masks0, factors, None)
         return 0
 
     lax.fori_loop(1, jnp.maximum(counts[1], counts[2]), coarse_sweep, 0)
@@ -486,9 +491,8 @@
     load = column_fine(lambda x, z: own[z, OWN["w"] + x], 1, xr, X_FIRST["w"], 1.0, 1.0)
     join_weights(load, yr, Y_FIRST["w"], w)
     join_h1(yp, yr, Y_FIRST["h1"], h1_all, q1)
-    join_w1(yp, yr, iw1)
     join_h2(yp, yr, Y_FIRST, h2_all, q2)
-    join_w2(yp, yr, iw2)
+    join_coarse_weights(coarse, xr, yr, iw1, iw2)
     relax_levels(counts, h0_all, q0, h1_all, q1, h2_all, q2)
     iterate(corrections(q1, iw1, q2, iw2, copies), q0, w, None, pf)
 
@@ -526,22 +530,19 @@
     relax_levels(counts, h0_all, q0, h1_all, q1, h2_all, q2)
     iterate(corrections(q1, iw1, q2, iw2, copies), q0, w, pf, pf_all)
     first = core() == 0
-    sending = []
     for x, (here, defect) in enumerate(defects(pf_all)):
         mine, rest = (jnp.where(first, both[0], both[1]) for both in (here, defect))
         weight = m[x]
         solved[x] = mine / weight
         left[x] = f[x] - weight * rest
-        if x % 4 == 3:
-            done = pl.ds(x - 3, 4)
-            for k, (source, target) in enumerate(((solved, solution_out), (left, residual_out))):
-                copy = pltpu.make_async_copy(
-                    source.at[done], target.at[done], sent.at[2 * (x // 4) + k]
-                )
-                copy.start()
-                sending.append(copy)
-    for copy in sending:
-        copy.wait()
+    sends = [
+        pltpu.make_async_copy(source, target, sent.at[k])
+        for k, (source, target) in enumerate(((solved, solution_out), (left, residual_out)))
+    ]
+    for send in sends:
+        send.start()
+    for send in sends:
+        send.wait()
 
 
 def call(kernel, outs, scratch, name, *operands, outside=0, outs_outside=False):
@@ -646,7 +647,7 @@
     return call(
         last_kernel,
         [tiles(16), tiles(16)],
-        [*spaces, space(18, 4), space(16), space(16), pltpu.SemaphoreType.DMA((8,))],
+        [*spaces, space(18, 4), space(16), space(16), pltpu.SemaphoreType.DMA((2,))],
         "second_cycle",
         *(own, metric, forcing, h0, xr, yp, yr, pf, w, iw1, iw2, copies),
         outs_outside=True,

time: 58.7 us -> 58.4 us (level)
  no operation moved by 1% of the time
where the time goes in v8:
time: 58.4 us; the launch traced here: 58.1 us
  blocking collectives  41.8 us (72%)
  starting transfers between devices  10.2 us (17%)
  Pallas kernels  5.29 us (9%)
  between operations  0.72 us (1%)
    all_gather x2, blocking collectives, trade_x(): lax.all_gather(packed, names, axis=0, axis_index_groups=groups)  17.5 us
    all_gather x5, blocking collectives, share(): return lax.all_gather(value, 'group', axis=0)  13.6 us
    all_gather x2, blocking collectives, trade_y(): lax.all_gather(packed_far, ('group', 'gy'), axis=0, tiled=True, axis_inde...  10.7 us
    ppermute x2, starting transfers between devices, trade_y(): near = lax.ppermute(packed, ('group', 'gy'), moves)  10.2 us
    pallas_call x6, Pallas kernels, call(): pl.pallas_call(kernel, out_shape=[jax.ShapeDtypeStruct(shape, F32) for sh...  5.29 us
  transfers between devices with their start and end apart: 2, of which 0 were waited for; matrix products, arithmetic and copies ran while one was open for 0% of the time, Pallas kernels for 0%

profile of v8, /device:TPU:241, one launch (start us, length us, event | category | flops | bytes accessed | tf_op | source)
XLA Modules:
  0.0 58.1 jit_solution(268215370172255705)
XLA Ops:
  0.6 1.2 %block_sums.1 = f32[43,8,128]{2,1,0:T(8,128)S(1)} custom-call(f32[16,8,128]{2,1,0:T(8,128)} %m.1, f32[16,8,128]{2,1,0:T(8,128)} %f.1, s32[2,3]{1,0:T(2,128)} %sweeps_whole.1), custom_call_target="tpu_custom_call" | custom-call | tf_op jit(solution)/shard_map/block_sums/pallas_call | solution.py:551
  1.8 2.4 %all-gather = f32[86,8,128]{2,1,0:T(8,128)S(1)} all-gather(f32[43,8,128]{2,1,0:T(8,128)S(1)} %block_sums.1), channel_id=2, replica_groups=mesh['group'=2,'gx'=16,'gy'=16] {'group'}, dimensions={0}, use_global_device_ids=true | all-gather | bytes 528384 | tf_op jit(solution)/shard_map/all_gather | solution.py:571
  4.2 9.1 %all-gather.1 = f32[28,8,128]{2,1,0:T(8,128)S(1)} all-gather(f32[14,8,128]{2,1,0:T(8,128)S(1)} %get-tuple-element.16), channel_id=3, replica_groups={{0,272},{1,273},{2,274},{3,275},{4,276},{5,277},{6,278},{7,279},{8,280}..., dimensions={0}, use_global_device_ids=true | all-gather | bytes 172032 | tf_op jit(solution)/shard_map/all_gather | solution.py:581
  13.3 3.2 %all-gather.2 = f32[4,14,8,128]{3,2,1,0:T(8,128)S(1)} all-gather(f32[2,14,8,128]{3,2,1,0:T(8,128)S(1)} %bitcast.17), channel_id=4, replica_groups=mesh['group'=2,'gx'=16,'gy'=16] {'group'}, dimensions={0}, use_global_device_ids=true | all-gather | bytes 344064 | tf_op jit(solution)/shard_map/all_gather | solution.py:571
  16.4 0.1 first_rows.1
  16.5 6.0 %collective-permute-start = (f32[43,8,128]{2,1,0:T(8,128)S(1)}, f32[43,8,128]{2,1,0:T(8,128)S(1)}, u32[]{:S(2)}, u32[]{:S(2)}) collective-permute-start(f32[43,8,128]{2,1,0:T(8,128)S(1)} %get-tuple-element.17.yp), channel_id=1, source_target_pairs={{0,257},{257,0},{1,258},{258,1},{2,259},{259,2},{3,260},{260,3},{4... | collective-permute-start | bytes 528392 | tf_op jit(solution)/shard_map/ppermute | solution.py:589
  22.5 5.3 %all_gather.54 = f32[6,8,128]{2,1,0:T(8,128)S(1)} all-gather(f32[3,8,128]{2,1,0:T(8,128)S(1)} %get-tuple-element.18), channel_id=1, replica_groups={{256,2},{257,3},{258,4},{259,5},{260,6},{261,7},{262,8},{263,9},{264,10..., dimensions={0}, use_global_device_ids=true | all-gather | bytes 36864 | tf_op jit(solution)/shard_map/all_gather | solution.py:592
  27.9 0.0 collective-permute-done
  27.9 0.0 copy-start
  27.9 0.0 copy-start.3
  27.9 2.2 %all-gather.3 = f32[98,8,128]{2,1,0:T(8,128)S(1)} all-gather(f32[49,8,128]{2,1,0:T(8,128)S(1)} %pad_maximum_fusion), channel_id=5, replica_groups=mesh['group'=2,'gx'=16,'gy'=16] {'group'}, dimensions={0}, use_global_device_ids=true | all-gather | bytes 602112 | tf_op jit(solution)/shard_map/all_gather | solution.py:571
  30.1 0.0 copy-done
  30.1 0.0 copy-done.3
  30.1 1.5 %first_cycle.1 = (f32[11,8,128]{2,1,0:T(8,128)S(1)}, f32[18,4,8,128]{3,2,1,0:T(8,128)S(1)}, f32[18,4,8,128]{3,2,1,0:T(8,128)S(1)}, f32[10,2,8,128]{3,2,1,0:T(8,1...) custom-call(f32[2,43,8,128]{3,2,1,0:T(8,128)S(1)} %bitcast.9, ...), custom_call_target="tpu_custom_call" | custom-call | tf_op jit(solution)/shard_map/first_cycle/pallas_call | solution.py:551
  31.7 8.4 %all-gather.4 = f32[22,8,128]{2,1,0:T(8,128)S(1)} all-gather(f32[11,8,128]{2,1,0:T(8,128)S(1)} %get-tuple-element.20), channel_id=6, replica_groups={{0,272},{1,273},{2,274},{3,275},{4,276},{5,277},{6,278},{7,279},{8,280}..., dimensions={0}, use_global_device_ids=true | all-gather | bytes 135168 | tf_op jit(solution)/shard_map/all_gather | solution.py:581
  40.1 3.6 %all-gather.5 = f32[4,11,8,128]{3,2,1,0:T(8,128)S(1)} all-gather(f32[2,11,8,128]{3,2,1,0:T(8,128)S(1)} %bitcast.18), channel_id=7, replica_groups=mesh['group'=2,'gx'=16,'gy'=16] {'group'}, dimensions={0}, use_global_device_ids=true | all-gather | bytes 270336 | tf_op jit(solution)/shard_map/all_gather | solution.py:571
  43.8 4.2 %collective-permute-start.1 = (f32[35,8,128]{2,1,0:T(8,128)S(1)}, f32[35,8,128]{2,1,0:T(8,128)S(1)}, u32[]{:S(2)}, u32[]{:S(2)}) collective-permute-start(f32[35,8,128]{2,1,0:T(8,128)S(1)} %get-tuple-element.22.yp), channel_id=1, source_target_pairs={{0,257},{257,0},{1,258},{258,1},{2,259},{259,2},{3,260},{260,3},{4... | collective-permute-start | bytes 430088 | tf_op jit(solution)/shard_map/ppermute | solution.py:589
  48.0 5.3 %all_gather.61 = f32[6,8,128]{2,1,0:T(8,128)S(1)} all-gather(f32[3,8,128]{2,1,0:T(8,128)S(1)} %get-tuple-element.23), channel_id=1, replica_groups={{256,2},{257,3},{258,4},{259,5},{260,6},{261,7},{262,8},{263,9},{264,10..., dimensions={0}, use_global_device_ids=true | all-gather | bytes 36864 | tf_op jit(solution)/shard_map/all_gather | solution.py:592
  53.3 0.0 collective-permute-done.1
  53.3 0.0 copy-start.1
  53.3 0.0 copy-start.2
  53.3 2.2 %all-gather.6 = f32[82,8,128]{2,1,0:T(8,128)S(1)} all-gather(f32[41,8,128]{2,1,0:T(8,128)S(1)} %pad_maximum_fusion.1), channel_id=8, replica_groups=mesh['group'=2,'gx'=16,'gy'=16] {'group'}, dimensions={0}, use_global_device_ids=true | all-gather | bytes 503808 | tf_op jit(solution)/shard_map/all_gather | solution.py:571
  55.5 0.0 copy-done.1
  55.5 0.0 copy-done.2
  55.5 2.5 %second_cycle.1 = (f32[16,8,128]{2,1,0:T(8,128)}, f32[16,8,128]{2,1,0:T(8,128)}) custom-call(f32[2,43,8,128]{3,2,1,0:T(8,128)S(1)} %bitcast.10, f32[16,8,128]{2,1,0:T(8,128)S(1)} %copy-done.1, f32[16,8,128]{2,1,0:T(8,128)S(1)} %copy-done.2, f32[16,2,8,128]{3,2,1,0:T(8,128)S(1)} %get-tuple-element.19.h0, f32[2,2,11,8,128]{4,3,2,1,0:T(8,128)S(1)} %bitcast.14, ...), custom_call_target="tpu_custom_call" | custom-call | tf_op jit(solution)/shard_map/second_cycle/pallas_call | solution.py:551
  (4 shorter events, 0.1 us)
Async XLA Ops:
  16.5 11.4 %collective-permute-start = (f32[43,8,128]{2,1,0:T(8,128)S(1)}, f32[43,8,128]{2,1,0:T(8,128)S(1)}, u32[]{:S(2)}, u32[]{:S(2)}) collective-permute-start(f32[43,8,128]{2,1,0:T(8,128)S(1)} %get-tuple-element.17.yp), channel_id=1, source_target_pairs={{0,257},{257,0},{1,258},{258,1},{2,259},{259,2},{3,260},{260,3},{4... | collective-permute-start | bytes 528392 | tf_op jit(solution)/shard_map/ppermute | solution.py:589
  27.9 2.3 %copy-start = (bf16[256,256]{1,0:T(8,128)(2,1)S(1)}, bf16[256,256]{1,0:T(8,128)(2,1)}, u32[]{:S(2)}) copy-start(bf16[256,256]{1,0:T(8,128)(2,1)} %constant.5.clone.copies) | copy-start | bytes 393220
  27.9 2.2 %copy-start.3 = (bf16[256,256]{1,0:T(8,128)(2,1)S(1)}, bf16[256,256]{1,0:T(8,128)(2,1)}, u32[]{:S(2)}) copy-start(bf16[256,256]{1,0:T(8,128)(2,1)} %constant.4.clone.sums) | copy-start | bytes 393220
  43.8 9.5 %collective-permute-start.1 = (f32[35,8,128]{2,1,0:T(8,128)S(1)}, f32[35,8,128]{2,1,0:T(8,128)S(1)}, u32[]{:S(2)}, u32[]{:S(2)}) collective-permute-start(f32[35,8,128]{2,1,0:T(8,128)S(1)} %get-tuple-element.22.yp), channel_id=1, source_target_pairs={{0,257},{257,0},{1,258},{258,1},{2,259},{259,2},{3,260},{260,3},{4... | collective-permute-start | bytes 430088 | tf_op jit(solution)/shard_map/ppermute | solution.py:589
  53.3 2.2 %copy-start.1 = (f32[16,8,128]{2,1,0:T(8,128)S(1)}, f32[16,8,128]{2,1,0:T(8,128)}, u32[]{:S(2)}) copy-start(f32[16,8,128]{2,1,0:T(8,128)} %m.1) | copy-start | bytes 196612
  53.3 2.2 %copy-start.2 = (f32[16,8,128]{2,1,0:T(8,128)S(1)}, f32[16,8,128]{2,1,0:T(8,128)}, u32[]{:S(2)}) copy-start(f32[16,8,128]{2,1,0:T(8,128)} %f.1) | copy-start | bytes 196612

commit v9 on v8

--- a/solution.py
+++ b/solution.py
@@ -418,8 +418,15 @@
         relax_planes(q0, h0, 1, 22, 4, before, masks0, factors, None)
         return 0
 
-    lax.fori_loop(1, jnp.maximum(counts[1], counts[2]), coarse_sweep, 0)
-    lax.fori_loop(1, counts[0], fine_sweep, 0)
+    def both_sweeps(k, _):
+        coarse_sweep(k, 0)
+        return fine_sweep(k, 0)
+
+    coarse_count = jnp.maximum(counts[1], counts[2])
+    shared = jnp.minimum(counts[0], coarse_count)
+    lax.fori_loop(1, shared, both_sweeps, 0)
+    lax.fori_loop(shared, coarse_count, coarse_sweep, 0)
+    lax.fori_loop(shared, counts[0], fine_sweep, 0)
 
 
 def sweep_counts(own, cycle):

time: 58.4 us -> 57.3 us (0.981)
  Pallas kernels: 5.29 us -> 4.2 us
    pallas_call x6, Pallas kernels: 5.29 us -> 4.2 us  [call(): pl.pallas_call(kernel, out_shape=[jax.ShapeDtypeStruct(shape, F32) for sh...]
where the time goes in v9:
time: 57.3 us; the launch traced here: 57 us
  blocking collectives  41.8 us (73%)
  starting transfers between devices  10.2 us (18%)
  Pallas kernels  4.2 us (7%)
  between operations  0.72 us (1%)
    all_gather x2, blocking collectives, trade_x(): lax.all_gather(packed, names, axis=0, axis_index_groups=groups)  17.5 us
    all_gather x5, blocking collectives, share(): return lax.all_gather(value, 'group', axis=0)  13.6 us
    all_gather x2, blocking collectives, trade_y(): lax.all_gather(packed_far, ('group', 'gy'), axis=0, tiled=True, axis_inde...  10.7 us
    ppermute x2, starting transfers between devices, trade_y(): near = lax.ppermute(packed, ('group', 'gy'), moves)  10.2 us
    pallas_call x6, Pallas kernels, call(): pl.pallas_call(kernel, out_shape=[jax.ShapeDtypeStruct(shape, F32) for sh...  4.2 us
  transfers between devices with their start and end apart: 2, of which 0 were waited for; matrix products, arithmetic and copies ran while one was open for 0% of the time, Pallas kernels for 0%

profile of v9, /device:TPU:241, one launch (start us, length us, event | category | flops | bytes accessed | tf_op | source)
XLA Modules:
  0.0 57.0 jit_solution(1270742208584600314)
XLA Ops:
  0.6 1.2 %block_sums.1 = f32[43,8,128]{2,1,0:T(8,128)S(1)} custom-call(f32[16,8,128]{2,1,0:T(8,128)} %m.1, f32[16,8,128]{2,1,0:T(8,128)} %f.1, s32[2,3]{1,0:T(2,128)} %sweeps_whole.1), custom_call_target="tpu_custom_call" | custom-call | tf_op jit(solution)/shard_map/block_sums/pallas_call | solution.py:558
  1.8 2.4 %all-gather = f32[86,8,128]{2,1,0:T(8,128)S(1)} all-gather(f32[43,8,128]{2,1,0:T(8,128)S(1)} %block_sums.1), channel_id=2, replica_groups=mesh['group'=2,'gx'=16,'gy'=16] {'group'}, dimensions={0}, use_global_device_ids=true | all-gather | bytes 528384 | tf_op jit(solution)/shard_map/all_gather | solution.py:578
  4.2 9.1 %all-gather.1 = f32[28,8,128]{2,1,0:T(8,128)S(1)} all-gather(f32[14,8,128]{2,1,0:T(8,128)S(1)} %get-tuple-element.16), channel_id=3, replica_groups={{0,272},{1,273},{2,274},{3,275},{4,276},{5,277},{6,278},{7,279},{8,280}..., dimensions={0}, use_global_device_ids=true | all-gather | bytes 172032 | tf_op jit(solution)/shard_map/all_gather | solution.py:588
  13.3 3.2 %all-gather.2 = f32[4,14,8,128]{3,2,1,0:T(8,128)S(1)} all-gather(f32[2,14,8,128]{3,2,1,0:T(8,128)S(1)} %bitcast.17), channel_id=4, replica_groups=mesh['group'=2,'gx'=16,'gy'=16] {'group'}, dimensions={0}, use_global_device_ids=true | all-gather | bytes 344064 | tf_op jit(solution)/shard_map/all_gather | solution.py:578
  16.4 0.1 first_rows.1
  16.5 6.0 %collective-permute-start = (f32[43,8,128]{2,1,0:T(8,128)S(1)}, f32[43,8,128]{2,1,0:T(8,128)S(1)}, u32[]{:S(2)}, u32[]{:S(2)}) collective-permute-start(f32[43,8,128]{2,1,0:T(8,128)S(1)} %get-tuple-element.17.yp), channel_id=1, source_target_pairs={{0,257},{257,0},{1,258},{258,1},{2,259},{259,2},{3,260},{260,3},{4... | collective-permute-start | bytes 528392 | tf_op jit(solution)/shard_map/ppermute | solution.py:596
  22.5 5.3 %all_gather.54 = f32[6,8,128]{2,1,0:T(8,128)S(1)} all-gather(f32[3,8,128]{2,1,0:T(8,128)S(1)} %get-tuple-element.18), channel_id=1, replica_groups={{256,2},{257,3},{258,4},{259,5},{260,6},{261,7},{262,8},{263,9},{264,10..., dimensions={0}, use_global_device_ids=true | all-gather | bytes 36864 | tf_op jit(solution)/shard_map/all_gather | solution.py:599
  27.9 0.0 collective-permute-done
  27.9 0.0 copy-start
  27.9 0.0 copy-start.3
  27.9 2.2 %all-gather.3 = f32[98,8,128]{2,1,0:T(8,128)S(1)} all-gather(f32[49,8,128]{2,1,0:T(8,128)S(1)} %pad_maximum_fusion), channel_id=5, replica_groups=mesh['group'=2,'gx'=16,'gy'=16] {'group'}, dimensions={0}, use_global_device_ids=true | all-gather | bytes 602112 | tf_op jit(solution)/shard_map/all_gather | solution.py:578
  30.1 0.0 copy-done
  30.1 0.0 copy-done.3
  30.1 1.2 %first_cycle.1 = (f32[11,8,128]{2,1,0:T(8,128)S(1)}, f32[18,4,8,128]{3,2,1,0:T(8,128)S(1)}, f32[18,4,8,128]{3,2,1,0:T(8,128)S(1)}, f32[10,2,8,128]{3,2,1,0:T(8,1...) custom-call(f32[2,43,8,128]{3,2,1,0:T(8,128)S(1)} %bitcast.9, ...), custom_call_target="tpu_custom_call" | custom-call | tf_op jit(solution)/shard_map/first_cycle/pallas_call | solution.py:558
  31.4 8.4 %all-gather.4 = f32[22,8,128]{2,1,0:T(8,128)S(1)} all-gather(f32[11,8,128]{2,1,0:T(8,128)S(1)} %get-tuple-element.20), channel_id=6, replica_groups={{0,272},{1,273},{2,274},{3,275},{4,276},{5,277},{6,278},{7,279},{8,280}..., dimensions={0}, use_global_device_ids=true | all-gather | bytes 135168 | tf_op jit(solution)/shard_map/all_gather | solution.py:588
  39.8 3.7 %all-gather.5 = f32[4,11,8,128]{3,2,1,0:T(8,128)S(1)} all-gather(f32[2,11,8,128]{3,2,1,0:T(8,128)S(1)} %bitcast.18), channel_id=7, replica_groups=mesh['group'=2,'gx'=16,'gy'=16] {'group'}, dimensions={0}, use_global_device_ids=true | all-gather | bytes 270336 | tf_op jit(solution)/shard_map/all_gather | solution.py:578
  43.5 4.2 %collective-permute-start.1 = (f32[35,8,128]{2,1,0:T(8,128)S(1)}, f32[35,8,128]{2,1,0:T(8,128)S(1)}, u32[]{:S(2)}, u32[]{:S(2)}) collective-permute-start(f32[35,8,128]{2,1,0:T(8,128)S(1)} %get-tuple-element.22.yp), channel_id=1, source_target_pairs={{0,257},{257,0},{1,258},{258,1},{2,259},{259,2},{3,260},{260,3},{4... | collective-permute-start | bytes 430088 | tf_op jit(solution)/shard_map/ppermute | solution.py:596
  47.7 5.3 %all_gather.61 = f32[6,8,128]{2,1,0:T(8,128)S(1)} all-gather(f32[3,8,128]{2,1,0:T(8,128)S(1)} %get-tuple-element.23), channel_id=1, replica_groups={{256,2},{257,3},{258,4},{259,5},{260,6},{261,7},{262,8},{263,9},{264,10..., dimensions={0}, use_global_device_ids=true | all-gather | bytes 36864 | tf_op jit(solution)/shard_map/all_gather | solution.py:599
  53.0 0.0 collective-permute-done.1
  53.0 0.0 copy-start.1
  53.1 0.0 copy-start.2
  53.1 2.2 %all-gather.6 = f32[82,8,128]{2,1,0:T(8,128)S(1)} all-gather(f32[41,8,128]{2,1,0:T(8,128)S(1)} %pad_maximum_fusion.1), channel_id=8, replica_groups=mesh['group'=2,'gx'=16,'gy'=16] {'group'}, dimensions={0}, use_global_device_ids=true | all-gather | bytes 503808 | tf_op jit(solution)/shard_map/all_gather | solution.py:578
  55.2 0.0 copy-done.1
  55.2 0.0 copy-done.2
  55.2 1.7 %second_cycle.1 = (f32[16,8,128]{2,1,0:T(8,128)}, f32[16,8,128]{2,1,0:T(8,128)}) custom-call(f32[2,43,8,128]{3,2,1,0:T(8,128)S(1)} %bitcast.10, f32[16,8,128]{2,1,0:T(8,128)S(1)} %copy-done.1, f32[16,8,128]{2,1,0:T(8,128)S(1)} %copy-done.2, f32[16,2,8,128]{3,2,1,0:T(8,128)S(1)} %get-tuple-element.19.h0, f32[2,2,11,8,128]{4,3,2,1,0:T(8,128)S(1)} %bitcast.14, ...), custom_call_target="tpu_custom_call" | custom-call | tf_op jit(solution)/shard_map/second_cycle/pallas_call | solution.py:558
  (4 shorter events, 0.1 us)
Async XLA Ops:
  16.5 11.4 %collective-permute-start = (f32[43,8,128]{2,1,0:T(8,128)S(1)}, f32[43,8,128]{2,1,0:T(8,128)S(1)}, u32[]{:S(2)}, u32[]{:S(2)}) collective-permute-start(f32[43,8,128]{2,1,0:T(8,128)S(1)} %get-tuple-element.17.yp), channel_id=1, source_target_pairs={{0,257},{257,0},{1,258},{258,1},{2,259},{259,2},{3,260},{260,3},{4... | collective-permute-start | bytes 528392 | tf_op jit(solution)/shard_map/ppermute | solution.py:596
  27.9 2.3 %copy-start = (bf16[256,256]{1,0:T(8,128)(2,1)S(1)}, bf16[256,256]{1,0:T(8,128)(2,1)}, u32[]{:S(2)}) copy-start(bf16[256,256]{1,0:T(8,128)(2,1)} %constant.5.clone.copies) | copy-start | bytes 393220
  27.9 2.2 %copy-start.3 = (bf16[256,256]{1,0:T(8,128)(2,1)S(1)}, bf16[256,256]{1,0:T(8,128)(2,1)}, u32[]{:S(2)}) copy-start(bf16[256,256]{1,0:T(8,128)(2,1)} %constant.4.clone.sums) | copy-start | bytes 393220
  43.5 9.5 %collective-permute-start.1 = (f32[35,8,128]{2,1,0:T(8,128)S(1)}, f32[35,8,128]{2,1,0:T(8,128)S(1)}, u32[]{:S(2)}, u32[]{:S(2)}) collective-permute-start(f32[35,8,128]{2,1,0:T(8,128)S(1)} %get-tuple-element.22.yp), channel_id=1, source_target_pairs={{0,257},{257,0},{1,258},{258,1},{2,259},{259,2},{3,260},{260,3},{4... | collective-permute-start | bytes 430088 | tf_op jit(solution)/shard_map/ppermute | solution.py:596
  53.0 2.2 %copy-start.1 = (f32[16,8,128]{2,1,0:T(8,128)S(1)}, f32[16,8,128]{2,1,0:T(8,128)}, u32[]{:S(2)}) copy-start(f32[16,8,128]{2,1,0:T(8,128)} %m.1) | copy-start | bytes 196612
  53.1 2.2 %copy-start.2 = (f32[16,8,128]{2,1,0:T(8,128)S(1)}, f32[16,8,128]{2,1,0:T(8,128)}, u32[]{:S(2)}) copy-start(f32[16,8,128]{2,1,0:T(8,128)} %f.1) | copy-start | bytes 196612

commit v10 on v9

--- a/solution.py
+++ b/solution.py
@@ -71,6 +71,14 @@
 
 def core():
     return lax.axis_index("group")
+
+
+def odd_x():
+    return lax.rem(lax.axis_index("gx"), 2)
+
+
+def upward_x():
+    return core() == odd_x()
 
 
 def flags():
@@ -149,7 +157,7 @@
 
 
 def pack_x(fine, h1, h2, xp, at):
-    upward = core() == 0
+    upward = upward_x()
     start = jnp.where(upward, 12, 0)
     for k in range(4):
         for z in range(2):
@@ -166,7 +174,7 @@
     h1, w1 = total[:4], total[4:8]
     h2, w2 = total[8:]
     pack_x(lambda x, z: own[z, x], h1, h2, xp, X_FIRST)
-    upward = core() == 0
+    upward = upward_x()
     edge = OWN["w"] + jnp.where(upward, 15, 0)
     for z in range(2):
         xp[X_FIRST["w"] + z] = own[z, edge]
@@ -179,10 +187,10 @@
 def column_fine(own, planes, xr, at, lo, hi):
     def load(p, z):
         if p < planes:
-            return xr[1, 0, at + 2 * p + z] * lo
+            return xr[1 - odd_x(), 0, at + 2 * p + z] * lo
         if p < 16 + planes:
             return own(p - planes, z)
-        return xr[0, 1, at + 2 * (p - 16 - planes) + z] * hi
+        return xr[odd_x(), 1, at + 2 * (p - 16 - planes) + z] * hi
 
     return load
 
@@ -198,11 +206,11 @@
     mine = (sub_index() < 4) == (core() == 1)
     pack_fine(column_fine(own, 4, xr, x_at["h0"], lo, hi), 24, mine, yp, at["h0"])
     for k in range(2):
-        yp[at["h1"] + k] = xr[1, 0, x_at["h1"] + k] * lo
-        yp[at["h1"] + 6 + k] = xr[0, 1, x_at["h1"] + k] * hi
+        yp[at["h1"] + k] = xr[1 - odd_x(), 0, x_at["h1"] + k] * lo
+        yp[at["h1"] + 6 + k] = xr[odd_x(), 1, x_at["h1"] + k] * hi
     for k in range(4):
         yp[at["h1"] + 2 + k] = h1(k)
-    two = [xr[1, 0, x_at["h2"]] * lo, h2(), xr[0, 1, x_at["h2"]] * hi]
+    two = [xr[1 - odd_x(), 0, x_at["h2"]] * lo, h2(), xr[odd_x(), 1, x_at["h2"]] * hi]
     for k in range(3):
         yp[at["h2"] + k] = two[k]
         y2p[k] = two[k]
@@ -210,13 +218,13 @@
 
 def column_w1(p, coarse, xr):
     if p in (0, 9):
-        return (xr[1, 0, X_FIRST["w12"]] if p == 0 else xr[0, 1, X_FIRST["w12"]]), 0
+        return (xr[1 - odd_x(), 0, X_FIRST["w12"]] if p == 0 else xr[odd_x(), 1, X_FIRST["w12"]]), 0
     return coarse[COARSE["w1"] + (p - 1) // 2], 4 * ((p - 1) % 2)
 
 
 def column_w2(p, coarse, xr):
     if p in (0, 5):
-        return (xr[1, 0, X_FIRST["w12"]] if p == 0 else xr[0, 1, X_FIRST["w12"]]), 4
+        return (xr[1 - odd_x(), 0, X_FIRST["w12"]] if p == 0 else xr[odd_x(), 1, X_FIRST["w12"]]), 4
     return coarse[COARSE["w2"]], 2 * (p - 1)
 
 
@@ -582,9 +590,12 @@
     names = ("group", "gx", "gy")
     sizes = [lax.axis_size(name) for name in names]
     index = np.arange(np.prod(sizes)).reshape(sizes)
-    inner = np.stack([index[0, :-1], index[1, 1:]], axis=-1).reshape(-1, 2)
-    ends = np.concatenate([index[0, -1], index[1, 0]]).reshape(-1, 2)
-    groups = np.concatenate([inner, ends]).tolist()
+    inner = [
+        np.stack([index[k, k:-1:2], index[k, k + 1 :: 2]], axis=-1)
+        for k in range(2)
+    ]
+    ends = [index[1, 0], index[1, -1]]
+    groups = np.concatenate([pair.reshape(-1, 2) for pair in [*inner, *ends]]).tolist()
     return share(lax.all_gather(packed, names, axis=0, axis_index_groups=groups))
 
 

time: 57.3 us -> 56.4 us (0.984)
  the two profiles are of different devices: /device:TPU:241 before, /device:TPU:9 now
where the time goes in v10:
time: 56.4 us; the launch traced here: 56.1 us
  blocking collectives  38.8 us (69%)
  starting transfers between devices  11.9 us (21%)
  Pallas kernels  4.61 us (8%)
  between operations  0.72 us (1%)
    all_gather x5, blocking collectives, share(): return lax.all_gather(value, 'group', axis=0)  20.9 us
    ppermute x2, starting transfers between devices, trade_y(): near = lax.ppermute(packed, ('group', 'gy'), moves)  11.9 us
    all_gather x2, blocking collectives, trade_y(): lax.all_gather(packed_far, ('group', 'gy'), axis=0, tiled=True, axis_inde...  10.7 us
    all_gather x2, blocking collectives, trade_x(): lax.all_gather(packed, names, axis=0, axis_index_groups=groups)  7.28 us
    pallas_call x6, Pallas kernels, call(): pl.pallas_call(kernel, out_shape=[jax.ShapeDtypeStruct(shape, F32) for sh...  4.61 us
  transfers between devices with their start and end apart: 2, of which 0 were waited for; matrix products, arithmetic and copies ran while one was open for 0% of the time, Pallas kernels for 0%

profile of v10, /device:TPU:9, one launch (start us, length us, event | category | flops | bytes accessed | tf_op | source)
XLA Modules:
  0.0 56.1 jit_solution(16413184603916006894)
XLA Ops:
  0.6 1.2 %block_sums.1 = f32[43,8,128]{2,1,0:T(8,128)S(1)} custom-call(f32[16,8,128]{2,1,0:T(8,128)} %m.1, f32[16,8,128]{2,1,0:T(8,128)} %f.1, s32[2,3]{1,0:T(2,128)} %sweeps_whole.1), custom_call_target="tpu_custom_call" | custom-call | tf_op jit(solution)/shard_map/block_sums/pallas_call | solution.py:566
  1.8 2.4 %all-gather = f32[86,8,128]{2,1,0:T(8,128)S(1)} all-gather(f32[43,8,128]{2,1,0:T(8,128)S(1)} %block_sums.1), channel_id=2, replica_groups=mesh['group'=2,'gx'=16,'gy'=16] {'group'}, dimensions={0}, use_global_device_ids=true | all-gather | bytes 528384 | tf_op jit(solution)/shard_map/all_gather | solution.py:586
  4.2 3.7 %all-gather.1 = f32[28,8,128]{2,1,0:T(8,128)S(1)} all-gather(f32[14,8,128]{2,1,0:T(8,128)S(1)} %get-tuple-element.16), channel_id=3, replica_groups={{0,16},{1,17},{2,18},{3,19},{4,20},{5,21},{6,22},{7,23},{8,24},{9,25},{..., dimensions={0}, use_global_device_ids=true | all-gather | bytes 172032 | tf_op jit(solution)/shard_map/all_gather | solution.py:599
  7.9 7.1 %all-gather.2 = f32[4,14,8,128]{3,2,1,0:T(8,128)S(1)} all-gather(f32[2,14,8,128]{3,2,1,0:T(8,128)S(1)} %bitcast.17), channel_id=4, replica_groups=mesh['group'=2,'gx'=16,'gy'=16] {'group'}, dimensions={0}, use_global_device_ids=true | all-gather | bytes 344064 | tf_op jit(solution)/shard_map/all_gather | solution.py:586
  15.0 0.1 first_rows.1
  15.1 4.5 %collective-permute-start = (f32[43,8,128]{2,1,0:T(8,128)S(1)}, f32[43,8,128]{2,1,0:T(8,128)S(1)}, u32[]{:S(2)}, u32[]{:S(2)}) collective-permute-start(f32[43,8,128]{2,1,0:T(8,128)S(1)} %get-tuple-element.17.yp), channel_id=1, source_target_pairs={{0,257},{257,0},{1,258},{258,1},{2,259},{259,2},{3,260},{260,3},{4... | collective-permute-start | bytes 528392 | tf_op jit(solution)/shard_map/ppermute | solution.py:607
  19.5 5.3 %all_gather.54 = f32[6,8,128]{2,1,0:T(8,128)S(1)} all-gather(f32[3,8,128]{2,1,0:T(8,128)S(1)} %get-tuple-element.18), channel_id=1, replica_groups={{256,2},{257,3},{258,4},{259,5},{260,6},{261,7},{262,8},{263,9},{264,10..., dimensions={0}, use_global_device_ids=true | all-gather | bytes 36864 | tf_op jit(solution)/shard_map/all_gather | solution.py:610
  24.9 0.0 collective-permute-done
  24.9 0.0 copy-start
  24.9 0.0 copy-start.3
  24.9 2.2 %all-gather.3 = f32[98,8,128]{2,1,0:T(8,128)S(1)} all-gather(f32[49,8,128]{2,1,0:T(8,128)S(1)} %pad_maximum_fusion), channel_id=5, replica_groups=mesh['group'=2,'gx'=16,'gy'=16] {'group'}, dimensions={0}, use_global_device_ids=true | all-gather | bytes 602112 | tf_op jit(solution)/shard_map/all_gather | solution.py:586
  27.1 0.0 copy-done
  27.1 0.0 copy-done.3
  27.1 1.4 %first_cycle.1 = (f32[11,8,128]{2,1,0:T(8,128)S(1)}, f32[18,4,8,128]{3,2,1,0:T(8,128)S(1)}, f32[18,4,8,128]{3,2,1,0:T(8,128)S(1)}, f32[10,2,8,128]{3,2,1,0:T(8,1...) custom-call(f32[2,43,8,128]{3,2,1,0:T(8,128)S(1)} %bitcast.9, ...), custom_call_target="tpu_custom_call" | custom-call | tf_op jit(solution)/shard_map/first_cycle/pallas_call | solution.py:566
  28.6 3.6 %all-gather.4 = f32[22,8,128]{2,1,0:T(8,128)S(1)} all-gather(f32[11,8,128]{2,1,0:T(8,128)S(1)} %get-tuple-element.20), channel_id=6, replica_groups={{0,16},{1,17},{2,18},{3,19},{4,20},{5,21},{6,22},{7,23},{8,24},{9,25},{..., dimensions={0}, use_global_device_ids=true | all-gather | bytes 135168 | tf_op jit(solution)/shard_map/all_gather | solution.py:599
  32.2 7.0 %all-gather.5 = f32[4,11,8,128]{3,2,1,0:T(8,128)S(1)} all-gather(f32[2,11,8,128]{3,2,1,0:T(8,128)S(1)} %bitcast.18), channel_id=7, replica_groups=mesh['group'=2,'gx'=16,'gy'=16] {'group'}, dimensions={0}, use_global_device_ids=true | all-gather | bytes 270336 | tf_op jit(solution)/shard_map/all_gather | solution.py:586
  39.2 7.4 %collective-permute-start.1 = (f32[35,8,128]{2,1,0:T(8,128)S(1)}, f32[35,8,128]{2,1,0:T(8,128)S(1)}, u32[]{:S(2)}, u32[]{:S(2)}) collective-permute-start(f32[35,8,128]{2,1,0:T(8,128)S(1)} %get-tuple-element.22.yp), channel_id=1, source_target_pairs={{0,257},{257,0},{1,258},{258,1},{2,259},{259,2},{3,260},{260,3},{4... | collective-permute-start | bytes 430088 | tf_op jit(solution)/shard_map/ppermute | solution.py:607
  46.6 5.3 %all_gather.61 = f32[6,8,128]{2,1,0:T(8,128)S(1)} all-gather(f32[3,8,128]{2,1,0:T(8,128)S(1)} %get-tuple-element.23), channel_id=1, replica_groups={{256,2},{257,3},{258,4},{259,5},{260,6},{261,7},{262,8},{263,9},{264,10..., dimensions={0}, use_global_device_ids=true | all-gather | bytes 36864 | tf_op jit(solution)/shard_map/all_gather | solution.py:610
  52.0 0.0 collective-permute-done.1
  52.0 0.0 copy-start.1
  52.0 0.0 copy-start.2
  52.0 2.2 %all-gather.6 = f32[82,8,128]{2,1,0:T(8,128)S(1)} all-gather(f32[41,8,128]{2,1,0:T(8,128)S(1)} %pad_maximum_fusion.1), channel_id=8, replica_groups=mesh['group'=2,'gx'=16,'gy'=16] {'group'}, dimensions={0}, use_global_device_ids=true | all-gather | bytes 503808 | tf_op jit(solution)/shard_map/all_gather | solution.py:586
  54.2 0.0 copy-done.1
  54.2 0.0 copy-done.2
  54.2 1.9 %second_cycle.1 = (f32[16,8,128]{2,1,0:T(8,128)}, f32[16,8,128]{2,1,0:T(8,128)}) custom-call(f32[2,43,8,128]{3,2,1,0:T(8,128)S(1)} %bitcast.10, f32[16,8,128]{2,1,0:T(8,128)S(1)} %copy-done.1, f32[16,8,128]{2,1,0:T(8,128)S(1)} %copy-done.2, f32[16,2,8,128]{3,2,1,0:T(8,128)S(1)} %get-tuple-element.19.h0, f32[2,2,11,8,128]{4,3,2,1,0:T(8,128)S(1)} %bitcast.14, ...), custom_call_target="tpu_custom_call" | custom-call | tf_op jit(solution)/shard_map/second_cycle/pallas_call | solution.py:566
  (4 shorter events, 0.1 us)
Async XLA Ops:
  15.1 9.8 %collective-permute-start = (f32[43,8,128]{2,1,0:T(8,128)S(1)}, f32[43,8,128]{2,1,0:T(8,128)S(1)}, u32[]{:S(2)}, u32[]{:S(2)}) collective-permute-start(f32[43,8,128]{2,1,0:T(8,128)S(1)} %get-tuple-element.17.yp), channel_id=1, source_target_pairs={{0,257},{257,0},{1,258},{258,1},{2,259},{259,2},{3,260},{260,3},{4... | collective-permute-start | bytes 528392 | tf_op jit(solution)/shard_map/ppermute | solution.py:607
  24.9 2.3 %copy-start = (bf16[256,256]{1,0:T(8,128)(2,1)S(1)}, bf16[256,256]{1,0:T(8,128)(2,1)}, u32[]{:S(2)}) copy-start(bf16[256,256]{1,0:T(8,128)(2,1)} %constant.5.clone.copies) | copy-start | bytes 393220
  24.9 2.2 %copy-start.3 = (bf16[256,256]{1,0:T(8,128)(2,1)S(1)}, bf16[256,256]{1,0:T(8,128)(2,1)}, u32[]{:S(2)}) copy-start(bf16[256,256]{1,0:T(8,128)(2,1)} %constant.4.clone.sums) | copy-start | bytes 393220
  39.2 12.8 %collective-permute-start.1 = (f32[35,8,128]{2,1,0:T(8,128)S(1)}, f32[35,8,128]{2,1,0:T(8,128)S(1)}, u32[]{:S(2)}, u32[]{:S(2)}) collective-permute-start(f32[35,8,128]{2,1,0:T(8,128)S(1)} %get-tuple-element.22.yp), channel_id=1, source_target_pairs={{0,257},{257,0},{1,258},{258,1},{2,259},{259,2},{3,260},{260,3},{4... | collective-permute-start | bytes 430088 | tf_op jit(solution)/shard_map/ppermute | solution.py:607
  52.0 2.2 %copy-start.1 = (f32[16,8,128]{2,1,0:T(8,128)S(1)}, f32[16,8,128]{2,1,0:T(8,128)}, u32[]{:S(2)}) copy-start(f32[16,8,128]{2,1,0:T(8,128)} %m.1) | copy-start | bytes 196612
  52.0 2.2 %copy-start.2 = (f32[16,8,128]{2,1,0:T(8,128)S(1)}, f32[16,8,128]{2,1,0:T(8,128)}, u32[]{:S(2)}) copy-start(f32[16,8,128]{2,1,0:T(8,128)} %f.1) | copy-start | bytes 196612

commit v11 on v10

--- a/solution.py
+++ b/solution.py
@@ -203,7 +203,7 @@
 
 def pack_y(own, h1, h2, xr, yp, y2p, x_at, at):
     lo, hi = flags()[:2]
-    mine = (sub_index() < 4) == (core() == 1)
+    mine = (sub_index() < 4) == (core() == 0)
     pack_fine(column_fine(own, 4, xr, x_at["h0"], lo, hi), 24, mine, yp, at["h0"])
     for k in range(2):
         yp[at["h1"] + k] = xr[1 - odd_x(), 0, x_at["h1"] + k] * lo
@@ -238,7 +238,7 @@
     )
     sub = sub_index()
     weights = column_fine(lambda x, z: own[z, OWN["w"] + x], 1, xr, X_FIRST["w"], 1.0, 1.0)
-    upward = core() == 0
+    upward = core() == 1
     for k in range(3):
         for z in range(2):
             packed = None
@@ -273,7 +273,7 @@
     sub = sub_index()
     for k in range(planes // 2):
         for z in range(2):
-            above, below = yr[0, at + 2 * k + z] * yhi, yr[1, at + 2 * k + z] * ylo
+            above, below = yr[1, at + 2 * k + z] * yhi, yr[0, at + 2 * k + z] * ylo
             halos = (
                 jnp.where(sub < 4, above, below),
                 turn(jnp.where(sub < 4, below, above), 4),
@@ -290,7 +290,7 @@
     for p in range(18):
         for z in range(2):
             tile, i = at + 2 * (p // 8) + z, p % 8
-            above, below = turn(yr[0, tile], -i), turn(yr[1, tile], 7 - i)
+            above, below = turn(yr[1, tile], -i), turn(yr[0, tile], 7 - i)
             out[p, z] = load(p, z)
             out[p, 2 + z] = jnp.where(sub < 7, above, below)
 
@@ -306,7 +306,7 @@
     ylo, yhi = flags()[2:4]
     for k in range(8):
         tile = at + k
-        own, above, below = yp[tile], yr[0, tile] * yhi, yr[1, tile] * ylo
+        own, above, below = yp[tile], yr[1, tile] * yhi, yr[0, tile] * ylo
         for i in range(2):
             both = four_rows(own, above, below, i)
             for out in outs:
@@ -317,7 +317,7 @@
     sub = sub_index()
     for p in range(16):
         packed, i = Y_FIRST["w12"] + p // 8, p % 8
-        above, below = yr[0, packed], yr[1, packed]
+        above, below = yr[1, packed], yr[0, packed]
         if p < 10:
             (tile, start), rows, out, plane = column_w1(p, coarse, xr), 4, iw1, p
         else:
@@ -332,8 +332,8 @@
     sub = sub_index()
     for k in range(3):
         tile, far = at["h2"] + k, at["far"] + k
-        own, above, below = yp[tile], yr[0, tile] * yhi, yr[1, tile] * ylo
-        above2, below2 = yr[1, far + 3] * yhi2, yr[0, far] * ylo2
+        own, above, below = yp[tile], yr[1, tile] * yhi, yr[0, tile] * ylo
+        above2, below2 = yr[0, far + 3] * yhi2, yr[1, far] * ylo2
         for i in range(4):
             first = jnp.where(sub < 2, turn(own, -2 * i), turn(above, 2 - 2 * i))
             upper = keep(sub < 6, turn(above2, 4 - 2 * i))
@@ -603,10 +603,10 @@
     size = lax.axis_size("gy")
     moves = []
     for i in range(size - 1):
-        moves += [(i, size + i + 1), (size + i + 1, i)]
+        moves += [(size + i, i + 1), (i + 1, size + i)]
     near = lax.ppermute(packed, ("group", "gy"), moves)
-    groups = [[size + i, i + 2] for i in range(size - 2)]
-    groups += [[0, 1], [2 * size - 2, 2 * size - 1]]
+    groups = [[i, size + i + 2] for i in range(size - 2)]
+    groups += [[size - 2, size - 1], [size, size + 1]]
     far = lax.all_gather(packed_far, ("group", "gy"), axis=0, tiled=True, axis_index_groups=groups)
     return share(jnp.concatenate([near, far], axis=0))
 

time: 56.4 us -> 56.2 us (level)
  the two profiles are of different devices: /device:TPU:9 before, /device:TPU:241 now
where the time goes in v11:
time: 56.2 us; the launch traced here: 56 us
  blocking collectives  45.3 us (81%)
  starting transfers between devices  5.07 us (9%)
  Pallas kernels  4.91 us (9%)
  between operations  0.72 us (1%)
    all_gather x2, blocking collectives, trade_x(): lax.all_gather(packed, names, axis=0, axis_index_groups=groups)  19.8 us
    all_gather x5, blocking collectives, share(): return lax.all_gather(value, 'group', axis=0)  12.9 us
    all_gather x2, blocking collectives, trade_y(): lax.all_gather(packed_far, ('group', 'gy'), axis=0, tiled=True, axis_inde...  12.6 us
    ppermute x2, starting transfers between devices, trade_y(): near = lax.ppermute(packed, ('group', 'gy'), moves)  5.07 us
    pallas_call x6, Pallas kernels, call(): pl.pallas_call(kernel, out_shape=[jax.ShapeDtypeStruct(shape, F32) for sh...  4.91 us
  transfers between devices with their start and end apart: 2, of which 0 were waited for; matrix products, arithmetic and copies ran while one was open for 0% of the time, Pallas kernels for 0%

profile of v11, /device:TPU:241, one launch (start us, length us, event | category | flops | bytes accessed | tf_op | source)
XLA Modules:
  0.0 56.0 jit_solution(17014329518356012302)
XLA Ops:
  0.6 1.2 %block_sums.1 = f32[43,8,128]{2,1,0:T(8,128)S(1)} custom-call(f32[16,8,128]{2,1,0:T(8,128)} %m.1, f32[16,8,128]{2,1,0:T(8,128)} %f.1, s32[2,3]{1,0:T(2,128)} %sweeps_whole.1), custom_call_target="tpu_custom_call" | custom-call | tf_op jit(solution)/shard_map/block_sums/pallas_call | solution.py:566
  1.8 2.4 %all-gather = f32[86,8,128]{2,1,0:T(8,128)S(1)} all-gather(f32[43,8,128]{2,1,0:T(8,128)S(1)} %block_sums.1), channel_id=2, replica_groups=mesh['group'=2,'gx'=16,'gy'=16] {'group'}, dimensions={0}, use_global_device_ids=true | all-gather | bytes 528384 | tf_op jit(solution)/shard_map/all_gather | solution.py:586
  4.2 9.7 %all-gather.1 = f32[28,8,128]{2,1,0:T(8,128)S(1)} all-gather(f32[14,8,128]{2,1,0:T(8,128)S(1)} %get-tuple-element.16), channel_id=3, replica_groups={{0,16},{1,17},{2,18},{3,19},{4,20},{5,21},{6,22},{7,23},{8,24},{9,25},{..., dimensions={0}, use_global_device_ids=true | all-gather | bytes 172032 | tf_op jit(solution)/shard_map/all_gather | solution.py:599
  13.9 2.0 %all-gather.2 = f32[4,14,8,128]{3,2,1,0:T(8,128)S(1)} all-gather(f32[2,14,8,128]{3,2,1,0:T(8,128)S(1)} %bitcast.17), channel_id=4, replica_groups=mesh['group'=2,'gx'=16,'gy'=16] {'group'}, dimensions={0}, use_global_device_ids=true | all-gather | bytes 344064 | tf_op jit(solution)/shard_map/all_gather | solution.py:586
  15.9 0.1 first_rows.1
  15.9 3.2 %collective-permute-start = (f32[43,8,128]{2,1,0:T(8,128)S(1)}, f32[43,8,128]{2,1,0:T(8,128)S(1)}, u32[]{:S(2)}, u32[]{:S(2)}) collective-permute-start(f32[43,8,128]{2,1,0:T(8,128)S(1)} %get-tuple-element.17.yp), channel_id=1, source_target_pairs={{256,1},{1,256},{257,2},{2,257},{258,3},{3,258},{259,4},{4,259},{2... | collective-permute-start | bytes 528392 | tf_op jit(solution)/shard_map/ppermute | solution.py:607
  19.1 6.2 %all_gather.54 = f32[6,8,128]{2,1,0:T(8,128)S(1)} all-gather(f32[3,8,128]{2,1,0:T(8,128)S(1)} %get-tuple-element.18), channel_id=1, replica_groups={{0,258},{1,259},{2,260},{3,261},{4,262},{5,263},{6,264},{7,265},{8,266}..., dimensions={0}, use_global_device_ids=true | all-gather | bytes 36864 | tf_op jit(solution)/shard_map/all_gather | solution.py:610
  25.3 0.0 collective-permute-done
  25.3 0.0 copy-start
  25.3 0.0 copy-start.3
  25.3 4.0 %all-gather.3 = f32[98,8,128]{2,1,0:T(8,128)S(1)} all-gather(f32[49,8,128]{2,1,0:T(8,128)S(1)} %pad_maximum_fusion), channel_id=5, replica_groups=mesh['group'=2,'gx'=16,'gy'=16] {'group'}, dimensions={0}, use_global_device_ids=true | all-gather | bytes 602112 | tf_op jit(solution)/shard_map/all_gather | solution.py:586
  29.3 0.0 copy-done
  29.3 0.0 copy-done.3
  29.3 1.4 %first_cycle.1 = (f32[11,8,128]{2,1,0:T(8,128)S(1)}, f32[18,4,8,128]{3,2,1,0:T(8,128)S(1)}, f32[18,4,8,128]{3,2,1,0:T(8,128)S(1)}, f32[10,2,8,128]{3,2,1,0:T(8,1...) custom-call(f32[2,43,8,128]{3,2,1,0:T(8,128)S(1)} %bitcast.9, ...), custom_call_target="tpu_custom_call" | custom-call | tf_op jit(solution)/shard_map/first_cycle/pallas_call | solution.py:566
  30.8 10.1 %all-gather.4 = f32[22,8,128]{2,1,0:T(8,128)S(1)} all-gather(f32[11,8,128]{2,1,0:T(8,128)S(1)} %get-tuple-element.20), channel_id=6, replica_groups={{0,16},{1,17},{2,18},{3,19},{4,20},{5,21},{6,22},{7,23},{8,24},{9,25},{..., dimensions={0}, use_global_device_ids=true | all-gather | bytes 135168 | tf_op jit(solution)/shard_map/all_gather | solution.py:599
  40.9 1.9 %all-gather.5 = f32[4,11,8,128]{3,2,1,0:T(8,128)S(1)} all-gather(f32[2,11,8,128]{3,2,1,0:T(8,128)S(1)} %bitcast.18), channel_id=7, replica_groups=mesh['group'=2,'gx'=16,'gy'=16] {'group'}, dimensions={0}, use_global_device_ids=true | all-gather | bytes 270336 | tf_op jit(solution)/shard_map/all_gather | solution.py:586
  42.8 1.9 %collective-permute-start.1 = (f32[35,8,128]{2,1,0:T(8,128)S(1)}, f32[35,8,128]{2,1,0:T(8,128)S(1)}, u32[]{:S(2)}, u32[]{:S(2)}) collective-permute-start(f32[35,8,128]{2,1,0:T(8,128)S(1)} %get-tuple-element.22.yp), channel_id=1, source_target_pairs={{256,1},{1,256},{257,2},{2,257},{258,3},{3,258},{259,4},{4,259},{2... | collective-permute-start | bytes 430088 | tf_op jit(solution)/shard_map/ppermute | solution.py:607
  44.8 6.3 %all_gather.61 = f32[6,8,128]{2,1,0:T(8,128)S(1)} all-gather(f32[3,8,128]{2,1,0:T(8,128)S(1)} %get-tuple-element.23), channel_id=1, replica_groups={{0,258},{1,259},{2,260},{3,261},{4,262},{5,263},{6,264},{7,265},{8,266}..., dimensions={0}, use_global_device_ids=true | all-gather | bytes 36864 | tf_op jit(solution)/shard_map/all_gather | solution.py:610
  51.1 0.0 collective-permute-done.1
  51.1 0.0 copy-start.1
  51.1 0.0 copy-start.2
  51.1 2.7 %all-gather.6 = f32[82,8,128]{2,1,0:T(8,128)S(1)} all-gather(f32[41,8,128]{2,1,0:T(8,128)S(1)} %pad_maximum_fusion.1), channel_id=8, replica_groups=mesh['group'=2,'gx'=16,'gy'=16] {'group'}, dimensions={0}, use_global_device_ids=true | all-gather | bytes 503808 | tf_op jit(solution)/shard_map/all_gather | solution.py:586
  53.8 0.0 copy-done.1
  53.8 0.0 copy-done.2
  53.8 2.2 %second_cycle.1 = (f32[16,8,128]{2,1,0:T(8,128)}, f32[16,8,128]{2,1,0:T(8,128)}) custom-call(f32[2,43,8,128]{3,2,1,0:T(8,128)S(1)} %bitcast.10, f32[16,8,128]{2,1,0:T(8,128)S(1)} %copy-done.1, f32[16,8,128]{2,1,0:T(8,128)S(1)} %copy-done.2, f32[16,2,8,128]{3,2,1,0:T(8,128)S(1)} %get-tuple-element.19.h0, f32[2,2,11,8,128]{4,3,2,1,0:T(8,128)S(1)} %bitcast.14, ...), custom_call_target="tpu_custom_call" | custom-call | tf_op jit(solution)/shard_map/second_cycle/pallas_call | solution.py:566
  (4 shorter events, 0.1 us)
Async XLA Ops:
  15.9 9.4 %collective-permute-start = (f32[43,8,128]{2,1,0:T(8,128)S(1)}, f32[43,8,128]{2,1,0:T(8,128)S(1)}, u32[]{:S(2)}, u32[]{:S(2)}) collective-permute-start(f32[43,8,128]{2,1,0:T(8,128)S(1)} %get-tuple-element.17.yp), channel_id=1, source_target_pairs={{256,1},{1,256},{257,2},{2,257},{258,3},{3,258},{259,4},{4,259},{2... | collective-permute-start | bytes 528392 | tf_op jit(solution)/shard_map/ppermute | solution.py:607
  25.3 4.0 %copy-start = (bf16[256,256]{1,0:T(8,128)(2,1)S(1)}, bf16[256,256]{1,0:T(8,128)(2,1)}, u32[]{:S(2)}) copy-start(bf16[256,256]{1,0:T(8,128)(2,1)} %constant.5.clone.copies) | copy-start | bytes 393220
  25.3 4.0 %copy-start.3 = (bf16[256,256]{1,0:T(8,128)(2,1)S(1)}, bf16[256,256]{1,0:T(8,128)(2,1)}, u32[]{:S(2)}) copy-start(bf16[256,256]{1,0:T(8,128)(2,1)} %constant.4.clone.sums) | copy-start | bytes 393220
  42.8 8.3 %collective-permute-start.1 = (f32[35,8,128]{2,1,0:T(8,128)S(1)}, f32[35,8,128]{2,1,0:T(8,128)S(1)}, u32[]{:S(2)}, u32[]{:S(2)}) collective-permute-start(f32[35,8,128]{2,1,0:T(8,128)S(1)} %get-tuple-element.22.yp), channel_id=1, source_target_pairs={{256,1},{1,256},{257,2},{2,257},{258,3},{3,258},{259,4},{4,259},{2... | collective-permute-start | bytes 430088 | tf_op jit(solution)/shard_map/ppermute | solution.py:607
  51.1 2.7 %copy-start.1 = (f32[16,8,128]{2,1,0:T(8,128)S(1)}, f32[16,8,128]{2,1,0:T(8,128)}, u32[]{:S(2)}) copy-start(f32[16,8,128]{2,1,0:T(8,128)} %m.1) | copy-start | bytes 196612
  51.1 2.7 %copy-start.2 = (f32[16,8,128]{2,1,0:T(8,128)S(1)}, f32[16,8,128]{2,1,0:T(8,128)}, u32[]{:S(2)}) copy-start(f32[16,8,128]{2,1,0:T(8,128)} %f.1) | copy-start | bytes 196612

commit v12 on v11

--- a/solution.py
+++ b/solution.py
@@ -361,6 +361,13 @@
     return (left + left) + sides_left, (right + right) + sides_right
 
 
+def along_z_half(mine, other, first):
+    lane = lane_index()
+    up = jnp.where(lane < 127, pltpu.roll(mine, 127, 1), keep(first, pltpu.roll(other, 127, 1)))
+    down = jnp.where(lane > 0, pltpu.roll(mine, 1, 1), jnp.where(first, 0.0, pltpu.roll(other, 1, 1)))
+    return (mine + mine) + (up + down)
+
+
 def along_z_coarse(tile):
     lane = lane_index()
     sides = keep(lane < 127, pltpu.roll(tile, 127, 1)) + keep(lane > 0, pltpu.roll(tile, 1, 1))
@@ -480,7 +487,7 @@
                         out[p, part] = total
 
 
-def defects(pf):
+def defects(pf, first=None):
     def load(p):
         return [pf[p, part] for part in range(4)]
 
@@ -489,8 +496,14 @@
     for x in range(16):
         after = load(x + 2)
         above = added(here, after)
-        summed = along_yz(added(below, above))
-        yield here[:2], [SELF_WEIGHT * here[z] - SIDE_CUBE * summed[z] for z in range(2)]
+        both = added(below, above)
+        if first is None:
+            own, summed = here[:2], along_yz(both)
+        else:
+            left, right = (along_y(both[z], both[2 + z])[0] for z in range(2))
+            mine, other = jnp.where(first, left, right), jnp.where(first, right, left)
+            own, summed = [jnp.where(first, here[0], here[1])], [along_z_half(mine, other, first)]
+        yield own, [SELF_WEIGHT * a - SIDE_CUBE * b for a, b in zip(own, summed)]
         here, below = after, above
 
 
@@ -545,8 +558,7 @@
     relax_levels(counts, h0_all, q0, h1_all, q1, h2_all, q2)
     iterate(corrections(q1, iw1, q2, iw2, copies), q0, w, pf, pf_all)
     first = core() == 0
-    for x, (here, defect) in enumerate(defects(pf_all)):
-        mine, rest = (jnp.where(first, both[0], both[1]) for both in (here, defect))
+    for x, ((mine,), (rest,)) in enumerate(defects(pf_all, first)):
         weight = m[x]
         solved[x] = mine / weight
         left[x] = f[x] - weight * rest

time: 56.2 us -> 56.2 us (level)
  no operation moved by 1% of the time
where the time goes in v12:
time: 56.2 us; the launch traced here: 55.9 us
  blocking collectives  45.3 us (81%)
  starting transfers between devices  5.07 us (9%)
  Pallas kernels  4.82 us (9%)
  between operations  0.72 us (1%)
    all_gather x2, blocking collectives, trade_x(): lax.all_gather(packed, names, axis=0, axis_index_groups=groups)  19.8 us
    all_gather x5, blocking collectives, share(): return lax.all_gather(value, 'group', axis=0)  12.9 us
    all_gather x2, blocking collectives, trade_y(): lax.all_gather(packed_far, ('group', 'gy'), axis=0, tiled=True, axis_inde...  12.6 us
    ppermute x2, starting transfers between devices, trade_y(): near = lax.ppermute(packed, ('group', 'gy'), moves)  5.07 us
    pallas_call x6, Pallas kernels, call(): pl.pallas_call(kernel, out_shape=[jax.ShapeDtypeStruct(shape, F32) for sh...  4.82 us
  transfers between devices with their start and end apart: 2, of which 0 were waited for; matrix products, arithmetic and copies ran while one was open for 0% of the time, Pallas kernels for 0%

profile of v12, /device:TPU:241, one launch (start us, length us, event | category | flops | bytes accessed | tf_op | source)
XLA Modules:
  0.0 55.9 jit_solution(18037063327985240113)
XLA Ops:
  0.6 1.2 %block_sums.1 = f32[43,8,128]{2,1,0:T(8,128)S(1)} custom-call(f32[16,8,128]{2,1,0:T(8,128)} %m.1, f32[16,8,128]{2,1,0:T(8,128)} %f.1, s32[2,3]{1,0:T(2,128)} %sweeps_whole.1), custom_call_target="tpu_custom_call" | custom-call | tf_op jit(solution)/shard_map/block_sums/pallas_call | solution.py:578
  1.8 2.4 %all-gather = f32[86,8,128]{2,1,0:T(8,128)S(1)} all-gather(f32[43,8,128]{2,1,0:T(8,128)S(1)} %block_sums.1), channel_id=2, replica_groups=mesh['group'=2,'gx'=16,'gy'=16] {'group'}, dimensions={0}, use_global_device_ids=true | all-gather | bytes 528384 | tf_op jit(solution)/shard_map/all_gather | solution.py:598
  4.2 9.7 %all-gather.1 = f32[28,8,128]{2,1,0:T(8,128)S(1)} all-gather(f32[14,8,128]{2,1,0:T(8,128)S(1)} %get-tuple-element.16), channel_id=3, replica_groups={{0,16},{1,17},{2,18},{3,19},{4,20},{5,21},{6,22},{7,23},{8,24},{9,25},{..., dimensions={0}, use_global_device_ids=true | all-gather | bytes 172032 | tf_op jit(solution)/shard_map/all_gather | solution.py:611
  13.9 2.0 %all-gather.2 = f32[4,14,8,128]{3,2,1,0:T(8,128)S(1)} all-gather(f32[2,14,8,128]{3,2,1,0:T(8,128)S(1)} %bitcast.17), channel_id=4, replica_groups=mesh['group'=2,'gx'=16,'gy'=16] {'group'}, dimensions={0}, use_global_device_ids=true | all-gather | bytes 344064 | tf_op jit(solution)/shard_map/all_gather | solution.py:598
  15.9 0.1 first_rows.1
  15.9 3.2 %collective-permute-start = (f32[43,8,128]{2,1,0:T(8,128)S(1)}, f32[43,8,128]{2,1,0:T(8,128)S(1)}, u32[]{:S(2)}, u32[]{:S(2)}) collective-permute-start(f32[43,8,128]{2,1,0:T(8,128)S(1)} %get-tuple-element.17.yp), channel_id=1, source_target_pairs={{256,1},{1,256},{257,2},{2,257},{258,3},{3,258},{259,4},{4,259},{2... | collective-permute-start | bytes 528392 | tf_op jit(solution)/shard_map/ppermute | solution.py:619
  19.1 6.2 %all_gather.54 = f32[6,8,128]{2,1,0:T(8,128)S(1)} all-gather(f32[3,8,128]{2,1,0:T(8,128)S(1)} %get-tuple-element.18), channel_id=1, replica_groups={{0,258},{1,259},{2,260},{3,261},{4,262},{5,263},{6,264},{7,265},{8,266}..., dimensions={0}, use_global_device_ids=true | all-gather | bytes 36864 | tf_op jit(solution)/shard_map/all_gather | solution.py:622
  25.3 0.0 collective-permute-done
  25.3 0.0 copy-start
  25.3 0.0 copy-start.3
  25.3 4.0 %all-gather.3 = f32[98,8,128]{2,1,0:T(8,128)S(1)} all-gather(f32[49,8,128]{2,1,0:T(8,128)S(1)} %pad_maximum_fusion), channel_id=5, replica_groups=mesh['group'=2,'gx'=16,'gy'=16] {'group'}, dimensions={0}, use_global_device_ids=true | all-gather | bytes 602112 | tf_op jit(solution)/shard_map/all_gather | solution.py:598
  29.3 0.0 copy-done
  29.3 0.0 copy-done.3
  29.3 1.2 %first_cycle.1 = (f32[11,8,128]{2,1,0:T(8,128)S(1)}, f32[18,4,8,128]{3,2,1,0:T(8,128)S(1)}, f32[18,4,8,128]{3,2,1,0:T(8,128)S(1)}, f32[10,2,8,128]{3,2,1,0:T(8,1...) custom-call(f32[2,43,8,128]{3,2,1,0:T(8,128)S(1)} %bitcast.9, ...), custom_call_target="tpu_custom_call" | custom-call | tf_op jit(solution)/shard_map/first_cycle/pallas_call | solution.py:578
  30.6 10.1 %all-gather.4 = f32[22,8,128]{2,1,0:T(8,128)S(1)} all-gather(f32[11,8,128]{2,1,0:T(8,128)S(1)} %get-tuple-element.20), channel_id=6, replica_groups={{0,16},{1,17},{2,18},{3,19},{4,20},{5,21},{6,22},{7,23},{8,24},{9,25},{..., dimensions={0}, use_global_device_ids=true | all-gather | bytes 135168 | tf_op jit(solution)/shard_map/all_gather | solution.py:611
  40.7 1.9 %all-gather.5 = f32[4,11,8,128]{3,2,1,0:T(8,128)S(1)} all-gather(f32[2,11,8,128]{3,2,1,0:T(8,128)S(1)} %bitcast.18), channel_id=7, replica_groups=mesh['group'=2,'gx'=16,'gy'=16] {'group'}, dimensions={0}, use_global_device_ids=true | all-gather | bytes 270336 | tf_op jit(solution)/shard_map/all_gather | solution.py:598
  42.6 1.9 %collective-permute-start.1 = (f32[35,8,128]{2,1,0:T(8,128)S(1)}, f32[35,8,128]{2,1,0:T(8,128)S(1)}, u32[]{:S(2)}, u32[]{:S(2)}) collective-permute-start(f32[35,8,128]{2,1,0:T(8,128)S(1)} %get-tuple-element.22.yp), channel_id=1, source_target_pairs={{256,1},{1,256},{257,2},{2,257},{258,3},{3,258},{259,4},{4,259},{2... | collective-permute-start | bytes 430088 | tf_op jit(solution)/shard_map/ppermute | solution.py:619
  44.6 6.3 %all_gather.61 = f32[6,8,128]{2,1,0:T(8,128)S(1)} all-gather(f32[3,8,128]{2,1,0:T(8,128)S(1)} %get-tuple-element.23), channel_id=1, replica_groups={{0,258},{1,259},{2,260},{3,261},{4,262},{5,263},{6,264},{7,265},{8,266}..., dimensions={0}, use_global_device_ids=true | all-gather | bytes 36864 | tf_op jit(solution)/shard_map/all_gather | solution.py:622
  50.9 0.0 collective-permute-done.1
  50.9 0.0 copy-start.1
  50.9 0.0 copy-start.2
  50.9 2.7 %all-gather.6 = f32[82,8,128]{2,1,0:T(8,128)S(1)} all-gather(f32[41,8,128]{2,1,0:T(8,128)S(1)} %pad_maximum_fusion.1), channel_id=8, replica_groups=mesh['group'=2,'gx'=16,'gy'=16] {'group'}, dimensions={0}, use_global_device_ids=true | all-gather | bytes 503808 | tf_op jit(solution)/shard_map/all_gather | solution.py:598
  53.6 0.0 copy-done.1
  53.6 0.0 copy-done.2
  53.6 2.3 %second_cycle.1 = (f32[16,8,128]{2,1,0:T(8,128)}, f32[16,8,128]{2,1,0:T(8,128)}) custom-call(f32[2,43,8,128]{3,2,1,0:T(8,128)S(1)} %bitcast.10, f32[16,8,128]{2,1,0:T(8,128)S(1)} %copy-done.1, f32[16,8,128]{2,1,0:T(8,128)S(1)} %copy-done.2, f32[16,2,8,128]{3,2,1,0:T(8,128)S(1)} %get-tuple-element.19.h0, f32[2,2,11,8,128]{4,3,2,1,0:T(8,128)S(1)} %bitcast.14, ...), custom_call_target="tpu_custom_call" | custom-call | tf_op jit(solution)/shard_map/second_cycle/pallas_call | solution.py:578
  (4 shorter events, 0.1 us)
Async XLA Ops:
  15.9 9.4 %collective-permute-start = (f32[43,8,128]{2,1,0:T(8,128)S(1)}, f32[43,8,128]{2,1,0:T(8,128)S(1)}, u32[]{:S(2)}, u32[]{:S(2)}) collective-permute-start(f32[43,8,128]{2,1,0:T(8,128)S(1)} %get-tuple-element.17.yp), channel_id=1, source_target_pairs={{256,1},{1,256},{257,2},{2,257},{258,3},{3,258},{259,4},{4,259},{2... | collective-permute-start | bytes 528392 | tf_op jit(solution)/shard_map/ppermute | solution.py:619
  25.3 4.0 %copy-start = (bf16[256,256]{1,0:T(8,128)(2,1)S(1)}, bf16[256,256]{1,0:T(8,128)(2,1)}, u32[]{:S(2)}) copy-start(bf16[256,256]{1,0:T(8,128)(2,1)} %constant.5.clone.copies) | copy-start | bytes 393220
  25.3 4.0 %copy-start.3 = (bf16[256,256]{1,0:T(8,128)(2,1)S(1)}, bf16[256,256]{1,0:T(8,128)(2,1)}, u32[]{:S(2)}) copy-start(bf16[256,256]{1,0:T(8,128)(2,1)} %constant.4.clone.sums) | copy-start | bytes 393220
  42.6 8.3 %collective-permute-start.1 = (f32[35,8,128]{2,1,0:T(8,128)S(1)}, f32[35,8,128]{2,1,0:T(8,128)S(1)}, u32[]{:S(2)}, u32[]{:S(2)}) collective-permute-start(f32[35,8,128]{2,1,0:T(8,128)S(1)} %get-tuple-element.22.yp), channel_id=1, source_target_pairs={{256,1},{1,256},{257,2},{2,257},{258,3},{3,258},{259,4},{4,259},{2... | collective-permute-start | bytes 430088 | tf_op jit(solution)/shard_map/ppermute | solution.py:619
  50.9 2.7 %copy-start.1 = (f32[16,8,128]{2,1,0:T(8,128)S(1)}, f32[16,8,128]{2,1,0:T(8,128)}, u32[]{:S(2)}) copy-start(f32[16,8,128]{2,1,0:T(8,128)} %m.1) | copy-start | bytes 196612
  50.9 2.7 %copy-start.2 = (f32[16,8,128]{2,1,0:T(8,128)S(1)}, f32[16,8,128]{2,1,0:T(8,128)}, u32[]{:S(2)}) copy-start(f32[16,8,128]{2,1,0:T(8,128)} %f.1) | copy-start | bytes 196612

commit v13 on v11

--- a/solution.py
+++ b/solution.py
@@ -545,17 +545,16 @@
     relax_levels(counts, h0_all, q0, h1_all, q1, h2_all, q2)
     iterate(corrections(q1, iw1, q2, iw2, copies), q0, w, pf, pf_all)
     first = core() == 0
-    for x, (here, defect) in enumerate(defects(pf_all)):
-        mine, rest = (jnp.where(first, both[0], both[1]) for both in (here, defect))
-        weight = m[x]
-        solved[x] = mine / weight
-        left[x] = f[x] - weight * rest
     sends = [
         pltpu.make_async_copy(source, target, sent.at[k])
         for k, (source, target) in enumerate(((solved, solution_out), (left, residual_out)))
     ]
-    for send in sends:
-        send.start()
+    for x in range(16):
+        solved[x] = jnp.where(first, pf_all[x + 1, 0], pf_all[x + 1, 1]) / m[x]
+    sends[0].start()
+    for x, (_, defect) in enumerate(defects(pf_all)):
+        left[x] = f[x] - m[x] * jnp.where(first, defect[0], defect[1])
+    sends[1].start()
     for send in sends:
         send.wait()
 

time: 56.2 us -> 55.9 us (level)
  no operation moved by 1% of the time
where the time goes in v13:
time: 55.9 us; the launch traced here: 55.5 us
  blocking collectives  45.3 us (81%)
  starting transfers between devices  5.07 us (9%)
  Pallas kernels  4.41 us (8%)
  between operations  0.72 us (1%)
    all_gather x2, blocking collectives, trade_x(): lax.all_gather(packed, names, axis=0, axis_index_groups=groups)  19.8 us
    all_gather x5, blocking collectives, share(): return lax.all_gather(value, 'group', axis=0)  12.9 us
    all_gather x2, blocking collectives, trade_y(): lax.all_gather(packed_far, ('group', 'gy'), axis=0, tiled=True, axis_inde...  12.6 us
    ppermute x2, starting transfers between devices, trade_y(): near = lax.ppermute(packed, ('group', 'gy'), moves)  5.07 us
    pallas_call x6, Pallas kernels, call(): pl.pallas_call(kernel, out_shape=[jax.ShapeDtypeStruct(shape, F32) for sh...  4.41 us
  transfers between devices with their start and end apart: 2, of which 0 were waited for; matrix products, arithmetic and copies ran while one was open for 0% of the time, Pallas kernels for 0%

profile of v13, /device:TPU:241, one launch (start us, length us, event | category | flops | bytes accessed | tf_op | source)
XLA Modules:
  0.0 55.5 jit_solution(5685556102511140665)
XLA Ops:
  0.6 1.2 %block_sums.1 = f32[43,8,128]{2,1,0:T(8,128)S(1)} custom-call(f32[16,8,128]{2,1,0:T(8,128)} %m.1, f32[16,8,128]{2,1,0:T(8,128)} %f.1, s32[2,3]{1,0:T(2,128)} %sweeps_whole.1), custom_call_target="tpu_custom_call" | custom-call | tf_op jit(solution)/shard_map/block_sums/pallas_call | solution.py:565
  1.8 2.4 %all-gather = f32[86,8,128]{2,1,0:T(8,128)S(1)} all-gather(f32[43,8,128]{2,1,0:T(8,128)S(1)} %block_sums.1), channel_id=2, replica_groups=mesh['group'=2,'gx'=16,'gy'=16] {'group'}, dimensions={0}, use_global_device_ids=true | all-gather | bytes 528384 | tf_op jit(solution)/shard_map/all_gather | solution.py:585
  4.2 9.7 %all-gather.1 = f32[28,8,128]{2,1,0:T(8,128)S(1)} all-gather(f32[14,8,128]{2,1,0:T(8,128)S(1)} %get-tuple-element.16), channel_id=3, replica_groups={{0,16},{1,17},{2,18},{3,19},{4,20},{5,21},{6,22},{7,23},{8,24},{9,25},{..., dimensions={0}, use_global_device_ids=true | all-gather | bytes 172032 | tf_op jit(solution)/shard_map/all_gather | solution.py:598
  13.9 2.0 %all-gather.2 = f32[4,14,8,128]{3,2,1,0:T(8,128)S(1)} all-gather(f32[2,14,8,128]{3,2,1,0:T(8,128)S(1)} %bitcast.17), channel_id=4, replica_groups=mesh['group'=2,'gx'=16,'gy'=16] {'group'}, dimensions={0}, use_global_device_ids=true | all-gather | bytes 344064 | tf_op jit(solution)/shard_map/all_gather | solution.py:585
  15.9 0.1 first_rows.1
  15.9 3.2 %collective-permute-start = (f32[43,8,128]{2,1,0:T(8,128)S(1)}, f32[43,8,128]{2,1,0:T(8,128)S(1)}, u32[]{:S(2)}, u32[]{:S(2)}) collective-permute-start(f32[43,8,128]{2,1,0:T(8,128)S(1)} %get-tuple-element.17.yp), channel_id=1, source_target_pairs={{256,1},{1,256},{257,2},{2,257},{258,3},{3,258},{259,4},{4,259},{2... | collective-permute-start | bytes 528392 | tf_op jit(solution)/shard_map/ppermute | solution.py:606
  19.1 6.2 %all_gather.54 = f32[6,8,128]{2,1,0:T(8,128)S(1)} all-gather(f32[3,8,128]{2,1,0:T(8,128)S(1)} %get-tuple-element.18), channel_id=1, replica_groups={{0,258},{1,259},{2,260},{3,261},{4,262},{5,263},{6,264},{7,265},{8,266}..., dimensions={0}, use_global_device_ids=true | all-gather | bytes 36864 | tf_op jit(solution)/shard_map/all_gather | solution.py:609
  25.3 0.0 collective-permute-done
  25.3 0.0 copy-start
  25.3 0.0 copy-start.3
  25.3 4.0 %all-gather.3 = f32[98,8,128]{2,1,0:T(8,128)S(1)} all-gather(f32[49,8,128]{2,1,0:T(8,128)S(1)} %pad_maximum_fusion), channel_id=5, replica_groups=mesh['group'=2,'gx'=16,'gy'=16] {'group'}, dimensions={0}, use_global_device_ids=true | all-gather | bytes 602112 | tf_op jit(solution)/shard_map/all_gather | solution.py:585
  29.3 0.0 copy-done
  29.3 0.0 copy-done.3
  29.3 1.1 %first_cycle.1 = (f32[11,8,128]{2,1,0:T(8,128)S(1)}, f32[18,4,8,128]{3,2,1,0:T(8,128)S(1)}, f32[18,4,8,128]{3,2,1,0:T(8,128)S(1)}, f32[10,2,8,128]{3,2,1,0:T(8,1...) custom-call(f32[2,43,8,128]{3,2,1,0:T(8,128)S(1)} %bitcast.9, ...), custom_call_target="tpu_custom_call" | custom-call | tf_op jit(solution)/shard_map/first_cycle/pallas_call | solution.py:565
  30.4 10.1 %all-gather.4 = f32[22,8,128]{2,1,0:T(8,128)S(1)} all-gather(f32[11,8,128]{2,1,0:T(8,128)S(1)} %get-tuple-element.20), channel_id=6, replica_groups={{0,16},{1,17},{2,18},{3,19},{4,20},{5,21},{6,22},{7,23},{8,24},{9,25},{..., dimensions={0}, use_global_device_ids=true | all-gather | bytes 135168 | tf_op jit(solution)/shard_map/all_gather | solution.py:598
  40.5 1.9 %all-gather.5 = f32[4,11,8,128]{3,2,1,0:T(8,128)S(1)} all-gather(f32[2,11,8,128]{3,2,1,0:T(8,128)S(1)} %bitcast.18), channel_id=7, replica_groups=mesh['group'=2,'gx'=16,'gy'=16] {'group'}, dimensions={0}, use_global_device_ids=true | all-gather | bytes 270336 | tf_op jit(solution)/shard_map/all_gather | solution.py:585
  42.4 1.9 %collective-permute-start.1 = (f32[35,8,128]{2,1,0:T(8,128)S(1)}, f32[35,8,128]{2,1,0:T(8,128)S(1)}, u32[]{:S(2)}, u32[]{:S(2)}) collective-permute-start(f32[35,8,128]{2,1,0:T(8,128)S(1)} %get-tuple-element.22.yp), channel_id=1, source_target_pairs={{256,1},{1,256},{257,2},{2,257},{258,3},{3,258},{259,4},{4,259},{2... | collective-permute-start | bytes 430088 | tf_op jit(solution)/shard_map/ppermute | solution.py:606
  44.4 6.3 %all_gather.61 = f32[6,8,128]{2,1,0:T(8,128)S(1)} all-gather(f32[3,8,128]{2,1,0:T(8,128)S(1)} %get-tuple-element.23), channel_id=1, replica_groups={{0,258},{1,259},{2,260},{3,261},{4,262},{5,263},{6,264},{7,265},{8,266}..., dimensions={0}, use_global_device_ids=true | all-gather | bytes 36864 | tf_op jit(solution)/shard_map/all_gather | solution.py:609
  50.7 0.0 collective-permute-done.1
  50.7 0.0 copy-start.1
  50.7 0.0 copy-start.2
  50.7 2.7 %all-gather.6 = f32[82,8,128]{2,1,0:T(8,128)S(1)} all-gather(f32[41,8,128]{2,1,0:T(8,128)S(1)} %pad_maximum_fusion.1), channel_id=8, replica_groups=mesh['group'=2,'gx'=16,'gy'=16] {'group'}, dimensions={0}, use_global_device_ids=true | all-gather | bytes 503808 | tf_op jit(solution)/shard_map/all_gather | solution.py:585
  53.4 0.0 copy-done.1
  53.4 0.0 copy-done.2
  53.4 2.1 %second_cycle.1 = (f32[16,8,128]{2,1,0:T(8,128)}, f32[16,8,128]{2,1,0:T(8,128)}) custom-call(f32[2,43,8,128]{3,2,1,0:T(8,128)S(1)} %bitcast.10, f32[16,8,128]{2,1,0:T(8,128)S(1)} %copy-done.1, f32[16,8,128]{2,1,0:T(8,128)S(1)} %copy-done.2, f32[16,2,8,128]{3,2,1,0:T(8,128)S(1)} %get-tuple-element.19.h0, f32[2,2,11,8,128]{4,3,2,1,0:T(8,128)S(1)} %bitcast.14, ...), custom_call_target="tpu_custom_call" | custom-call | tf_op jit(solution)/shard_map/second_cycle/pallas_call | solution.py:565
  (4 shorter events, 0.1 us)
Async XLA Ops:
  15.9 9.4 %collective-permute-start = (f32[43,8,128]{2,1,0:T(8,128)S(1)}, f32[43,8,128]{2,1,0:T(8,128)S(1)}, u32[]{:S(2)}, u32[]{:S(2)}) collective-permute-start(f32[43,8,128]{2,1,0:T(8,128)S(1)} %get-tuple-element.17.yp), channel_id=1, source_target_pairs={{256,1},{1,256},{257,2},{2,257},{258,3},{3,258},{259,4},{4,259},{2... | collective-permute-start | bytes 528392 | tf_op jit(solution)/shard_map/ppermute | solution.py:606
  25.3 4.0 %copy-start = (bf16[256,256]{1,0:T(8,128)(2,1)S(1)}, bf16[256,256]{1,0:T(8,128)(2,1)}, u32[]{:S(2)}) copy-start(bf16[256,256]{1,0:T(8,128)(2,1)} %constant.5.clone.copies) | copy-start | bytes 393220
  25.3 4.0 %copy-start.3 = (bf16[256,256]{1,0:T(8,128)(2,1)S(1)}, bf16[256,256]{1,0:T(8,128)(2,1)}, u32[]{:S(2)}) copy-start(bf16[256,256]{1,0:T(8,128)(2,1)} %constant.4.clone.sums) | copy-start | bytes 393220
  42.4 8.3 %collective-permute-start.1 = (f32[35,8,128]{2,1,0:T(8,128)S(1)}, f32[35,8,128]{2,1,0:T(8,128)S(1)}, u32[]{:S(2)}, u32[]{:S(2)}) collective-permute-start(f32[35,8,128]{2,1,0:T(8,128)S(1)} %get-tuple-element.22.yp), channel_id=1, source_target_pairs={{256,1},{1,256},{257,2},{2,257},{258,3},{3,258},{259,4},{4,259},{2... | collective-permute-start | bytes 430088 | tf_op jit(solution)/shard_map/ppermute | solution.py:606
  50.7 2.7 %copy-start.1 = (f32[16,8,128]{2,1,0:T(8,128)S(1)}, f32[16,8,128]{2,1,0:T(8,128)}, u32[]{:S(2)}) copy-start(f32[16,8,128]{2,1,0:T(8,128)} %m.1) | copy-start | bytes 196612
  50.7 2.7 %copy-start.2 = (f32[16,8,128]{2,1,0:T(8,128)S(1)}, f32[16,8,128]{2,1,0:T(8,128)}, u32[]{:S(2)}) copy-start(f32[16,8,128]{2,1,0:T(8,128)} %f.1) | copy-start | bytes 196612
